TPU v7x, 32 devices: a whole 2x2x4 slice. The times are simulated.
32 devices in a mesh: dp: 2 (over x), gx: 4 (over y, core), gy: 4 (over z).
Axes of the slice: x: 2, y: 2, z: 4, core: 2. Of those that a mesh axis runs over, the one named last changes fastest.
Arguments:
- tokens: bfloat16 [960, 11264], P('gy', ('dp', 'gx')), may hold values from -6 to 6
- segment_ids: int32 [8, 1408], P(('dp', 'gy')), may hold values from 0 to 3, never falling along the last dimension, each value on 1 to 704 neighbouring positions
- slot_table: int32 [5], replicated, may hold values from 0 to 7, as said below
- w_qkv: bfloat16 [960, 2560], P('gy', 'gx'), may hold values from -0.1875 to 0.1875
- w_out: bfloat16 [960, 1536], P('gy', 'gx'), may hold values from -1.5 to 1.5
- w_gate_up: bfloat16 [960, 2, 2560], P('gy', None, 'gx'), may hold values from -0.1875 to 0.1875
- w_down: bfloat16 [960, 2560], P('gy', 'gx'), may hold values from -0.125 to 0.125
- gain_attn: float32 [960], P('gy'), may hold values from 0.5 to 1.5
- gain_mlp: float32 [960], P('gy'), may hold values from 0.5 to 1.5
- cotangent: bfloat16 [960, 11264], P('gy', ('dp', 'gx')), may hold values from -6 to 6
Outputs:
- layer_out: bfloat16 [960, 11264], P('gy', ('dp', 'gx'))
- input_grad: bfloat16 [960, 11264], P('gy', ('dp', 'gx'))
- grad_qkv: float32 [960, 2560], P('gy', 'gx')
- grad_out: float32 [960, 1536], P('gy', 'gx')
- grad_gate_up: float32 [960, 2, 2560], P('gy', None, 'gx')
- grad_down: float32 [960, 2560], P('gy', 'gx')
- grad_gain_attn: float32 [960], P('gy')
- grad_gain_mlp: float32 [960], P('gy')
Inputs may be any that keep to these rules, and one draw needn't show every extreme that they name: `slot_table`: the 5 entries name distinct slots; slot // 2 is a weight-grid row. One row holds two groups in its slots 2 r and 2 r + 1, every other row one group in slot 2 r. `segment_ids`: within a sequence ids never fall.
All inputs are finite; a program needn't handle non-finite values.
Results may differ from a plain program's by a relative error of at most 0.019.
Values may be sent and summed in bfloat16 or wider, within the bound.
No kernel may reach another device: no remote copies, remote signals or barrier semaphores. Data moves between devices by JAX's collectives and lax.ppermute only.
A program may use at most 192 MiB of HBM per device.

v0:
```python
import functools

import jax
import jax.numpy as jnp
from jax import lax
from jax.experimental import pallas as pl
from jax.experimental.pallas import tpu as pltpu
from jax.sharding import PartitionSpec as P

D = 960
HD = 64
QPK = 3
L = 1408
SEGS = 4
QW = QPK * HD
SLOT_W = QW + 2 * HD
PACK = SLOT_W + QW
GROUPS = 5
ROWS = 4
CH = L // ROWS
CP = 384
FB = D // ROWS
ODD = PACK // ROWS

EPSILON = 1e-05
THETA_BASE = 100000.0
NEGATIVE = -1e30
SEQ_MAP = (0, 2, 1, 3)
SEQ_BACK = (0, 2, 1, 3)
BF = jnp.bfloat16
F32 = jnp.float32
VMEM_LIMIT = 58 * 1024 * 1024
HALF = HD // 2
AW = 2 * QW
AP = AW + AW // ROWS
KV = 2 * HD
BP = KV + KV // ROWS + 16


def tn(a, b):
    return lax.dot_general(a, b, (((0,), (0,)), ((), ())), preferred_element_type=F32)


def nn(a, b):
    return lax.dot_general(a, b, (((1,), (0,)), ((), ())), preferred_element_type=F32)


def nt(a, b):
    return lax.dot_general(a, b, (((1,), (1,)), ((), ())), preferred_element_type=F32)


def rows_at(block, size=FB):
    return pl.ds(pl.multiple_of(block * FB, 16), size)


def rope(a, b, cos_a, sin_a):
    return a * cos_a - b * sin_a, b * cos_a + a * sin_a


def split_kernel(with_tail, sc, *refs):
    t_ref = refs[0]
    outs = refs[-ROWS:]
    iy = sc[1]
    if with_tail:
        lane = lax.broadcasted_iota(jnp.int32, (FB, CP - CH), 1)
        tail = jnp.zeros((FB, CP - CH), F32)
        for i in range(2):
            rest = refs[1 + i][...]
            for part in range(3):
                piece = rest.astype(BF).astype(F32)
                rest = rest - piece
                tail = jnp.where(lane == 3 * i + part, piece, tail)
        tail = tail.astype(BF)
    else:
        tail = jnp.zeros((FB, CP - CH), BF)
    for q in range(ROWS):
        block = jnp.concatenate([t_ref[:, q * CH : (q + 1) * CH], tail], axis=1)
        for k in range(ROWS):

            @pl.when((iy ^ k) == q)
            def _(k=k, block=block):
                outs[k][...] = block


def join_kernel(sc, *refs):
    for k in range(ROWS):
        refs[ROWS][rows_at(sc[0] ^ k)] = refs[k][...]


def merge_kernel(sc, *refs):
    iy = sc[1]
    for i in range(2):
        rows = slice(i * FB, (i + 1) * FB)
        parts = []
        for q in range(ROWS):
            value = refs[0][rows, :CH]
            for k in range(1, ROWS):
                value = jnp.where((iy ^ k) == q, refs[k][rows, :CH], value)
            parts.append(value)
        refs[ROWS + i][...] = jnp.concatenate(parts, axis=1)


def qkv_kernel(sc, *refs):
    toks = refs[:4]
    w_all = refs[4]
    cos_ref, sin_ref = refs[5:7]
    x_ref, n1_ref, r1_ref, g1_ref, g2_ref, w5_ref, qs_ref, kv_ref = refs[7:]
    ix = sc[0]
    lane = lax.broadcasted_iota(jnp.int32, (FB, CP), 1)
    for k in range(ROWS):
        rows = rows_at(ix ^ k)
        piece = toks[k][...].astype(F32)
        x_ref[rows] = jnp.where(lane < CH, piece, 0.0).astype(BF)
        for i, out in enumerate((g1_ref, g2_ref)):
            here = (lane >= CH + 3 * i) & (lane < CH + 3 * i + 3)
            out[rows] = jnp.sum(jnp.where(here, piece, 0.0), axis=1, keepdims=True)
    x = x_ref[...].astype(F32)
    r1 = lax.rsqrt(jnp.sum(x * x, axis=0, keepdims=True) / D + EPSILON)
    r1_ref[...] = r1
    n1_ref[...] = (x * r1 * g1_ref[...]).astype(BF)
    for k in range(ROWS):
        w5_ref[k] = w_all[ix ^ k, :, :PACK]
        w5_ref[GROUPS - 1, :, k * ODD : (k + 1) * ODD] = w_all[k, :, PACK:]
    cos_a = cos_ref[...]
    sin_a = sin_ref[...]
    for g in range(GROUPS):
        p = tn(w5_ref[g, :, :SLOT_W], n1_ref[...])
        for j in range(QPK + 1):
            first, second = rope(
                p[j * HD : j * HD + HALF], p[j * HD + HALF : (j + 1) * HD], cos_a, sin_a
            )
            first = first.astype(BF)
            second = second.astype(BF)
            if j < QPK:
                qs_ref[g, j * HD : j * HD + HALF] = (first.astype(F32) * HD**-0.5).astype(BF)
                qs_ref[g, j * HD + HALF : (j + 1) * HD] = (second.astype(F32) * HD**-0.5).astype(BF)
            else:
                kv_ref[g, :HALF] = first
                kv_ref[g, HALF:HD] = second
        kv_ref[g, HD:] = p[(QPK + 1) * HD :].astype(BF)


def attend_kernel(
    sc, qs_ref, kv0, kv1, kv2, kv3, bias_ref, w_ref, x_ref, gain_ref,
    o_ref, lse_ref, h_ref, n2_ref, r2_ref, m_s, l_s, acc_s,
):
    g = pl.program_id(0)
    kvs = (kv0, kv1, kv2, kv3)

    def fold(k, fresh):
        keys = kvs[k][0, :HD]
        values = kvs[k][0, HD:]
        bias = bias_ref[k]
        for j in range(QPK):
            s = tn(keys, qs_ref[0, j * HD : (j + 1) * HD]) + bias
            top = jnp.max(s, axis=0, keepdims=True)
            if fresh:
                m = top
                e = jnp.exp(s - m)
                l_s[j : j + 1] = jnp.sum(e, axis=0, keepdims=True)
                acc_s[j * HD : (j + 1) * HD] = nn(values, e.astype(BF))
            else:
                old = m_s[j : j + 1]
                m = jnp.maximum(old, top)
                fade = jnp.exp(old - m)
                e = jnp.exp(s - m)
                l_s[j : j + 1] = l_s[j : j + 1] * fade + jnp.sum(e, axis=0, keepdims=True)
                acc_s[j * HD : (j + 1) * HD] = acc_s[j * HD : (j + 1) * HD] * fade + nn(
                    values, e.astype(BF)
                )
            m_s[j : j + 1] = m

    fold(0, True)
    for k in range(1, ROWS):
        pl.when(sc[4 + k] != 0)(functools.partial(fold, k, False))
    for j in range(QPK):
        total = l_s[j : j + 1]
        o_ref[0, j * HD : (j + 1) * HD] = (acc_s[j * HD : (j + 1) * HD] / total).astype(BF)
        lse_ref[0, j : j + 1] = m_s[j : j + 1] + jnp.log(total)
    part = nn(w_ref[0, :, SLOT_W:], o_ref[0])

    @pl.when(g == 0)
    def _():
        h_ref[...] = x_ref[...].astype(F32) + part

    @pl.when(g != 0)
    def _():
        h_ref[...] += part

    @pl.when(g == GROUPS - 1)
    def _():
        h = h_ref[...]
        r2 = lax.rsqrt(jnp.sum(h * h, axis=0, keepdims=True) / D + EPSILON)
        r2_ref[...] = r2
        n2_ref[...] = (h * r2 * gain_ref[...]).astype(BF)


def row_sums(values):
    return lax.dot_general(
        jnp.ones((16, CP), F32), values, (((1,), (1,)), ((), ())),
        precision=lax.Precision.HIGHEST, preferred_element_type=F32,
    )


def attend_back_kernel(
    sc, qs_ref, kv0, kv1, kv2, kv3, bias_ref, w_ref, o_ref, lse_ref, n1_ref, cos_ref, sin_ref,
    dn_a, dn_b, dn_c, h_ref, r2_ref, gain_ref, dy_ref,
    dq_ref, d0, d1, d2, d3, dh_ref, gg_ref, pa0, pa1, pa2, pa3, datt_s, do_s, dl_s, dq_s,
):
    g = pl.program_id(0)
    kvs = (kv0, kv1, kv2, kv3)
    outs = (d0, d1, d2, d3)
    packs = (pa0, pa1, pa2, pa3)

    @pl.when(g == 0)
    def _():
        dn2 = dn_a[...].astype(F32) + dn_b[...].astype(F32) + dn_c[...].astype(F32)
        h = h_ref[...]
        r2 = r2_ref[...]
        weighted = dn2 * gain_ref[...]
        inner = jnp.sum(weighted * h, axis=0, keepdims=True)
        dh = dy_ref[...].astype(F32) + r2 * weighted - h * (r2 * r2 * r2 * inner / D)
        dh_ref[...] = dh
        datt_s[...] = dh.astype(BF)
        for b in range(ROWS):
            rows = slice(b * FB, (b + 1) * FB)
            gg_ref[b] = row_sums(dn2[rows] * h[rows] * r2)

    do_s[...] = tn(w_ref[0, :, SLOT_W:], datt_s[...]).astype(BF)
    for j in range(QPK):
        rows = slice(j * HD, (j + 1) * HD)
        dl_s[j : j + 1] = jnp.sum(
            do_s[rows].astype(F32) * o_ref[0, rows].astype(F32), axis=0, keepdims=True
        )

    def fold(k, fresh):
        keys = kvs[k][0, :HD]
        values = kvs[k][0, HD:]
        bias = bias_ref[k]
        dk = jnp.zeros((HD, CP), F32)
        dv = jnp.zeros((HD, CP), F32)
        for j in range(QPK):
            rows = slice(j * HD, (j + 1) * HD)
            s = tn(keys, qs_ref[0, rows]) + bias
            p = jnp.exp(s - lse_ref[0, j : j + 1])
            do_j = do_s[rows]
            dp = tn(values, do_j)
            ds = (p * (dp - dl_s[j : j + 1])).astype(BF)
            dv = dv + nt(do_j, p.astype(BF))
            dk = dk + nt(qs_ref[0, rows], ds)
            dq = nn(keys, ds)
            if fresh:
                dq_s[rows] = dq
            else:
                dq_s[rows] += dq
        outs[k][0, :HD] = dk.astype(outs[k].dtype)
        outs[k][0, HD:] = dv.astype(outs[k].dtype)

    fold(0, True)
    for k in range(1, ROWS):
        pl.when(sc[4 + k] != 0)(functools.partial(fold, k, False))

        @pl.when(sc[4 + k] == 0)
        def _(k=k):
            outs[k][...] = jnp.zeros(outs[k].shape, outs[k].dtype)

    cos_a = cos_ref[...]
    sin_a = sin_ref[...]
    for j in range(QPK):
        first, second = rope(
            dq_s[j * HD : j * HD + HALF] * HD**-0.5,
            dq_s[j * HD + HALF : (j + 1) * HD] * HD**-0.5,
            cos_a, -sin_a,
        )
        dq_ref[0, j * HD : j * HD + HALF] = first.astype(BF)
        dq_ref[0, j * HD + HALF : (j + 1) * HD] = second.astype(BF)

    for b in range(ROWS):
        rows = slice(b * FB, (b + 1) * FB)
        block = jnp.concatenate(
            [nt(dq_ref[0], n1_ref[rows]).astype(BF), nt(o_ref[0], datt_s[rows]).astype(BF)], axis=0
        )
        for k in range(ROWS):

            @pl.when(g == k)
            def _(k=k, block=block, b=b):
                packs[k][b, :AW] = block

        @pl.when(g == GROUPS - 1)
        def _(block=block, b=b):
            for k in range(ROWS):
                share = AW // ROWS
                for q in range(ROWS):

                    @pl.when((sc[0] ^ k) == q)
                    def _(k=k, q=q):
                        packs[k][b, AW:] = block[q * share : (q + 1) * share]


def final_kernel(
    sc, dq_ref, d0, d1, d2, w_ref, n1_ref, cos_ref, sin_ref, x_ref, r1_ref, gain_ref, dh_ref, gg_ref,
    h_ref, mlp_a, mlp_b, mlp_c,
    pb0, pb1, pb2, pb3, out0, out1, out2, out3, dn_s, dpg_s, dx_s, lo_s,
):
    g = pl.program_id(0)
    packs = (pb0, pb1, pb2, pb3)
    outs = (out0, out1, out2, out3)
    dkv = d0[0] + d1[0].astype(F32) + d2[0].astype(F32)
    first, second = rope(dkv[:HALF], dkv[HALF:HD], cos_ref[...], -sin_ref[...])
    dpg_s[:QW] = dq_ref[0]
    dpg_s[QW : QW + HALF] = first.astype(BF)
    dpg_s[QW + HALF : QW + HD] = second.astype(BF)
    dpg_s[QW + HD :] = dkv[HD:].astype(BF)
    part = nn(w_ref[0, :, :SLOT_W], dpg_s[...])

    @pl.when(g == 0)
    def _():
        dn_s[...] = part

    @pl.when(g != 0)
    def _():
        dn_s[...] += part

    for b in range(ROWS):
        block = nt(dpg_s[QW:], n1_ref[b * FB : (b + 1) * FB]).astype(BF)
        for k in range(ROWS):

            @pl.when(g == k)
            def _(k=k, block=block, b=b):
                packs[k][b, :KV] = block

        @pl.when(g == GROUPS - 1)
        def _(block=block, b=b):
            share = KV // ROWS
            for k in range(ROWS):
                for q in range(ROWS):

                    @pl.when((sc[0] ^ k) == q)
                    def _(k=k, q=q):
                        packs[k][b, KV : KV + share] = block[q * share : (q + 1) * share]

    @pl.when(g == GROUPS - 1)
    def _():
        dn1 = dn_s[...]
        x = x_ref[...].astype(F32)
        r1 = r1_ref[...]
        weighted = dn1 * gain_ref[...]
        inner = jnp.sum(weighted * x, axis=0, keepdims=True)
        dx = dh_ref[...] + r1 * weighted - x * (r1 * r1 * r1 * inner / D)
        dx_s[...] = dx.astype(BF)
        row = lax.broadcasted_iota(jnp.int32, (16, FB), 0)
        for b in range(ROWS):
            rows = slice(b * FB, (b + 1) * FB)
            sums = row_sums(dn1[rows] * x[rows] * r1)
            sums = jnp.where(row == 0, sums, jnp.where(row == 1, gg_ref[b], 0.0)).astype(BF)
            for k in range(ROWS):
                packs[k][b, KV + KV // ROWS :] = sums
        lo_s[...] = (
            h_ref[...] + mlp_a[...].astype(F32) + mlp_b[...].astype(F32) + mlp_c[...].astype(F32)
        ).astype(BF)
        for k in range(ROWS):
            outs[k][:FB] = lo_s[rows_at(sc[0] ^ k)]
            outs[k][FB:] = dx_s[rows_at(sc[0] ^ k)]


def mlp_kernel(count, halves, sc, *refs):
    if halves:
        w = refs[-1]
        part = refs[0].shape[0] // ROWS
        for h in range(2):
            shift = (FB - part) * (sc[3] if h == 0 else 1 - sc[3])
            for b in range(ROWS):
                w[pl.ds(pl.multiple_of(b * FB + shift, 16), part)] = refs[h][b * part : (b + 1) * part]
        wd = refs[2]
        refs = refs[3:-1]
    else:
        w, wd = refs[:2]
        refs = refs[2:]
    width = wd.shape[1]
    for i in range(count):
        n2 = refs[i]
        dy = refs[count + i]
        a_ref, dg_ref, du_ref, mlp_ref, dn_ref = refs[2 * count + 5 * i : 2 * count + 5 * i + 5]
        step = 128
        for f in range(0, width, step):
            cols = slice(f, f + step)
            gate = tn(w[:, f : f + step], n2[...])
            up = tn(w[:, width + f : width + f + step], n2[...])
            da = tn(wd[:, cols], dy[...])
            sigma = jax.nn.sigmoid(gate)
            silu = gate * sigma
            a_ref[cols] = (silu * up).astype(BF)
            dg_ref[cols] = (da * up * sigma * (1.0 + gate * (1.0 - sigma))).astype(BF)
            du_ref[cols] = (da * silu).astype(BF)
        dn_ref[...] = (nn(w[:, :width], dg_ref[...]) + nn(w[:, width : 2 * width], du_ref[...])).astype(BF)
        mlp_ref[...] = nn(wd[...], a_ref[...]).astype(BF)


def mlp_grad_kernel(*refs):
    n2s, dys, acts, gates, ups = (refs[ROWS * i : ROWS * (i + 1)] for i in range(5))
    out = refs[-1]
    width = acts[0].shape[0]
    step = 128
    for part, (left, right) in enumerate(((n2s, gates), (n2s, ups), (dys, acts))):
        for f in range(0, width, step):
            total = nt(left[0][...], right[0][f : f + step])
            for k in range(1, ROWS):
                total = total + nt(left[k][...], right[k][f : f + step])
            out[:, part * width + f : part * width + f + step] = total.astype(BF)


def grads_kernel(sc, g_ref, o0, o1, o2, o3, qkv_ref, out_ref, gains_ref, oa_s, ob_s):
    ix = sc[0]
    share_a = AW // ROWS
    share_b = KV // ROWS
    for k, odd in enumerate((o0, o1, o2, o3)):
        oa_s[pl.ds(pl.multiple_of((ix ^ k) * share_a, 8), share_a)] = odd[:share_a]
        ob_s[pl.ds(pl.multiple_of((ix ^ k) * share_b, 8), share_b)] = odd[share_a:]
    live = (ix == sc[2]).astype(F32)
    oa = oa_s[...] * live
    ob = ob_s[...] * live
    qkv_ref[...] = jnp.transpose(
        jnp.concatenate([g_ref[:QW], g_ref[AP : AP + KV], oa[:QW], ob], axis=0)
    )
    out_ref[...] = jnp.transpose(jnp.concatenate([g_ref[QW:AW], oa[QW:]], axis=0))
    gains_ref[...] = g_ref[AP + KV + share_b : AP + KV + share_b + 8]


def whole(*shape):
    return pl.BlockSpec(shape, lambda *_: (0,) * len(shape))


def per_group(*shape):
    return pl.BlockSpec((1,) + shape, lambda g, *_: (g,) + (0,) * len(shape))


def kv_blocks():
    def spec(k):
        return pl.BlockSpec((1, KV, CP), lambda g, *_: (jnp.where(g < ROWS, g ^ k, g), 0, 0))

    return [spec(k) for k in range(ROWS)]


def sds(shape, dtype):
    return jax.ShapeDtypeStruct(shape, dtype)


MICROSECONDS = {
    "split_tokens": 3, "split_grad": 3, "join": 2, "qkv": 7, "attend": 18, "mlp_near": 13, "mlp_far": 13,
    "mlp_grad": 18, "attend_back": 30, "final": 19, "merge": 2, "grads": 3,
}


def cost(name):
    return pl.CostEstimate(
        flops=MICROSECONDS[name] * 100 * 10**6, bytes_accessed=MICROSECONDS[name] * 3000 * 100, transcendentals=0
    )


def simple(kernel, name, outs, *operands, scalars=None, scratch=(), limit=VMEM_LIMIT):
    specs = [pl.BlockSpec(memory_space=pltpu.VMEM)] * len(operands)
    if scalars is not None:
        specs = [pl.BlockSpec(memory_space=pltpu.SMEM)] + specs
        operands = (scalars,) + operands
    return pl.pallas_call(
        kernel,
        in_specs=specs,
        out_specs=[pl.BlockSpec(memory_space=pltpu.VMEM)] * len(outs),
        out_shape=list(outs),
        scratch_shapes=list(scratch),
        compiler_params=pltpu.CompilerParams(vmem_limit_bytes=limit),
        cost_estimate=cost(name),
        name=name,
    )(*operands)


def grouped(kernel, name, in_specs, outs, out_specs, scratch, sc, *operands):
    return pl.pallas_call(
        kernel,
        grid_spec=pltpu.PrefetchScalarGridSpec(
            num_scalar_prefetch=1,
            grid=(GROUPS,),
            in_specs=in_specs,
            out_specs=out_specs,
            scratch_shapes=scratch,
        ),
        out_shape=outs,
        compiler_params=pltpu.CompilerParams(vmem_limit_bytes=VMEM_LIMIT),
        cost_estimate=cost(name),
        name=name,
    )(sc, *operands)


def swap(values, bit):
    return lax.ppermute(values, "gx", [(i, i ^ bit) for i in range(ROWS)])


def row_gather(own):
    far = swap(own, 2)
    mate = swap(own, 1)
    return own, mate, far, swap(far, 1)


def after(values, *first):
    return lax.optimization_barrier((values,) + first)[0]


def row_near(blocks):
    far = (blocks[2].astype(F32) + swap(blocks[3], 1).astype(F32)).astype(BF)
    return blocks[0], swap(blocks[1], 1), far


def row_terms(blocks, first=()):
    a, b, far = row_near(blocks)
    if first:
        far = after(far, *first)
    return a, b, swap(far, 2)


def row_scatter(blocks, first=()):
    a, b, c = row_terms(blocks, first)
    return (a.astype(F32) + b.astype(F32) + c.astype(F32)).astype(BF)


def ring(values):
    return lax.ppermute(values, "gy", [(i, (i + 1) % ROWS) for i in range(ROWS)])


def ring_scatter(blocks, iy):
    def take(at):
        return lax.dynamic_index_in_dim(blocks, at % ROWS, 0, keepdims=False)

    moving = take(iy + 3)
    for s in range(ROWS - 1):
        moving = (ring(moving).astype(F32) + take(iy + 2 - s).astype(F32)).astype(BF)
    return moving


def dp_sum(values):
    if lax.axis_size("dp") == 2:
        return values.astype(F32) + lax.ppermute(values, "dp", [(0, 1), (1, 0)]).astype(F32)
    return lax.psum(values, "dp").astype(F32)


def to_tokens(pieces):
    out = []
    for k in range(ROWS):
        pairs = [(a * ROWS + b, (b ^ k) * ROWS + SEQ_MAP[a]) for a in range(ROWS) for b in range(ROWS)]
        out.append(lax.ppermute(pieces[k], ("gx", "gy"), pairs))
    return out


def to_features(pieces):
    back = []
    for k in range(ROWS):
        pairs = [(a * ROWS + b, SEQ_BACK[b] * ROWS + (a ^ k)) for a in range(ROWS) for b in range(ROWS)]
        back.append(lax.ppermute(pieces[k], ("gx", "gy"), pairs))
    return back


def per_device(
    tokens, segment_ids, slot_table, w_qkv, w_out, w_gate_up, w_down, gain_attn, gain_mlp, cotangent
):
    ix = lax.axis_index("gx")
    iy = lax.axis_index("gy")
    ff = w_down.shape[1]
    odd_row = jnp.sum(jnp.where(slot_table % 2 == 1, slot_table // 2, 0))

    seg = lax.ppermute(segment_ids, "gy", [(i, SEQ_MAP[i]) for i in range(ROWS)]).reshape(ROWS, CH)
    seg_own = lax.dynamic_index_in_dim(seg, ix, 0, keepdims=False)
    starts = [jnp.sum(seg < s).astype(jnp.int32) for s in range(SEGS)]
    first = sum(jnp.where(seg_own == s, starts[s], 0) for s in range(SEGS))
    at_own = jnp.arange(CP, dtype=jnp.int32)
    position = (ix * CH + at_own - jnp.pad(first, (0, CP - CH))).astype(F32)
    frequency = THETA_BASE ** (-2.0 * jnp.arange(HALF, dtype=F32) / HD)
    angles = frequency[:, None] * position[None, :]
    cos_a = jnp.cos(angles)
    sin_a = jnp.sin(angles)
    query_docs = jnp.pad(seg_own, (0, CP - CH), constant_values=-1)
    biases = []
    flags = []
    for k in range(ROWS):
        seg_k = lax.dynamic_index_in_dim(seg, ix ^ k, 0, keepdims=False)
        key_docs = jnp.pad(seg_k, (0, CP - CH), constant_values=-2)
        allowed = (key_docs[:, None] == query_docs[None, :]) & (
            ((ix ^ k) * CH + at_own)[:, None] <= (ix * CH + at_own)[None, :]
        )
        biases.append(jnp.where(allowed, 0.0, NEGATIVE).astype(F32))
        flags.append(((ix ^ k) <= ix) & (seg_k[CH - 1] >= seg_own[0]))
    bias = jnp.stack(biases)
    idp = lax.axis_index("dp")
    at = jnp.stack([ix, iy, odd_row, idp]).astype(jnp.int32)
    sc = jnp.concatenate([at, jnp.stack(flags).astype(jnp.int32)])

    piece = sds((FB, CP), BF)
    pieces = simple(
        functools.partial(split_kernel, True), "split_tokens", [piece] * ROWS,
        tokens, gain_attn[:, None], gain_mlp[:, None], scalars=at,
    )
    toks = to_tokens(pieces)
    odd = jnp.concatenate([w_qkv[:, SLOT_W:], w_out[:, QW:]], axis=1)
    odd = jnp.where(ix == odd_row, odd, jnp.zeros_like(odd))
    quarter = row_scatter([lax.dynamic_slice(odd, (0, ODD * (ix ^ k)), (FB, ODD)) for k in range(ROWS)])
    w_all = lax.all_gather(
        jnp.concatenate([w_qkv[:, :SLOT_W], w_out[:, :QW], quarter], axis=1),
        ("gx", "gy"), axis=0, tiled=True,
    ).reshape(ROWS, D, PACK + ODD)
    dy_pieces = simple(
        functools.partial(split_kernel, False), "split_grad", [piece] * ROWS,
        after(cotangent, pieces[0]), scalars=at,
    )
    dy_pieces = to_tokens(dy_pieces)
    toks[0] = after(toks[0], *dy_pieces)
    x, n1, r1, gain_one, gain_two, w5, qs, kv = simple(
        qkv_kernel, "qkv",
        [
            sds((D, CP), BF), sds((D, CP), BF), sds((1, CP), F32), sds((D, 1), F32), sds((D, 1), F32),
            sds((GROUPS, D, PACK), BF), sds((GROUPS, QW, CP), BF), sds((GROUPS, KV, CP), BF),
        ],
        *toks, w_all, cos_a, sin_a,
        scalars=at,
    )

    dy = simple(join_kernel, "join", [sds((D, CP), BF)], *dy_pieces, scalars=at)[0]
    w_gu = jnp.concatenate([w_gate_up[:, 0], w_gate_up[:, 1]], axis=1)
    halves = lax.axis_size("dp") == 2
    if halves:
        w_gu = lax.dynamic_slice(w_gu, ((FB - 128) * idp, 0), (128, 2 * ff))
    w_gu = [lax.all_gather(w_gu, "gy", axis=0, tiled=True)]
    if halves:
        w_gu.append(lax.ppermute(w_gu[0], "dp", [(0, 1), (1, 0)]))
    w_d = lax.all_gather(w_down, "gy", axis=0, tiled=True)

    kvs = row_gather(kv)
    dys = row_gather(after(dy, kvs[2]))
    o, lse, h, n2, r2 = grouped(
        attend_kernel, "attend",
        [per_group(QW, CP)] + kv_blocks()
        + [whole(ROWS, CP, CP), per_group(D, PACK), whole(D, CP), whole(D, 1)],
        [
            sds((GROUPS, QW, CP), BF), sds((GROUPS, 8, CP), F32), sds((D, CP), F32), sds((D, CP), BF),
            sds((1, CP), F32),
        ],
        [per_group(QW, CP), per_group(8, CP), whole(D, CP), whole(D, CP), whole(1, CP)],
        [pltpu.VMEM((8, CP), F32), pltpu.VMEM((8, CP), F32), pltpu.VMEM((QW, CP), F32)],
        sc, after(qs, w_gu[0]), *kvs, bias, w5, x, gain_two,
    )

    n2s = row_gather(n2)
    per_block = [sds((ff, CP), BF)] * 3 + [sds((D, CP), BF)] * 2
    def feed_forward(name, some_n2, some_dy):
        return simple(
            functools.partial(mlp_kernel, 2, halves), name, per_block * 2, *w_gu, w_d, *some_n2, *some_dy,
            scalars=at, scratch=[pltpu.VMEM((D, 2 * ff), BF)] if halves else [],
        )

    near = feed_forward("mlp_near", n2s[:2], dys[:2])
    far = feed_forward("mlp_far", n2s[2:], dys[2:])
    blocks = [near[:5], near[5:], far[:5], far[5:]]
    dn2_terms = list(row_near([b[4] for b in blocks]))
    mlp_terms = list(row_near([b[3] for b in blocks]))

    def beside_dn2(far, *operands):
        return swap(far, 2), simple(
            mlp_grad_kernel, "mlp_grad", [sds((D, 3 * ff), BF)],
            *operands,
        )[0]

    dn2_terms[2], g_mlp = beside_dn2(
        dn2_terms[2], *n2s, *dys, *[b[0] for b in blocks], *[b[1] for b in blocks], *[b[2] for b in blocks]
    )

    pack_a = sds((ROWS, AP, FB), BF)

    def beside_back(far, *operands):
        return swap(far, 2), grouped(
        attend_back_kernel, "attend_back",
        [per_group(QW, CP)] + kv_blocks()
        + [whole(ROWS, CP, CP), per_group(D, PACK), per_group(QW, CP), per_group(8, CP), whole(D, CP),
           whole(HALF, CP), whole(HALF, CP)]
        + [whole(D, CP)] * 4 + [whole(1, CP), whole(D, 1), whole(D, CP)],
        [sds((GROUPS, QW, CP), BF), sds((GROUPS, KV, CP), F32)] + [sds((GROUPS, KV, CP), BF)] * 3
        + [sds((D, CP), F32), sds((ROWS, 16, FB), F32)] + [pack_a] * ROWS,
        [per_group(QW, CP)] + kv_blocks() + [whole(D, CP), whole(ROWS, 16, FB)]
        + [whole(ROWS, AP, FB)] * ROWS,
        [pltpu.VMEM((D, CP), BF), pltpu.VMEM((QW, CP), BF), pltpu.VMEM((8, CP), F32), pltpu.VMEM((QW, CP), F32)],
            *operands,
        )

    g_down = lax.psum_scatter(g_mlp[:, 2 * ff :], "gy", scatter_dimension=0, tiled=True)
    g_gate_up = lax.psum_scatter(g_mlp[:, : 2 * ff], "gy", scatter_dimension=0, tiled=True)
    mlp_terms[2] = after(mlp_terms[2], dn2_terms[2])
    dn2_terms[1] = after(dn2_terms[1], g_mlp, mlp_terms[2])
    mlp_terms[2], back = beside_back(
        mlp_terms[2],
        sc, qs, *kvs, bias, w5, o, lse, n1, cos_a, sin_a, *dn2_terms, h, r2, gain_two, dy,
    )
    dq, dkv, dh, gg, packs_a = back[0], list(back[1:5]), back[5], back[6], back[7:]
    dkv[2] = after(dkv[2], mlp_terms[2], g_down)
    dkv_terms = list(row_terms(dkv))
    a_terms = list(row_near(packs_a))
    a_terms[2] = after(a_terms[2], dkv_terms[2])
    dkv_terms[0] = after(dkv_terms[0], a_terms[2])
    a_terms[2] = swap(a_terms[2], 2)
    final = grouped(
        final_kernel, "final",
        [per_group(QW, CP)] + [per_group(KV, CP)] * 3
        + [per_group(D, PACK), whole(D, CP), whole(HALF, CP), whole(HALF, CP), whole(D, CP), whole(1, CP),
           whole(D, 1), whole(D, CP), whole(ROWS, 16, FB)] + [whole(D, CP)] * 4,
        [sds((ROWS, BP, FB), BF)] * ROWS + [sds((2 * FB, CP), BF)] * ROWS,
        [whole(ROWS, BP, FB)] * ROWS + [whole(2 * FB, CP)] * ROWS,
        [pltpu.VMEM((D, CP), F32), pltpu.VMEM((SLOT_W, CP), BF)] + [pltpu.VMEM((D, CP), BF)] * 2,
        sc, dq, *dkv_terms, w5, n1, cos_a, sin_a, x, r1, gain_one, dh, gg, h, *mlp_terms,
    )
    packs_b, out_pieces = final[:ROWS], final[ROWS:]
    back = to_features(out_pieces)
    layer_out, input_grad = simple(merge_kernel, "merge", [sds((FB, L), BF)] * 2, *back, scalars=at)

    grad_down = dp_sum(g_down)
    g_mlp = dp_sum(g_gate_up)
    g_a = sum(term.astype(F32) for term in a_terms).astype(BF)
    packs_b = list(packs_b)
    packs_b[2] = after(packs_b[2], a_terms[2])
    g_all = jnp.concatenate([g_a, row_scatter(packs_b)], axis=1)
    g_all = ring_scatter(after(g_all, *back[:2]), iy)
    g_all = dp_sum(after(g_all, *back[2:]))
    odds = jnp.concatenate([g_all[AW:AP], g_all[AP + KV : AP + KV + KV // ROWS]], axis=0)
    grad_qkv, grad_out, grad_gains = simple(
        grads_kernel, "grads",
        [sds((FB, 2 * SLOT_W), F32), sds((FB, 2 * QW), F32), sds((8, FB), F32)],
        g_all, *row_gather(odds), scalars=at,
        scratch=[pltpu.VMEM((AW, FB), F32), pltpu.VMEM((KV, FB), F32)],
    )
    grad_gate_up = jnp.stack([g_mlp[:, :ff], g_mlp[:, ff : 2 * ff]], axis=1)
    return (
        layer_out,
        input_grad,
        grad_qkv,
        grad_out,
        grad_gate_up,
        grad_down,
        grad_gains[0],
        grad_gains[1],
    )


def solution(mesh):
    placed = (
        P("gy", ("dp", "gx")),
        P(("dp", "gy"), None),
        P(),
        P("gy", "gx"),
        P("gy", "gx"),
        P("gy", None, "gx"),
        P("gy", "gx"),
        P("gy"),
        P("gy"),
        P("gy", ("dp", "gx")),
    )
    return jax.shard_map(
        per_device,
        mesh=mesh,
        in_specs=placed,
        out_specs=(
            P("gy", ("dp", "gx")),
            P("gy", ("dp", "gx")),
            P("gy", "gx"),
            P("gy", "gx"),
            P("gy", None, "gx"),
            P("gy", "gx"),
            P("gy"),
            P("gy"),
        ),
        check_vma=False,
    )
```

profile of v0, /device:TPU:11, one launch (start us, length us, event | category | flops | bytes accessed | tf_op | source)
XLA Modules:
  0.0 489.9 jit_solution(10908341542492494574)
XLA Ops:
  22.0 2.7 split_tokens.1
  24.7 3.2 collective-permute-start.1
  27.9 2.5 split_grad.1
  30.4 4.5 collective-permute-start.2
  36.6 3.8 collective-permute-start
  40.4 14.1 %collective-permute-done = s32[1,1408]{1,0:T(1,128)S(1)} collective-permute-done((s32[1,1408]{1,0:T(1,128)S(1)}, s32[1,1408]{1,0:T(1,128)S(1)}, u32[]{:S(2)}, u32[]{:S(2)}) %collective-permute-start) | collective-permute-done | bytes 5664 | tf_op jit(solution)/shard_map/ppermute | solution.py:569
  54.5 4.4 collective-permute-start.5
  59.8 2.5 select_add_fusion
  62.4 8.0 %collective-permute-start.7 = (bf16[240,384]{1,0:T(8,128)(2,1)}, bf16[240,384]{1,0:T(8,128)(2,1)S(1)}, u32[]{:S(2)}, u32[]{:S(2)}) collective-permute-start(bf16[240,384]{1,0:T(8,128)(2,1)} %get-tuple-element.93), channel_id=1, source_target_pairs={{0,8},{1,12},{2,0},{3,4},{4,10},{5,14},{6,2},{7,6},{8,9},{9,13},{1... | collective-permute-start | bytes 552968 | tf_op jit(solution)/shard_map/ppermute | solution.py:549
  73.2 10.4 %collective-permute-done.7.refs_2_ = bf16[240,384]{1,0:T(8,128)(2,1)S(1)} collective-permute-done((bf16[240,384]{1,0:T(8,128)(2,1)}, bf16[240,384]{1,0:T(8,128)(2,1)S(1)}, u32[]{:S(2)}, u32[]{:S(2)}) %collective-permute-start.7) | collective-permute-done | bytes 184352 | tf_op jit(solution)/shard_map/ppermute | solution.py:549
  83.6 12.3 %collective-permute-done.8.refs_3_ = bf16[240,384]{1,0:T(8,128)(2,1)S(1)} collective-permute-done((bf16[240,384]{1,0:T(8,128)(2,1)}, bf16[240,384]{1,0:T(8,128)(2,1)S(1)}, u32[]{:S(2)}, u32[]{:S(2)}) %collective-permute-start.8) | collective-permute-done | bytes 184352 | tf_op jit(solution)/shard_map/ppermute | solution.py:549
  95.9 9.0 %all-gather.4.cloned.1.call-done = bf16[3840,640]{1,0:T(8,128)(2,1)} async-done(((bf16[240,640]{1,0:T(8,128)(2,1)}), bf16[3840,640]{1,0:T(8,128)(2,1)}) %all-gather.4.cloned.1.call-update) | async-done | bytes 4915216 | tf_op jit(solution)/shard_map/all_gather | solution.py:604
  104.9 8.0 %qkv.1 = (bf16[960,384]{1,0:T(8,128)(2,1)}, bf16[960,384]{1,0:T(8,128)(2,1)}, f32[1,384]{1,0:T(1,128)}, f32[960,1]{1,0:T(8,128)}, f32[960,1]{1,0:T(8,128)}, /*in...) custom-call(s32[4]{0:T(128)} %pad_add_fusion.sc, ...), custom_call_target="tpu_custom_call" | custom-call | flops 700000000 | bytes 2100000 | tf_op jit(solution)/shard_map/qkv/pallas_call | solution.py:465
  115.4 8.7 %collective-permute-done.13.kv2 = bf16[5,128,384]{2,1,0:T(8,128)(2,1)S(1)} collective-permute-done((bf16[5,128,384]{2,1,0:T(8,128)(2,1)}, bf16[5,128,384]{2,1,0:T(8,128)(2,1)S(1)}, u32[]{:S(2)}, u32[]{:S(2)}) %collective-permute-start.13) | collective-permute-done | bytes 491552 | tf_op jit(solution)/shard_map/ppermute | solution.py:495
  124.1 2.7 collective-permute-start.14
  136.0 2.2 join.1.refs_5_.refs_4_.dy_ref
  138.1 2.1 all-gather.6.cloned.1.call-done.refs_0_
  142.2 22.0 %attend.1 = (bf16[5,192,384]{2,1,0:T(8,128)(2,1)}, f32[5,8,384]{2,1,0:T(8,128)}, f32[960,384]{1,0:T(8,128)}, bf16[960,384]{1,0:T(8,128)(2,1)}, f32[1,384]{1,0:T(1,128)}) custom-call(s32[8]{0:T(128)} %concatenate.19.sc, bf16[5,192,384]{2,1,0:T(8,128)(2,1)} %get-tuple-element.98.qs_ref, bf16[5,128,384]{2,1,0:T(8,128)(2,1)} %get-tuple-element.96.kv0, ...), custom_call_target="tpu_custom_call" | custom-call | flops 1800000000 | bytes 5400000 | tf_op jit(solution)/shard_map/attend/pallas_call | solution.py:478
  164.8 8.3 %collective-permute-start.17 = (bf16[960,384]{1,0:T(8,128)(2,1)S(1)}, bf16[960,384]{1,0:T(8,128)(2,1)}, u32[]{:S(2)}, u32[]{:S(2)}) collective-permute-start(bf16[960,384]{1,0:T(8,128)(2,1)S(1)} %copy-done.1), channel_id=1, source_target_pairs={{0,4},{4,0},{8,12},{12,8},{1,5},{5,1},{9,13},{13,9},{2,6},{6,2},{1... | collective-permute-start | bytes 2211848 | tf_op jit(solution)/shard_map/ppermute | solution.py:495
  173.7 4.4 collective-permute-done.19.refs_3_.refs_2_
  178.1 10.3 %collective-permute-done.15.refs_1_ = bf16[512,1280]{1,0:T(8,128)(2,1)} collective-permute-done((bf16[512,1280]{1,0:T(8,128)(2,1)S(1)}, bf16[512,1280]{1,0:T(8,128)(2,1)}, u32[]{:S(2)}, u32[]{:S(2)}) %collective-permute-start.15) | collective-permute-done | bytes 1310752 | tf_op jit(solution)/shard_map/ppermute | solution.py:631
  188.3 12.8 %mlp_near.1 = (bf16[640,384]{1,0:T(8,128)(2,1)}, bf16[640,384]{1,0:T(8,128)(2,1)}, bf16[640,384]{1,0:T(8,128)(2,1)}, bf16[960,384]{1,0:T(8,128)(2,1)}, bf16[960,...) custom-call(s32[4]{0:T(128)} %pad_add_fusion.sc, ...), custom_call_target="tpu_custom_call" | custom-call | flops 1300000000 | bytes 3900000 | tf_op jit(solution)/shard_map/mlp_near/pallas_call | solution.py:465
  201.1 12.9 %mlp_far.1 = (bf16[640,384]{1,0:T(8,128)(2,1)}, bf16[640,384]{1,0:T(8,128)(2,1)}, bf16[640,384]{1,0:T(8,128)(2,1)}, bf16[960,384]{1,0:T(8,128)(2,1)}, bf16[960,3...) custom-call(s32[4]{0:T(128)} %pad_add_fusion.sc, ...), custom_call_target="tpu_custom_call" | custom-call | flops 1300000000 | bytes 3900000 | tf_op jit(solution)/shard_map/mlp_far/pallas_call | solution.py:465
  214.0 18.1 %mlp_grad.1 = bf16[960,1920]{1,0:T(8,128)(2,1)} custom-call(bf16[960,384]{1,0:T(8,128)(2,1)} %get-tuple-element.104.refs_3_.refs_0_, bf16[960,384]{1,0:T(8,128)(2,1)} %collective-permute-done.16.refs_4_.refs_1_, bf16[960,384]{1,0:T(8,128)(2,1)} %collective-permute-done.19.refs_3_.refs_2_, bf16[960,384]{1,0:T(8,128)(2,1)} %collective-permute-done.20.refs_4_.refs_3_, ...), custom_call_target="tpu_custom_call" | custom-call | flops 1800000000 | bytes 5400000 | tf_op jit(solution)/shard_map/mlp_grad/pallas_call | solution.py:465
  232.2 2.6 slice.84
  234.8 7.6 %collective-permute-start.24 = (bf16[960,384]{1,0:T(8,128)(2,1)S(1)}, bf16[960,384]{1,0:T(8,128)(2,1)S(1)}, u32[]{:S(2)}, u32[]{:S(2)}) collective-permute-start(bf16[960,384]{1,0:T(8,128)(2,1)S(1)} %copy-done.38), channel_id=1, source_target_pairs={{0,4},{4,0},{8,12},{12,8},{1,5},{5,1},{9,13},{13,9},{2,6},{6,2},{1... | collective-permute-start | bytes 2211848 | tf_op jit(solution)/shard_map/ppermute | solution.py:495
  246.5 15.7 %collective-permute-done.25.dn_c = bf16[960,384]{1,0:T(8,128)(2,1)S(1)} collective-permute-done((bf16[960,384]{1,0:T(8,128)(2,1)S(1)}, bf16[960,384]{1,0:T(8,128)(2,1)S(1)}, u32[]{:S(2)}, u32[]{:S(2)}) %collective-permute-start.25) | collective-permute-done | bytes 737312 | tf_op jit(solution)/shard_map/ppermute | solution.py:495
  264.4 36.3 %attend_back.1 = (bf16[5,192,384]{2,1,0:T(8,128)(2,1)}, f32[5,128,384]{2,1,0:T(8,128)}, bf16[5,128,384]{2,1,0:T(8,128)(2,1)}, bf16[5,128,384]{2,1,0:T(8,128)(2,1...) custom-call(s32[8]{0:T(128)} %concatenate.19.sc, ...), custom_call_target="tpu_custom_call" | custom-call | flops 3000000000 | bytes 9000000 | tf_op jit(solution)/shard_map/attend_back/pallas_call | solution.py:478
  305.7 11.8 %collective-permute-done.29.d2 = bf16[5,128,384]{2,1,0:T(8,128)(2,1)S(1)} collective-permute-done((bf16[5,128,384]{2,1,0:T(8,128)(2,1)S(1)}, bf16[5,128,384]{2,1,0:T(8,128)(2,1)S(1)}, u32[]{:S(2)}, u32[]{:S(2)}) %collective-permute-start.29) | collective-permute-done | bytes 491552 | tf_op jit(solution)/shard_map/ppermute | solution.py:495
  319.7 19.1 %final.1 = (bf16[4,176,240]{2,1,0:T(8,128)(2,1)}, bf16[4,176,240]{2,1,0:T(8,128)(2,1)}, bf16[4,176,240]{2,1,0:T(8,128)(2,1)}, bf16[4,176,240]{2,1,0:T(8,128)(2,1...) custom-call(s32[8]{0:T(128)} %concatenate.19.sc, ...), custom_call_target="tpu_custom_call" | custom-call | flops 1900000000 | bytes 5700000 | tf_op jit(solution)/shard_map/final/pallas_call | solution.py:478
  343.8 3.1 collective-permute-start.32
  347.8 4.2 collective-permute-done.40
  353.4 29.1 %collective-permute-done.32.refs_0_ = bf16[480,384]{1,0:T(8,128)(2,1)S(1)} collective-permute-done((bf16[480,384]{1,0:T(8,128)(2,1)}, bf16[480,384]{1,0:T(8,128)(2,1)S(1)}, u32[]{:S(2)}, u32[]{:S(2)}) %collective-permute-start.32) | collective-permute-done | bytes 368672 | tf_op jit(solution)/shard_map/ppermute | solution.py:557
  382.5 11.7 %collective-permute-done.33.refs_1_ = bf16[480,384]{1,0:T(8,128)(2,1)} collective-permute-done((bf16[480,384]{1,0:T(8,128)(2,1)}, bf16[480,384]{1,0:T(8,128)(2,1)}, u32[]{:S(2)}, u32[]{:S(2)}) %collective-permute-start.33) | collective-permute-done | bytes 368672 | tf_op jit(solution)/shard_map/ppermute | solution.py:557
  394.3 7.4 %collective-permute-done.41 = bf16[656,240]{1,0:T(8,128)(2,1)S(1)} collective-permute-done((bf16[656,240]{1,0:T(8,128)(2,1)S(1)}, bf16[656,240]{1,0:T(8,128)(2,1)S(1)}, u32[]{:S(2)}, u32[]{:S(2)}) %collective-permute-start.41) | collective-permute-done | bytes 314912 | tf_op jit(solution)/shard_map/ppermute | solution.py:526
  401.8 2.3 collective-permute-start.42
  404.0 6.6 %collective-permute-done.42 = bf16[656,240]{1,0:T(8,128)(2,1)S(1)} collective-permute-done((bf16[656,240]{1,0:T(8,128)(2,1)S(1)}, bf16[656,240]{1,0:T(8,128)(2,1)S(1)}, u32[]{:S(2)}, u32[]{:S(2)}) %collective-permute-start.42) | collective-permute-done | bytes 314912 | tf_op jit(solution)/shard_map/ppermute | solution.py:526
  410.7 2.2 collective-permute-start.43
  413.6 4.3 collective-permute-start.35
  418.2 3.4 collective-permute-done.43
  421.6 22.6 %collective-permute-done.34.refs_2_ = bf16[480,384]{1,0:T(8,128)(2,1)S(1)} collective-permute-done((bf16[480,384]{1,0:T(8,128)(2,1)}, bf16[480,384]{1,0:T(8,128)(2,1)S(1)}, u32[]{:S(2)}, u32[]{:S(2)}) %collective-permute-start.34) | collective-permute-done | bytes 368672 | tf_op jit(solution)/shard_map/ppermute | solution.py:557
  444.2 8.0 %collective-permute-done.35.refs_3_ = bf16[480,384]{1,0:T(8,128)(2,1)S(1)} collective-permute-done((bf16[480,384]{1,0:T(8,128)(2,1)}, bf16[480,384]{1,0:T(8,128)(2,1)S(1)}, u32[]{:S(2)}, u32[]{:S(2)}) %collective-permute-start.35) | collective-permute-done | bytes 368672 | tf_op jit(solution)/shard_map/ppermute | solution.py:557
  453.7 1.9 convert_add_fusion.5
  455.7 2.7 merge.1
  458.4 2.8 collective-permute-done.44
  461.5 2.3 collective-permute-start.45
  463.7 10.7 %collective-permute-done.48 = bf16[240,1280]{1,0:T(8,128)(2,1)S(1)} collective-permute-done((bf16[240,1280]{1,0:T(8,128)(2,1)}, bf16[240,1280]{1,0:T(8,128)(2,1)S(1)}, u32[]{:S(2)}, u32[]{:S(2)}) %collective-permute-start.48) | collective-permute-done | bytes 614432 | tf_op jit(solution)/shard_map/ppermute | solution.py:541
  479.1 2.5 grads.1
  (217 shorter events, 58.6 us)
Async XLA Ops:
  7.2 97.7 %all-gather.4.cloned.1.call-start = ((), (), s32[]{:S(2)}) async-start(), calls=%async_computation.2 | async-start | bytes 5222400 | tf_op jit(solution)/shard_map/all_gather | solution.py:604
  17.3 122.9 %all-gather.6.cloned.1.call-start = ((), (), s32[]{:S(2)}) async-start(), calls=%async_computation.3 | async-start | bytes 1638400 | tf_op jit(solution)/shard_map/all_gather | solution.py:629
  19.2 158.9 %all-gather.8.cloned.1.call-start = ((), (), s32[]{:S(2)}) async-start(), calls=%async_computation.4 | async-start | bytes 1536000 | tf_op jit(solution)/shard_map/all_gather | solution.py:632
  24.7 48.4 %collective-permute-start.1 = (bf16[240,384]{1,0:T(8,128)(2,1)}, bf16[240,384]{1,0:T(8,128)(2,1)S(1)}, u32[]{:S(2)}, u32[]{:S(2)}) collective-permute-start(bf16[240,384]{1,0:T(8,128)(2,1)} %get-tuple-element.85), channel_id=1, source_target_pairs={{0,0},{1,4},{2,8},{3,12},{4,2},{5,6},{6,10},{7,14},{8,1},{9,5},{10... | collective-permute-start | bytes 552968 | tf_op jit(solution)/shard_map/ppermute | solution.py:549
  30.4 31.9 %collective-permute-start.2 = (bf16[240,384]{1,0:T(8,128)(2,1)}, bf16[240,384]{1,0:T(8,128)(2,1)S(1)}, u32[]{:S(2)}, u32[]{:S(2)}) collective-permute-start(bf16[240,384]{1,0:T(8,128)(2,1)} %get-tuple-element.87), channel_id=1, source_target_pairs={{0,0},{1,4},{2,8},{3,12},{4,2},{5,6},{6,10},{7,14},{8,1},{9,5},{10... | collective-permute-start | bytes 552968 | tf_op jit(solution)/shard_map/ppermute | solution.py:549
  34.9 27.4 %collective-permute-start.3 = (bf16[240,384]{1,0:T(8,128)(2,1)}, bf16[240,384]{1,0:T(8,128)(2,1)S(1)}, u32[]{:S(2)}, u32[]{:S(2)}) collective-permute-start(bf16[240,384]{1,0:T(8,128)(2,1)} %get-tuple-element.88), channel_id=1, source_target_pairs={{0,4},{1,0},{2,12},{3,8},{4,6},{5,2},{6,14},{7,10},{8,5},{9,1},{10... | collective-permute-start | bytes 552968 | tf_op jit(solution)/shard_map/ppermute | solution.py:549
  36.6 33.8 %collective-permute-start.4 = (bf16[240,384]{1,0:T(8,128)(2,1)}, bf16[240,384]{1,0:T(8,128)(2,1)S(1)}, u32[]{:S(2)}, u32[]{:S(2)}) collective-permute-start(bf16[240,384]{1,0:T(8,128)(2,1)} %get-tuple-element.89), channel_id=1, source_target_pairs={{0,8},{1,12},{2,0},{3,4},{4,10},{5,14},{6,2},{7,6},{8,9},{9,13},{1... | collective-permute-start | bytes 552968 | tf_op jit(solution)/shard_map/ppermute | solution.py:549
  36.6 17.9 %collective-permute-start = (s32[1,1408]{1,0:T(1,128)S(1)}, s32[1,1408]{1,0:T(1,128)S(1)}, u32[]{:S(2)}, u32[]{:S(2)}) collective-permute-start(s32[1,1408]{1,0:T(1,128)S(1)} %copy-done.40), channel_id=1, source_target_pairs={{0,0},{1,2},{2,1},{3,3},{4,4},{5,6},{6,5},{7,7},{8,8},{9,10},{10,9... | collective-permute-start | bytes 16904 | tf_op jit(solution)/shard_map/ppermute | solution.py:569
  54.5 18.7 %collective-permute-start.5 = (bf16[240,384]{1,0:T(8,128)(2,1)}, bf16[240,384]{1,0:T(8,128)(2,1)S(1)}, u32[]{:S(2)}, u32[]{:S(2)}) collective-permute-start(bf16[240,384]{1,0:T(8,128)(2,1)} %get-tuple-element.90), channel_id=1, source_target_pairs={{0,12},{1,8},{2,4},{3,0},{4,14},{5,10},{6,6},{7,2},{8,13},{9,9},{1... | collective-permute-start | bytes 552968 | tf_op jit(solution)/shard_map/ppermute | solution.py:549
  62.3 10.9 %collective-permute-start.6 = (bf16[240,384]{1,0:T(8,128)(2,1)}, bf16[240,384]{1,0:T(8,128)(2,1)S(1)}, u32[]{:S(2)}, u32[]{:S(2)}) collective-permute-start(bf16[240,384]{1,0:T(8,128)(2,1)} %get-tuple-element.92), channel_id=1, source_target_pairs={{0,4},{1,0},{2,12},{3,8},{4,6},{5,2},{6,14},{7,10},{8,5},{9,1},{10... | collective-permute-start | bytes 552968 | tf_op jit(solution)/shard_map/ppermute | solution.py:549
  62.4 21.2 %collective-permute-start.7 = (bf16[240,384]{1,0:T(8,128)(2,1)}, bf16[240,384]{1,0:T(8,128)(2,1)S(1)}, u32[]{:S(2)}, u32[]{:S(2)}) collective-permute-start(bf16[240,384]{1,0:T(8,128)(2,1)} %get-tuple-element.93), channel_id=1, source_target_pairs={{0,8},{1,12},{2,0},{3,4},{4,10},{5,14},{6,2},{7,6},{8,9},{9,13},{1... | collective-permute-start | bytes 552968 | tf_op jit(solution)/shard_map/ppermute | solution.py:549
  70.4 25.5 %collective-permute-start.8 = (bf16[240,384]{1,0:T(8,128)(2,1)}, bf16[240,384]{1,0:T(8,128)(2,1)S(1)}, u32[]{:S(2)}, u32[]{:S(2)}) collective-permute-start(bf16[240,384]{1,0:T(8,128)(2,1)} %get-tuple-element.94), channel_id=1, source_target_pairs={{0,12},{1,8},{2,4},{3,0},{4,14},{5,10},{6,6},{7,2},{8,13},{9,9},{1... | collective-permute-start | bytes 552968 | tf_op jit(solution)/shard_map/ppermute | solution.py:549
  113.0 11.2 %collective-permute-start.13 = (bf16[5,128,384]{2,1,0:T(8,128)(2,1)}, bf16[5,128,384]{2,1,0:T(8,128)(2,1)S(1)}, u32[]{:S(2)}, u32[]{:S(2)}) collective-permute-start(bf16[5,128,384]{2,1,0:T(8,128)(2,1)} %get-tuple-element.96.kv0), channel_id=1, source_target_pairs={{0,8},{4,12},{8,0},{12,4},{1,9},{5,13},{9,1},{13,5},{2,10},{6,14},... | collective-permute-start | bytes 1474568 | tf_op jit(solution)/shard_map/ppermute | solution.py:495
  113.7 189.2 %reduce-scatter.3.cloned.1.call-start = ((), (), s32[]{:S(2)}) async-start(), calls=%async_computation.5 | async-start | bytes 1536000 | tf_op jit(solution)/shard_map/reduce_scatter | solution.py:690
  114.1 27.4 %collective-permute-start.12 = (bf16[5,128,384]{2,1,0:T(8,128)(2,1)}, bf16[5,128,384]{2,1,0:T(8,128)(2,1)S(1)}, u32[]{:S(2)}, u32[]{:S(2)}) collective-permute-start(bf16[5,128,384]{2,1,0:T(8,128)(2,1)} %get-tuple-element.96.kv0), channel_id=1, source_target_pairs={{0,4},{4,0},{8,12},{12,8},{1,5},{5,1},{9,13},{13,9},{2,6},{6,2},{1... | collective-permute-start | bytes 1474568 | tf_op jit(solution)/shard_map/ppermute | solution.py:495
  124.1 17.3 %collective-permute-start.14 = (bf16[5,128,384]{2,1,0:T(8,128)(2,1)S(1)}, bf16[5,128,384]{2,1,0:T(8,128)(2,1)}, u32[]{:S(2)}, u32[]{:S(2)}) collective-permute-start(bf16[5,128,384]{2,1,0:T(8,128)(2,1)S(1)} %collective-permute-done.13.kv2), channel_id=1, source_target_pairs={{0,4},{4,0},{8,12},{12,8},{1,5},{5,1},{9,13},{13,9},{2,6},{6,2},{1... | collective-permute-start | bytes 1474568 | tf_op jit(solution)/shard_map/ppermute | solution.py:495
  140.3 32.9 %collective-permute-start.21 = (bf16[960,384]{1,0:T(8,128)(2,1)}, bf16[960,384]{1,0:T(8,128)(2,1)S(1)}, u32[]{:S(2)}, u32[]{:S(2)}) collective-permute-start(bf16[960,384]{1,0:T(8,128)(2,1)} %join.1.refs_5_.refs_4_.dy_ref), channel_id=1, source_target_pairs={{0,8},{4,12},{8,0},{12,4},{1,9},{5,13},{9,1},{13,5},{2,10},{6,14},... | collective-permute-start | bytes 2211848 | tf_op jit(solution)/shard_map/ppermute | solution.py:495
  164.2 13.8 %collective-permute-start.19 = (bf16[960,384]{1,0:T(8,128)(2,1)}, bf16[960,384]{1,0:T(8,128)(2,1)}, u32[]{:S(2)}, u32[]{:S(2)}) collective-permute-start(bf16[960,384]{1,0:T(8,128)(2,1)} %get-tuple-element.104.refs_3_.refs_0_), channel_id=1, source_target_pairs={{0,8},{4,12},{8,0},{12,4},{1,9},{5,13},{9,1},{13,5},{2,10},{6,14},... | collective-permute-start | bytes 2211848 | tf_op jit(solution)/shard_map/ppermute | solution.py:495
  164.6 23.8 %collective-permute-start.15 = (bf16[512,1280]{1,0:T(8,128)(2,1)S(1)}, bf16[512,1280]{1,0:T(8,128)(2,1)}, u32[]{:S(2)}, u32[]{:S(2)}) collective-permute-start(bf16[512,1280]{1,0:T(8,128)(2,1)S(1)} %copy-done.2), channel_id=1, source_target_pairs={{0,16},{16,0},{1,17},{17,1},{2,18},{18,2},{3,19},{19,3},{4,20},{20... | collective-permute-start | bytes 3932168 | tf_op jit(solution)/shard_map/ppermute | solution.py:631
  164.8 23.5 %collective-permute-start.17 = (bf16[960,384]{1,0:T(8,128)(2,1)S(1)}, bf16[960,384]{1,0:T(8,128)(2,1)}, u32[]{:S(2)}, u32[]{:S(2)}) collective-permute-start(bf16[960,384]{1,0:T(8,128)(2,1)S(1)} %copy-done.1), channel_id=1, source_target_pairs={{0,4},{4,0},{8,12},{12,8},{1,5},{5,1},{9,13},{13,9},{2,6},{6,2},{1... | collective-permute-start | bytes 2211848 | tf_op jit(solution)/shard_map/ppermute | solution.py:495
  173.2 15.2 %collective-permute-start.16 = (bf16[960,384]{1,0:T(8,128)(2,1)}, bf16[960,384]{1,0:T(8,128)(2,1)}, u32[]{:S(2)}, u32[]{:S(2)}) collective-permute-start(bf16[960,384]{1,0:T(8,128)(2,1)} %get-tuple-element.104.refs_3_.refs_0_), channel_id=1, source_target_pairs={{0,4},{4,0},{8,12},{12,8},{1,5},{5,1},{9,13},{13,9},{2,6},{6,2},{1... | collective-permute-start | bytes 2211848 | tf_op jit(solution)/shard_map/ppermute | solution.py:495
  173.2 27.9 %collective-permute-start.22 = (bf16[960,384]{1,0:T(8,128)(2,1)S(1)}, bf16[960,384]{1,0:T(8,128)(2,1)}, u32[]{:S(2)}, u32[]{:S(2)}) collective-permute-start(bf16[960,384]{1,0:T(8,128)(2,1)S(1)} %collective-permute-done.21.refs_5_.refs_6_), channel_id=1, source_target_pairs={{0,4},{4,0},{8,12},{12,8},{1,5},{5,1},{9,13},{13,9},{2,6},{6,2},{1... | collective-permute-start | bytes 2211848 | tf_op jit(solution)/shard_map/ppermute | solution.py:495
  178.1 23.1 %collective-permute-start.20 = (bf16[960,384]{1,0:T(8,128)(2,1)}, bf16[960,384]{1,0:T(8,128)(2,1)}, u32[]{:S(2)}, u32[]{:S(2)}) collective-permute-start(bf16[960,384]{1,0:T(8,128)(2,1)} %collective-permute-done.19.refs_3_.refs_2_), channel_id=1, source_target_pairs={{0,4},{4,0},{8,12},{12,8},{1,5},{5,1},{9,13},{13,9},{2,6},{6,2},{1... | collective-permute-start | bytes 2211848 | tf_op jit(solution)/shard_map/ppermute | solution.py:495
  234.8 217.5 %reduce-scatter.5.cloned.1.call-start = ((), (), s32[]{:S(2)}) async-start(), calls=%async_computation.6 | async-start | bytes 3072000 | tf_op jit(solution)/shard_map/reduce_scatter | solution.py:691
  234.8 9.4 %collective-permute-start.24 = (bf16[960,384]{1,0:T(8,128)(2,1)S(1)}, bf16[960,384]{1,0:T(8,128)(2,1)S(1)}, u32[]{:S(2)}, u32[]{:S(2)}) collective-permute-start(bf16[960,384]{1,0:T(8,128)(2,1)S(1)} %copy-done.38), channel_id=1, source_target_pairs={{0,4},{4,0},{8,12},{12,8},{1,5},{5,1},{9,13},{13,9},{2,6},{6,2},{1... | collective-permute-start | bytes 2211848 | tf_op jit(solution)/shard_map/ppermute | solution.py:495
  244.4 17.9 %collective-permute-start.25 = (bf16[960,384]{1,0:T(8,128)(2,1)S(1)}, bf16[960,384]{1,0:T(8,128)(2,1)S(1)}, u32[]{:S(2)}, u32[]{:S(2)}) collective-permute-start(bf16[960,384]{1,0:T(8,128)(2,1)S(1)} %add_convert_fusion.2), channel_id=1, source_target_pairs={{0,8},{4,12},{8,0},{12,4},{1,9},{5,13},{9,1},{13,5},{2,10},{6,14},... | collective-permute-start | bytes 2211848 | tf_op jit(solution)/shard_map/ppermute | solution.py:495
  245.7 17.8 %collective-permute-start.18 = (bf16[960,384]{1,0:T(8,128)(2,1)}, bf16[960,384]{1,0:T(8,128)(2,1)S(1)}, u32[]{:S(2)}, u32[]{:S(2)}) collective-permute-start(bf16[960,384]{1,0:T(8,128)(2,1)} %get-tuple-element.107), channel_id=1, source_target_pairs={{0,4},{4,0},{8,12},{12,8},{1,5},{5,1},{9,13},{13,9},{2,6},{6,2},{1... | collective-permute-start | bytes 2211848 | tf_op jit(solution)/shard_map/ppermute | solution.py:495
  262.3 40.6 %collective-permute-start.27 = (bf16[960,384]{1,0:T(8,128)(2,1)S(1)}, bf16[960,384]{1,0:T(8,128)(2,1)S(1)}, u32[]{:S(2)}, u32[]{:S(2)}) collective-permute-start(bf16[960,384]{1,0:T(8,128)(2,1)S(1)} %add_convert_fusion.3), channel_id=1, source_target_pairs={{0,8},{4,12},{8,0},{12,4},{1,9},{5,13},{9,1},{13,5},{2,10},{6,14},... | collective-permute-start | bytes 2211848 | tf_op jit(solution)/shard_map/ppermute | solution.py:495
  300.7 4.7 collective-permute-start.26
  304.6 12.9 %collective-permute-start.29 = (bf16[5,128,384]{2,1,0:T(8,128)(2,1)S(1)}, bf16[5,128,384]{2,1,0:T(8,128)(2,1)S(1)}, u32[]{:S(2)}, u32[]{:S(2)}) collective-permute-start(bf16[5,128,384]{2,1,0:T(8,128)(2,1)S(1)} %add_convert_fusion.4), channel_id=1, source_target_pairs={{0,8},{4,12},{8,0},{12,4},{1,9},{5,13},{9,1},{13,5},{2,10},{6,14},... | collective-permute-start | bytes 1474568 | tf_op jit(solution)/shard_map/ppermute | solution.py:495
  304.9 13.9 %collective-permute-start.31 = (bf16[960,384]{1,0:T(8,128)(2,1)S(1)}, bf16[960,384]{1,0:T(8,128)(2,1)S(1)}, u32[]{:S(2)}, u32[]{:S(2)}) collective-permute-start(bf16[960,384]{1,0:T(8,128)(2,1)S(1)} %copy-done.36), channel_id=1, source_target_pairs={{0,4},{4,0},{8,12},{12,8},{1,5},{5,1},{9,13},{13,9},{2,6},{6,2},{1... | collective-permute-start | bytes 2211848 | tf_op jit(solution)/shard_map/ppermute | solution.py:495
  305.2 13.6 %collective-permute-start.30 = (bf16[5,128,384]{2,1,0:T(8,128)(2,1)S(1)}, bf16[5,128,384]{2,1,0:T(8,128)(2,1)}, u32[]{:S(2)}, u32[]{:S(2)}) collective-permute-start(bf16[5,128,384]{2,1,0:T(8,128)(2,1)S(1)} %copy-done.39), channel_id=1, source_target_pairs={{0,4},{4,0},{8,12},{12,8},{1,5},{5,1},{9,13},{13,9},{2,6},{6,2},{1... | collective-permute-start | bytes 1474568 | tf_op jit(solution)/shard_map/ppermute | solution.py:495
  317.5 22.5 %collective-permute-start.37 = (bf16[4,480,240]{2,1,0:T(8,128)(2,1)S(1)}, bf16[4,480,240]{2,1,0:T(8,128)(2,1)S(1)}, u32[]{:S(2)}, u32[]{:S(2)}) collective-permute-start(bf16[4,480,240]{2,1,0:T(8,128)(2,1)S(1)} %add_convert_fusion.1), channel_id=1, source_target_pairs={{0,8},{4,12},{8,0},{12,4},{1,9},{5,13},{9,1},{13,5},{2,10},{6,14},... | collective-permute-start | bytes 2764808 | tf_op jit(solution)/shard_map/ppermute | solution.py:495
  317.7 29.7 %collective-permute-start.36 = (bf16[4,480,240]{2,1,0:T(8,128)(2,1)}, bf16[4,480,240]{2,1,0:T(8,128)(2,1)S(1)}, u32[]{:S(2)}, u32[]{:S(2)}) collective-permute-start(bf16[4,480,240]{2,1,0:T(8,128)(2,1)} %get-tuple-element.151), channel_id=1, source_target_pairs={{0,4},{4,0},{8,12},{12,8},{1,5},{5,1},{9,13},{13,9},{2,6},{6,2},{1... | collective-permute-start | bytes 2764808 | tf_op jit(solution)/shard_map/ppermute | solution.py:495
  338.9 8.9 %collective-permute-start.38 = (bf16[4,176,240]{2,1,0:T(8,128)(2,1)}, bf16[4,176,240]{2,1,0:T(8,128)(2,1)}, u32[]{:S(2)}, u32[]{:S(2)}) collective-permute-start(bf16[4,176,240]{2,1,0:T(8,128)(2,1)} %get-tuple-element.153), channel_id=1, source_target_pairs={{0,4},{4,0},{8,12},{12,8},{1,5},{5,1},{9,13},{13,9},{2,6},{6,2},{1... | collective-permute-start | bytes 1013768 | tf_op jit(solution)/shard_map/ppermute | solution.py:495
  342.6 9.4 %collective-permute-start.40 = (bf16[4,176,240]{2,1,0:T(8,128)(2,1)}, bf16[4,176,240]{2,1,0:T(8,128)(2,1)}, u32[]{:S(2)}, u32[]{:S(2)}) collective-permute-start(bf16[4,176,240]{2,1,0:T(8,128)(2,1)} %add_convert_fusion.6), channel_id=1, source_target_pairs={{0,8},{4,12},{8,0},{12,4},{1,9},{5,13},{9,1},{13,5},{2,10},{6,14},... | collective-permute-start | bytes 1013768 | tf_op jit(solution)/shard_map/ppermute | solution.py:495
  343.8 38.7 %collective-permute-start.32 = (bf16[480,384]{1,0:T(8,128)(2,1)}, bf16[480,384]{1,0:T(8,128)(2,1)S(1)}, u32[]{:S(2)}, u32[]{:S(2)}) collective-permute-start(bf16[480,384]{1,0:T(8,128)(2,1)} %get-tuple-element.144), channel_id=1, source_target_pairs={{0,0},{1,8},{2,4},{3,12},{4,1},{5,9},{6,5},{7,13},{8,2},{9,10},{10... | collective-permute-start | bytes 1105928 | tf_op jit(solution)/shard_map/ppermute | solution.py:557
  347.0 47.2 %collective-permute-start.33 = (bf16[480,384]{1,0:T(8,128)(2,1)}, bf16[480,384]{1,0:T(8,128)(2,1)}, u32[]{:S(2)}, u32[]{:S(2)}) collective-permute-start(bf16[480,384]{1,0:T(8,128)(2,1)} %get-tuple-element.145), channel_id=1, source_target_pairs={{0,1},{1,9},{2,5},{3,13},{4,0},{5,8},{6,4},{7,12},{8,3},{9,11},{10... | collective-permute-start | bytes 1105928 | tf_op jit(solution)/shard_map/ppermute | solution.py:557
  394.2 7.4 %collective-permute-start.41 = (bf16[656,240]{1,0:T(8,128)(2,1)S(1)}, bf16[656,240]{1,0:T(8,128)(2,1)S(1)}, u32[]{:S(2)}, u32[]{:S(2)}) collective-permute-start(bf16[656,240]{1,0:T(8,128)(2,1)S(1)} %dynamic-slice_bitcast_fusion), channel_id=1, source_target_pairs={{0,1},{1,2},{2,3},{3,0},{4,5},{5,6},{6,7},{7,4},{8,9},{9,10},{10,1... | collective-permute-start | bytes 944648 | tf_op jit(solution)/shard_map/ppermute | solution.py:526
  401.8 8.9 %collective-permute-start.42 = (bf16[656,240]{1,0:T(8,128)(2,1)S(1)}, bf16[656,240]{1,0:T(8,128)(2,1)S(1)}, u32[]{:S(2)}, u32[]{:S(2)}) collective-permute-start(bf16[656,240]{1,0:T(8,128)(2,1)S(1)} %fusion.2), channel_id=1, source_target_pairs={{0,1},{1,2},{2,3},{3,0},{4,5},{5,6},{6,7},{7,4},{8,9},{9,10},{10,1... | collective-permute-start | bytes 944648 | tf_op jit(solution)/shard_map/ppermute | solution.py:526
  410.7 10.8 %collective-permute-start.43 = (bf16[656,240]{1,0:T(8,128)(2,1)S(1)}, bf16[656,240]{1,0:T(8,128)(2,1)S(1)}, u32[]{:S(2)}, u32[]{:S(2)}) collective-permute-start(bf16[656,240]{1,0:T(8,128)(2,1)S(1)} %fusion.1), channel_id=1, source_target_pairs={{0,1},{1,2},{2,3},{3,0},{4,5},{5,6},{6,7},{7,4},{8,9},{9,10},{10,1... | collective-permute-start | bytes 944648 | tf_op jit(solution)/shard_map/ppermute | solution.py:526
  412.9 31.3 %collective-permute-start.34 = (bf16[480,384]{1,0:T(8,128)(2,1)}, bf16[480,384]{1,0:T(8,128)(2,1)S(1)}, u32[]{:S(2)}, u32[]{:S(2)}) collective-permute-start(bf16[480,384]{1,0:T(8,128)(2,1)} %get-tuple-element.146), channel_id=1, source_target_pairs={{0,2},{1,10},{2,6},{3,14},{4,3},{5,11},{6,7},{7,15},{8,0},{9,8},{1... | collective-permute-start | bytes 1105928 | tf_op jit(solution)/shard_map/ppermute | solution.py:557
  413.6 38.7 %collective-permute-start.35 = (bf16[480,384]{1,0:T(8,128)(2,1)}, bf16[480,384]{1,0:T(8,128)(2,1)S(1)}, u32[]{:S(2)}, u32[]{:S(2)}) collective-permute-start(bf16[480,384]{1,0:T(8,128)(2,1)} %get-tuple-element.147), channel_id=1, source_target_pairs={{0,3},{1,11},{2,7},{3,15},{4,2},{5,10},{6,6},{7,14},{8,1},{9,9},{1... | collective-permute-start | bytes 1105928 | tf_op jit(solution)/shard_map/ppermute | solution.py:557
  417.9 35.8 %collective-permute-start.49 = (bf16[240,640]{1,0:T(8,128)(2,1)}, bf16[240,640]{1,0:T(8,128)(2,1)}, u32[]{:S(2)}, u32[]{:S(2)}) collective-permute-start(bf16[240,640]{1,0:T(8,128)(2,1)} %reduce-scatter.3.cloned.1.call-done), channel_id=1, source_target_pairs={{0,16},{16,0},{1,17},{17,1},{2,18},{18,2},{3,19},{19,3},{4,20},{20... | collective-permute-start | bytes 921608 | tf_op jit(solution)/shard_map/ppermute | solution.py:541
  452.2 9.0 %collective-permute-start.44 = (bf16[656,240]{1,0:T(8,128)(2,1)S(1)}, bf16[656,240]{1,0:T(8,128)(2,1)S(1)}, u32[]{:S(2)}, u32[]{:S(2)}) collective-permute-start(bf16[656,240]{1,0:T(8,128)(2,1)S(1)} %fusion), channel_id=1, source_target_pairs={{0,16},{16,0},{1,17},{17,1},{2,18},{18,2},{3,19},{19,3},{4,20},{20... | collective-permute-start | bytes 944648 | tf_op jit(solution)/shard_map/ppermute | solution.py:541
  452.3 22.2 %collective-permute-start.48 = (bf16[240,1280]{1,0:T(8,128)(2,1)}, bf16[240,1280]{1,0:T(8,128)(2,1)S(1)}, u32[]{:S(2)}, u32[]{:S(2)}) collective-permute-start(bf16[240,1280]{1,0:T(8,128)(2,1)} %reduce-scatter.5.cloned.1.call-done), channel_id=1, source_target_pairs={{0,16},{16,0},{1,17},{17,1},{2,18},{18,2},{3,19},{19,3},{4,20},{20... | collective-permute-start | bytes 1843208 | tf_op jit(solution)/shard_map/ppermute | solution.py:541
  461.4 13.3 %collective-permute-start.46 = (f32[128,240]{1,0:T(8,128)S(1)}, f32[128,240]{1,0:T(8,128)S(1)}, u32[]{:S(2)}, u32[]{:S(2)}) collective-permute-start(f32[128,240]{1,0:T(8,128)S(1)} %pad_maximum_fusion.4.o0), channel_id=1, source_target_pairs={{0,8},{4,12},{8,0},{12,4},{1,9},{5,13},{9,1},{13,5},{2,10},{6,14},... | collective-permute-start | bytes 368648 | tf_op jit(solution)/shard_map/ppermute | solution.py:495
  461.5 16.3 %collective-permute-start.45 = (f32[128,240]{1,0:T(8,128)S(1)}, f32[128,240]{1,0:T(8,128)S(1)}, u32[]{:S(2)}, u32[]{:S(2)}) collective-permute-start(f32[128,240]{1,0:T(8,128)S(1)} %pad_maximum_fusion.4.o0), channel_id=1, source_target_pairs={{0,4},{4,0},{8,12},{12,8},{1,5},{5,1},{9,13},{13,9},{2,6},{6,2},{1... | collective-permute-start | bytes 368648 | tf_op jit(solution)/shard_map/ppermute | solution.py:495
  (48 other events, 613.2 us)
Sparse Core Ops, SparseCore 0:
  17.4 87.4 all-gather.3
  107.0 33.1 all-gather.5
  141.8 30.4 all-gather.7
  234.9 35.7 reduce-scatter.2
  303.0 77.5 reduce-scatter.4
where the time goes:
time: 494 us; the launch traced here: 490 us
  waiting for transfers between devices  211 us (43%)
  Pallas kernels  142 us (29%)
  starting transfers between devices  79.3 us (16%)
  between operations  20.7 us (4%)
  other arithmetic  18.9 us (4%)
  local copies, waits for them, and re-layouts  18.1 us (4%)
    pallas_call x3, Pallas kernels, grouped(): pl.pallas_call(kernel, grid_spec=pltpu.PrefetchScalarGridSpec(num_scalar_...  77.4 us
    ppermute x4, waiting for transfers between devices, to_features(): back.append(lax.ppermute(pieces[k], ('gx', 'gy'), pairs))  71.4 us
    pallas_call x9, Pallas kernels, simple(): pl.pallas_call(kernel, in_specs=specs, out_specs=[pl.BlockSpec(memory_spa...  64.3 us
    ppermute x30, waiting for transfers between devices, swap(): return lax.ppermute(values, 'gx', [(i, i ^ bit) for i in range(ROWS)])  50.6 us
    ppermute x30, starting transfers between devices, swap(): return lax.ppermute(values, 'gx', [(i, i ^ bit) for i in range(ROWS)])  36.4 us
    ppermute x8, starting transfers between devices, to_tokens(): out.append(lax.ppermute(pieces[k], ('gx', 'gy'), pairs))  23.7 us
    ppermute x8, waiting for transfers between devices, to_tokens(): out.append(lax.ppermute(pieces[k], ('gx', 'gy'), pairs))  22.7 us
    ppermute x3, waiting for transfers between devices, ring(): lax.ppermute(values, 'gy', [(i, (i + 1) % ROWS) for i in range(ROWS)])  17.3 us
  transfers between devices with their start and end apart: 55, of which 25 were waited for; matrix products, arithmetic and copies ran while one was open for 5% of the time, Pallas kernels for 22%

commit v1 on v0

--- a/solution.py
+++ b/solution.py
@@ -102,9 +102,9 @@
 
 def qkv_kernel(sc, *refs):
     toks = refs[:4]
-    w_all = refs[4]
-    cos_ref, sin_ref = refs[5:7]
-    x_ref, n1_ref, r1_ref, g1_ref, g2_ref, w5_ref, qs_ref, kv_ref = refs[7:]
+    w_rows = refs[4:8]
+    cos_ref, sin_ref = refs[8:10]
+    x_ref, n1_ref, r1_ref, g1_ref, g2_ref, w5_ref, qs_ref, kv_ref = refs[10:]
     ix = sc[0]
     lane = lax.broadcasted_iota(jnp.int32, (FB, CP), 1)
     for k in range(ROWS):
@@ -119,8 +119,9 @@
     r1_ref[...] = r1
     n1_ref[...] = (x * r1 * g1_ref[...]).astype(BF)
     for k in range(ROWS):
-        w5_ref[k] = w_all[ix ^ k, :, :PACK]
-        w5_ref[GROUPS - 1, :, k * ODD : (k + 1) * ODD] = w_all[k, :, PACK:]
+        w5_ref[k] = w_rows[k][:, :PACK]
+        lanes = pl.ds(pl.multiple_of((ix ^ k) * ODD, ODD), ODD)
+        w5_ref[GROUPS - 1, :, lanes] = w_rows[k][:, PACK:]
     cos_a = cos_ref[...]
     sin_a = sin_ref[...]
     for g in range(GROUPS):
@@ -398,15 +399,18 @@
 
 def mlp_grad_kernel(*refs):
     n2s, dys, acts, gates, ups = (refs[ROWS * i : ROWS * (i + 1)] for i in range(5))
-    out = refs[-1]
+    outs = refs[-2:]
     width = acts[0].shape[0]
+    edge = outs[0].shape[1]
     step = 128
     for part, (left, right) in enumerate(((n2s, gates), (n2s, ups), (dys, acts))):
         for f in range(0, width, step):
             total = nt(left[0][...], right[0][f : f + step])
             for k in range(1, ROWS):
                 total = total + nt(left[k][...], right[k][f : f + step])
-            out[:, part * width + f : part * width + f + step] = total.astype(BF)
+            col = part * width + f
+            out = outs[col // edge]
+            out[:, col % edge : col % edge + step] = total.astype(BF)
 
 
 def grads_kernel(sc, g_ref, o0, o1, o2, o3, qkv_ref, out_ref, gains_ref, oa_s, ob_s):
@@ -601,27 +605,17 @@
     odd = jnp.concatenate([w_qkv[:, SLOT_W:], w_out[:, QW:]], axis=1)
     odd = jnp.where(ix == odd_row, odd, jnp.zeros_like(odd))
     quarter = row_scatter([lax.dynamic_slice(odd, (0, ODD * (ix ^ k)), (FB, ODD)) for k in range(ROWS)])
-    w_all = lax.all_gather(
-        jnp.concatenate([w_qkv[:, :SLOT_W], w_out[:, :QW], quarter], axis=1),
-        ("gx", "gy"), axis=0, tiled=True,
-    ).reshape(ROWS, D, PACK + ODD)
+    w_own = lax.all_gather(
+        jnp.concatenate([w_qkv[:, :SLOT_W], w_out[:, :QW], quarter], axis=1), "gy", axis=0, tiled=True
+    )
     dy_pieces = simple(
         functools.partial(split_kernel, False), "split_grad", [piece] * ROWS,
         after(cotangent, pieces[0]), scalars=at,
     )
     dy_pieces = to_tokens(dy_pieces)
-    toks[0] = after(toks[0], *dy_pieces)
-    x, n1, r1, gain_one, gain_two, w5, qs, kv = simple(
-        qkv_kernel, "qkv",
-        [
-            sds((D, CP), BF), sds((D, CP), BF), sds((1, CP), F32), sds((D, 1), F32), sds((D, 1), F32),
-            sds((GROUPS, D, PACK), BF), sds((GROUPS, QW, CP), BF), sds((GROUPS, KV, CP), BF),
-        ],
-        *toks, w_all, cos_a, sin_a,
-        scalars=at,
-    )
-
-    dy = simple(join_kernel, "join", [sds((D, CP), BF)], *dy_pieces, scalars=at)[0]
+    w_own = after(w_own, *toks)
+    w_far = after(swap(w_own, 2), *dy_pieces)
+    w_rows = [w_own, swap(w_own, 1), w_far, swap(w_far, 1)]
     w_gu = jnp.concatenate([w_gate_up[:, 0], w_gate_up[:, 1]], axis=1)
     halves = lax.axis_size("dp") == 2
     if halves:
@@ -629,6 +623,17 @@
     w_gu = [lax.all_gather(w_gu, "gy", axis=0, tiled=True)]
     if halves:
         w_gu.append(lax.ppermute(w_gu[0], "dp", [(0, 1), (1, 0)]))
+    x, n1, r1, gain_one, gain_two, w5, qs, kv = simple(
+        qkv_kernel, "qkv",
+        [
+            sds((D, CP), BF), sds((D, CP), BF), sds((1, CP), F32), sds((D, 1), F32), sds((D, 1), F32),
+            sds((GROUPS, D, PACK), BF), sds((GROUPS, QW, CP), BF), sds((GROUPS, KV, CP), BF),
+        ],
+        *toks, *w_rows, cos_a, sin_a,
+        scalars=at,
+    )
+
+    dy = simple(join_kernel, "join", [sds((D, CP), BF)], *dy_pieces, scalars=at)[0]
     w_d = lax.all_gather(w_down, "gy", axis=0, tiled=True)
 
     kvs = row_gather(kv)
@@ -643,7 +648,7 @@
         ],
         [per_group(QW, CP), per_group(8, CP), whole(D, CP), whole(D, CP), whole(1, CP)],
         [pltpu.VMEM((8, CP), F32), pltpu.VMEM((8, CP), F32), pltpu.VMEM((QW, CP), F32)],
-        sc, after(qs, w_gu[0]), *kvs, bias, w5, x, gain_two,
+        sc, qs, *kvs, bias, w5, x, gain_two,
     )
 
     n2s = row_gather(n2)
@@ -654,20 +659,18 @@
             scalars=at, scratch=[pltpu.VMEM((D, 2 * ff), BF)] if halves else [],
         )
 
-    near = feed_forward("mlp_near", n2s[:2], dys[:2])
     far = feed_forward("mlp_far", n2s[2:], dys[2:])
+    near = feed_forward("mlp_near", [after(n2s[0], far[9]), n2s[1]], dys[:2])
     blocks = [near[:5], near[5:], far[:5], far[5:]]
     dn2_terms = list(row_near([b[4] for b in blocks]))
     mlp_terms = list(row_near([b[3] for b in blocks]))
 
-    def beside_dn2(far, *operands):
-        return swap(far, 2), simple(
-            mlp_grad_kernel, "mlp_grad", [sds((D, 3 * ff), BF)],
-            *operands,
-        )[0]
-
-    dn2_terms[2], g_mlp = beside_dn2(
-        dn2_terms[2], *n2s, *dys, *[b[0] for b in blocks], *[b[1] for b in blocks], *[b[2] for b in blocks]
+    dn2_terms[2] = swap(dn2_terms[2], 2)
+    wide = (3 * ff // 2 + 127) // 128 * 128
+    g_mlp = simple(
+        mlp_grad_kernel, "mlp_grad", [sds((D, wide), BF), sds((D, 3 * ff - wide), BF)],
+        after(n2s[0], dn2_terms[2]), *n2s[1:], *dys,
+        *[b[0] for b in blocks], *[b[1] for b in blocks], *[b[2] for b in blocks],
     )
 
     pack_a = sds((ROWS, AP, FB), BF)
@@ -687,16 +690,15 @@
             *operands,
         )
 
-    g_down = lax.psum_scatter(g_mlp[:, 2 * ff :], "gy", scatter_dimension=0, tiled=True)
-    g_gate_up = lax.psum_scatter(g_mlp[:, : 2 * ff], "gy", scatter_dimension=0, tiled=True)
     mlp_terms[2] = after(mlp_terms[2], dn2_terms[2])
-    dn2_terms[1] = after(dn2_terms[1], g_mlp, mlp_terms[2])
+    dn2_terms[1] = after(dn2_terms[1], g_mlp[0], mlp_terms[2])
     mlp_terms[2], back = beside_back(
         mlp_terms[2],
         sc, qs, *kvs, bias, w5, o, lse, n1, cos_a, sin_a, *dn2_terms, h, r2, gain_two, dy,
     )
     dq, dkv, dh, gg, packs_a = back[0], list(back[1:5]), back[5], back[6], back[7:]
-    dkv[2] = after(dkv[2], mlp_terms[2], g_down)
+    g_mlp = [lax.psum_scatter(g, "gy", scatter_dimension=0, tiled=True) for g in g_mlp]
+    dkv[2] = after(dkv[2], mlp_terms[2], g_mlp[0])
     dkv_terms = list(row_terms(dkv))
     a_terms = list(row_near(packs_a))
     a_terms[2] = after(a_terms[2], dkv_terms[2])
@@ -716,8 +718,8 @@
     back = to_features(out_pieces)
     layer_out, input_grad = simple(merge_kernel, "merge", [sds((FB, L), BF)] * 2, *back, scalars=at)
 
-    grad_down = dp_sum(g_down)
-    g_mlp = dp_sum(g_gate_up)
+    g_mlp = jnp.concatenate([dp_sum(g) for g in g_mlp], axis=1)
+    grad_down = g_mlp[:, 2 * ff :]
     g_a = sum(term.astype(F32) for term in a_terms).astype(BF)
     packs_b = list(packs_b)
     packs_b[2] = after(packs_b[2], a_terms[2])

time: 494 us -> 496 us (level)
  the two profiles are of different devices: /device:TPU:11 before, /device:TPU:0 now
where the time goes in v1:
time: 496 us; the launch traced here: 487 us
  waiting for transfers between devices  161 us (32%)
  starting transfers between devices  141 us (28%)
  Pallas kernels  125 us (25%)
  other arithmetic  21.8 us (4%)
  between operations  20.8 us (4%)
  local copies, waits for them, and re-layouts  17.4 us (4%)
    ppermute x33, starting transfers between devices, swap(): return lax.ppermute(values, 'gx', [(i, i ^ bit) for i in range(ROWS)])  76.2 us
    pallas_call x9, Pallas kernels, simple(): pl.pallas_call(kernel, in_specs=specs, out_specs=[pl.BlockSpec(memory_spa...  62.7 us
    pallas_call x3, Pallas kernels, grouped(): pl.pallas_call(kernel, grid_spec=pltpu.PrefetchScalarGridSpec(num_scalar_...  62.5 us
    ppermute x8, waiting for transfers between devices, to_tokens(): out.append(lax.ppermute(pieces[k], ('gx', 'gy'), pairs))  58.2 us
    ppermute x33, waiting for transfers between devices, swap(): return lax.ppermute(values, 'gx', [(i, i ^ bit) for i in range(ROWS)])  38.9 us
    ppermute x3, starting transfers between devices, ring(): lax.ppermute(values, 'gy', [(i, (i + 1) % ROWS) for i in range(ROWS)])  27 us
    ppermute x4, waiting for transfers between devices, to_features(): back.append(lax.ppermute(pieces[k], ('gx', 'gy'), pairs))  19 us
    ppermute x8, starting transfers between devices, to_tokens(): out.append(lax.ppermute(pieces[k], ('gx', 'gy'), pairs))  16.3 us
  transfers between devices with their start and end apart: 58, of which 24 were waited for; matrix products, arithmetic and copies ran while one was open for 5% of the time, Pallas kernels for 19%

profile of v1, /device:TPU:0, one launch (start us, length us, event | category | flops | bytes accessed | tf_op | source)
XLA Modules:
  0.0 486.7 jit_solution(4437005831925745339)
XLA Ops:
  13.0 2.9 collective-permute-start.7
  16.0 2.3 collective-permute-done.7
  22.1 2.7 split_tokens.1
  26.4 3.5 collective-permute-start.2
  30.2 4.0 collective-permute-start.4
  34.3 30.1 %collective-permute-done.2.refs_1_ = bf16[240,384]{1,0:T(8,128)(2,1)S(1)} collective-permute-done((bf16[240,384]{1,0:T(8,128)(2,1)}, bf16[240,384]{1,0:T(8,128)(2,1)S(1)}, u32[]{:S(2)}, u32[]{:S(2)}) %collective-permute-start.2) | collective-permute-done | bytes 184352 | tf_op jit(solution)/shard_map/ppermute | solution.py:553
  65.1 7.0 %all-gather.4.cloned.1.call-done.refs_4_ = bf16[960,640]{1,0:T(8,128)(2,1)} async-done(((bf16[240,640]{1,0:T(8,128)(2,1)}), bf16[960,640]{1,0:T(8,128)(2,1)}) %all-gather.4.cloned.1.call-update) | async-done | bytes 1228816 | tf_op jit(solution)/shard_map/all_gather | solution.py:608
  72.1 3.2 collective-permute-start.9
  77.2 2.4 split_grad.1
  81.2 2.7 collective-permute-start.12
  83.9 2.6 collective-permute-start.13
  88.2 19.0 %collective-permute-done.11.refs_1_ = bf16[240,384]{1,0:T(8,128)(2,1)S(1)} collective-permute-done((bf16[240,384]{1,0:T(8,128)(2,1)}, bf16[240,384]{1,0:T(8,128)(2,1)S(1)}, u32[]{:S(2)}, u32[]{:S(2)}) %collective-permute-start.11) | collective-permute-done | bytes 184352 | tf_op jit(solution)/shard_map/ppermute | solution.py:553
  107.2 8.4 %collective-permute-done.12.refs_2_ = bf16[240,384]{1,0:T(8,128)(2,1)S(1)} collective-permute-done((bf16[240,384]{1,0:T(8,128)(2,1)}, bf16[240,384]{1,0:T(8,128)(2,1)S(1)}, u32[]{:S(2)}, u32[]{:S(2)}) %collective-permute-start.12) | collective-permute-done | bytes 184352 | tf_op jit(solution)/shard_map/ppermute | solution.py:553
  115.6 6.2 %collective-permute-start.14 = (bf16[960,640]{1,0:T(8,128)(2,1)S(1)}, bf16[960,640]{1,0:T(8,128)(2,1)}, u32[]{:S(2)}, u32[]{:S(2)}) collective-permute-start(bf16[960,640]{1,0:T(8,128)(2,1)S(1)} %collective-permute-done.9.refs_6_), channel_id=1, source_target_pairs={{0,4},{4,0},{8,12},{12,8},{1,5},{5,1},{9,13},{13,9},{2,6},{6,2},{1... | collective-permute-start | bytes 3686408 | tf_op jit(solution)/shard_map/ppermute | solution.py:499
  123.5 2.6 select_add_fusion
  127.0 6.9 %qkv.1 = (bf16[960,384]{1,0:T(8,128)(2,1)}, bf16[960,384]{1,0:T(8,128)(2,1)}, f32[1,384]{1,0:T(1,128)}, f32[960,1]{1,0:T(8,128)}, f32[960,1]{1,0:T(8,128)}, /*in...) custom-call(s32[4]{0:T(128)} %pad_add_fusion.sc, ...), custom_call_target="tpu_custom_call" | custom-call | flops 700000000 | bytes 2100000 | tf_op jit(solution)/shard_map/qkv/pallas_call | solution.py:469
  134.0 7.2 %collective-permute-start.16 = (bf16[5,128,384]{2,1,0:T(8,128)(2,1)}, bf16[5,128,384]{2,1,0:T(8,128)(2,1)S(1)}, u32[]{:S(2)}, u32[]{:S(2)}) collective-permute-start(bf16[5,128,384]{2,1,0:T(8,128)(2,1)} %get-tuple-element.101.kv0), channel_id=1, source_target_pairs={{0,8},{4,12},{8,0},{12,4},{1,9},{5,13},{9,1},{13,5},{2,10},{6,14},... | collective-permute-start | bytes 1474568 | tf_op jit(solution)/shard_map/ppermute | solution.py:499
  147.6 5.6 %collective-permute-done.16.kv2 = bf16[5,128,384]{2,1,0:T(8,128)(2,1)S(1)} collective-permute-done((bf16[5,128,384]{2,1,0:T(8,128)(2,1)}, bf16[5,128,384]{2,1,0:T(8,128)(2,1)S(1)}, u32[]{:S(2)}, u32[]{:S(2)}) %collective-permute-start.16) | collective-permute-done | bytes 491552 | tf_op jit(solution)/shard_map/ppermute | solution.py:499
  160.7 15.2 %attend.1 = (bf16[5,192,384]{2,1,0:T(8,128)(2,1)}, f32[5,8,384]{2,1,0:T(8,128)}, f32[960,384]{1,0:T(8,128)}, bf16[960,384]{1,0:T(8,128)(2,1)}, f32[1,384]{1,0:T(1,128)}) custom-call(s32[8]{0:T(128)} %concatenate.22.sc, bf16[5,192,384]{2,1,0:T(8,128)(2,1)} %get-tuple-element.100.qs_ref, bf16[5,128,384]{2,1,0:T(8,128)(2,1)} %get-tuple-element.101.kv0, ...), custom_call_target="tpu_custom_call" | custom-call | flops 1800000000 | bytes 5400000 | tf_op jit(solution)/shard_map/attend/pallas_call | solution.py:482
  175.9 13.6 %collective-permute-start.19 = (bf16[960,384]{1,0:T(8,128)(2,1)}, bf16[960,384]{1,0:T(8,128)(2,1)}, u32[]{:S(2)}, u32[]{:S(2)}) collective-permute-start(bf16[960,384]{1,0:T(8,128)(2,1)} %get-tuple-element.115.refs_3_.refs_0_), channel_id=1, source_target_pairs={{0,8},{4,12},{8,0},{12,4},{1,9},{5,13},{9,1},{13,5},{2,10},{6,14},... | collective-permute-start | bytes 2211848 | tf_op jit(solution)/shard_map/ppermute | solution.py:499
  189.7 11.9 %collective-permute-done.19.refs_3_.refs_2_ = bf16[960,384]{1,0:T(8,128)(2,1)} collective-permute-done((bf16[960,384]{1,0:T(8,128)(2,1)}, bf16[960,384]{1,0:T(8,128)(2,1)}, u32[]{:S(2)}, u32[]{:S(2)}) %collective-permute-start.19) | collective-permute-done | bytes 737312 | tf_op jit(solution)/shard_map/ppermute | solution.py:499
  201.6 12.3 %collective-permute-done.18.refs_1_ = bf16[512,1280]{1,0:T(8,128)(2,1)S(1)} collective-permute-done((bf16[512,1280]{1,0:T(8,128)(2,1)}, bf16[512,1280]{1,0:T(8,128)(2,1)S(1)}, u32[]{:S(2)}, u32[]{:S(2)}) %collective-permute-start.18) | collective-permute-done | bytes 1310752 | tf_op jit(solution)/shard_map/ppermute | solution.py:625
  215.0 12.7 %mlp_far.1 = (bf16[640,384]{1,0:T(8,128)(2,1)}, bf16[640,384]{1,0:T(8,128)(2,1)}, bf16[640,384]{1,0:T(8,128)(2,1)}, bf16[960,384]{1,0:T(8,128)(2,1)}, bf16[960,3...) custom-call(s32[4]{0:T(128)} %pad_add_fusion.sc, ...), custom_call_target="tpu_custom_call" | custom-call | flops 1300000000 | bytes 3900000 | tf_op jit(solution)/shard_map/mlp_far/pallas_call | solution.py:469
  235.1 12.9 %mlp_near.1 = (bf16[640,384]{1,0:T(8,128)(2,1)}, bf16[640,384]{1,0:T(8,128)(2,1)}, bf16[640,384]{1,0:T(8,128)(2,1)}, bf16[960,384]{1,0:T(8,128)(2,1)}, bf16[960,...) custom-call(s32[4]{0:T(128)} %pad_add_fusion.sc, ...), custom_call_target="tpu_custom_call" | custom-call | flops 1300000000 | bytes 3900000 | tf_op jit(solution)/shard_map/mlp_near/pallas_call | solution.py:469
  247.9 2.3 collective-permute-done.27.dn_c
  250.2 17.7 %mlp_grad.1 = (bf16[960,1024]{1,0:T(8,128)(2,1)}, bf16[960,896]{1,0:T(8,128)(2,1)}) custom-call(bf16[960,384]{1,0:T(8,128)(2,1)} %get-tuple-element.115.refs_3_.refs_0_, bf16[960,384]{1,0:T(8,128)(2,1)} %copy-done.6, bf16[960,384]{1,0:T(8,128)(2,1)} %collective-permute-done.19.refs_3_.refs_2_, bf16[960,384]{1,0:T(8,128)(2,1)} %collective-permute-done.20.refs_4_.refs_3_, ...), custom_call_target="tpu_custom_call" | custom-call | flops 1800000000 | bytes 5400000 | tf_op jit(solution)/shard_map/mlp_grad/pallas_call | solution.py:469
  274.1 28.2 %attend_back.1 = (bf16[5,192,384]{2,1,0:T(8,128)(2,1)}, f32[5,128,384]{2,1,0:T(8,128)}, bf16[5,128,384]{2,1,0:T(8,128)(2,1)}, bf16[5,128,384]{2,1,0:T(8,128)(2,1...) custom-call(s32[8]{0:T(128)} %concatenate.22.sc, ...), custom_call_target="tpu_custom_call" | custom-call | flops 3000000000 | bytes 9000000 | tf_op jit(solution)/shard_map/attend_back/pallas_call | solution.py:482
  302.2 7.6 %collective-permute-start.31 = (bf16[5,128,384]{2,1,0:T(8,128)(2,1)}, bf16[5,128,384]{2,1,0:T(8,128)(2,1)S(1)}, u32[]{:S(2)}, u32[]{:S(2)}) collective-permute-start(bf16[5,128,384]{2,1,0:T(8,128)(2,1)} %get-tuple-element.141), channel_id=1, source_target_pairs={{0,4},{4,0},{8,12},{12,8},{1,5},{5,1},{9,13},{13,9},{2,6},{6,2},{1... | collective-permute-start | bytes 1474568 | tf_op jit(solution)/shard_map/ppermute | solution.py:499
  309.9 5.4 %reduce-scatter.3.cloned.1.call-done = bf16[240,1024]{1,0:T(8,128)(2,1)} async-done(((bf16[960,1024]{1,0:T(8,128)(2,1)}), bf16[240,1024]{1,0:T(8,128)(2,1)}) %reduce-scatter.3.cloned.1.call-update) | async-done | bytes 491536 | tf_op jit(solution)/shard_map/reduce_scatter | solution.py:700
  316.7 5.0 %collective-permute-start.32 = (bf16[5,128,384]{2,1,0:T(8,128)(2,1)S(1)}, bf16[5,128,384]{2,1,0:T(8,128)(2,1)S(1)}, u32[]{:S(2)}, u32[]{:S(2)}) collective-permute-start(bf16[5,128,384]{2,1,0:T(8,128)(2,1)S(1)} %add_convert_fusion.4), channel_id=1, source_target_pairs={{0,8},{4,12},{8,0},{12,4},{1,9},{5,13},{9,1},{13,5},{2,10},{6,14},... | collective-permute-start | bytes 1474568 | tf_op jit(solution)/shard_map/ppermute | solution.py:499
  322.6 10.7 %collective-permute-done.32.d2 = bf16[5,128,384]{2,1,0:T(8,128)(2,1)S(1)} collective-permute-done((bf16[5,128,384]{2,1,0:T(8,128)(2,1)S(1)}, bf16[5,128,384]{2,1,0:T(8,128)(2,1)S(1)}, u32[]{:S(2)}, u32[]{:S(2)}) %collective-permute-start.32) | collective-permute-done | bytes 491552 | tf_op jit(solution)/shard_map/ppermute | solution.py:499
  335.8 19.1 %final.1 = (bf16[4,176,240]{2,1,0:T(8,128)(2,1)}, bf16[4,176,240]{2,1,0:T(8,128)(2,1)}, bf16[4,176,240]{2,1,0:T(8,128)(2,1)}, bf16[4,176,240]{2,1,0:T(8,128)(2,1...) custom-call(s32[8]{0:T(128)} %concatenate.22.sc, ...), custom_call_target="tpu_custom_call" | custom-call | flops 1900000000 | bytes 5700000 | tf_op jit(solution)/shard_map/final/pallas_call | solution.py:482
  361.4 10.1 %collective-permute-start.36 = (bf16[480,384]{1,0:T(8,128)(2,1)}, bf16[480,384]{1,0:T(8,128)(2,1)}, u32[]{:S(2)}, u32[]{:S(2)}) collective-permute-start(bf16[480,384]{1,0:T(8,128)(2,1)} %get-tuple-element.152), channel_id=1, source_target_pairs={{0,1},{1,9},{2,5},{3,13},{4,0},{5,8},{6,4},{7,12},{8,3},{9,11},{10... | collective-permute-start | bytes 1105928 | tf_op jit(solution)/shard_map/ppermute | solution.py:561
  373.9 6.1 %collective-permute-done.36.refs_1_ = bf16[480,384]{1,0:T(8,128)(2,1)} collective-permute-done((bf16[480,384]{1,0:T(8,128)(2,1)}, bf16[480,384]{1,0:T(8,128)(2,1)}, u32[]{:S(2)}, u32[]{:S(2)}) %collective-permute-start.36) | collective-permute-done | bytes 368672 | tf_op jit(solution)/shard_map/ppermute | solution.py:561
  380.1 12.8 %collective-permute-start.44 = (bf16[656,240]{1,0:T(8,128)(2,1)S(1)}, bf16[656,240]{1,0:T(8,128)(2,1)S(1)}, u32[]{:S(2)}, u32[]{:S(2)}) collective-permute-start(bf16[656,240]{1,0:T(8,128)(2,1)S(1)} %dynamic-slice_bitcast_fusion), channel_id=1, source_target_pairs={{0,1},{1,2},{2,3},{3,0},{4,5},{5,6},{6,7},{7,4},{8,9},{9,10},{10,1... | collective-permute-start | bytes 944648 | tf_op jit(solution)/shard_map/ppermute | solution.py:530
  392.9 4.7 collective-permute-done.44
  397.7 11.8 %collective-permute-start.45 = (bf16[656,240]{1,0:T(8,128)(2,1)S(1)}, bf16[656,240]{1,0:T(8,128)(2,1)S(1)}, u32[]{:S(2)}, u32[]{:S(2)}) collective-permute-start(bf16[656,240]{1,0:T(8,128)(2,1)S(1)} %fusion.2), channel_id=1, source_target_pairs={{0,1},{1,2},{2,3},{3,0},{4,5},{5,6},{6,7},{7,4},{8,9},{9,10},{10,1... | collective-permute-start | bytes 944648 | tf_op jit(solution)/shard_map/ppermute | solution.py:530
  409.4 7.9 %collective-permute-done.45 = bf16[656,240]{1,0:T(8,128)(2,1)S(1)} collective-permute-done((bf16[656,240]{1,0:T(8,128)(2,1)S(1)}, bf16[656,240]{1,0:T(8,128)(2,1)S(1)}, u32[]{:S(2)}, u32[]{:S(2)}) %collective-permute-start.45) | collective-permute-done | bytes 314912 | tf_op jit(solution)/shard_map/ppermute | solution.py:530
  418.2 2.5 collective-permute-start.46
  424.5 2.3 collective-permute-start.38
  426.9 3.5 collective-permute-done.46
  431.5 5.7 %collective-permute-done.37.refs_2_ = bf16[480,384]{1,0:T(8,128)(2,1)S(1)} collective-permute-done((bf16[480,384]{1,0:T(8,128)(2,1)}, bf16[480,384]{1,0:T(8,128)(2,1)S(1)}, u32[]{:S(2)}, u32[]{:S(2)}) %collective-permute-start.37) | collective-permute-done | bytes 368672 | tf_op jit(solution)/shard_map/ppermute | solution.py:561
  437.1 7.2 %collective-permute-done.38.refs_3_ = bf16[480,384]{1,0:T(8,128)(2,1)} collective-permute-done((bf16[480,384]{1,0:T(8,128)(2,1)}, bf16[480,384]{1,0:T(8,128)(2,1)}, u32[]{:S(2)}, u32[]{:S(2)}) %collective-permute-start.38) | collective-permute-done | bytes 368672 | tf_op jit(solution)/shard_map/ppermute | solution.py:561
  447.5 3.9 collective-permute-done.47
  453.4 14.0 %collective-permute-start.48 = (f32[128,240]{1,0:T(8,128)S(1)}, f32[128,240]{1,0:T(8,128)S(1)}, u32[]{:S(2)}, u32[]{:S(2)}) collective-permute-start(f32[128,240]{1,0:T(8,128)S(1)} %pad_maximum_fusion.5.o0), channel_id=1, source_target_pairs={{0,4},{4,0},{8,12},{12,8},{1,5},{5,1},{9,13},{13,9},{2,6},{6,2},{1... | collective-permute-start | bytes 368648 | tf_op jit(solution)/shard_map/ppermute | solution.py:499
  467.4 2.8 collective-permute-start.50
  472.0 2.7 merge.1
  475.9 2.5 grads.1
  (219 shorter events, 71.3 us)
Async XLA Ops:
  7.2 64.9 %all-gather.4.cloned.1.call-start = ((), (), s32[]{:S(2)}) async-start(), calls=%async_computation.2 | async-start | bytes 1536000 | tf_op jit(solution)/shard_map/all_gather | solution.py:608
  19.2 170.4 %all-gather.6.cloned.1.call-start = ((), (), s32[]{:S(2)}) async-start(), calls=%async_computation.3 | async-start | bytes 1638400 | tf_op jit(solution)/shard_map/all_gather | solution.py:623
  24.8 9.4 %collective-permute-start.1 = (bf16[240,384]{1,0:T(8,128)(2,1)}, bf16[240,384]{1,0:T(8,128)(2,1)S(1)}, u32[]{:S(2)}, u32[]{:S(2)}) collective-permute-start(bf16[240,384]{1,0:T(8,128)(2,1)} %get-tuple-element.89), channel_id=1, source_target_pairs={{0,0},{1,4},{2,8},{3,12},{4,2},{5,6},{6,10},{7,14},{8,1},{9,5},{10... | collective-permute-start | bytes 552968 | tf_op jit(solution)/shard_map/ppermute | solution.py:553
  26.4 37.9 %collective-permute-start.2 = (bf16[240,384]{1,0:T(8,128)(2,1)}, bf16[240,384]{1,0:T(8,128)(2,1)S(1)}, u32[]{:S(2)}, u32[]{:S(2)}) collective-permute-start(bf16[240,384]{1,0:T(8,128)(2,1)} %get-tuple-element.90), channel_id=1, source_target_pairs={{0,4},{1,0},{2,12},{3,8},{4,6},{5,2},{6,14},{7,10},{8,5},{9,1},{10... | collective-permute-start | bytes 552968 | tf_op jit(solution)/shard_map/ppermute | solution.py:553
  29.8 35.2 %collective-permute-start.3 = (bf16[240,384]{1,0:T(8,128)(2,1)}, bf16[240,384]{1,0:T(8,128)(2,1)S(1)}, u32[]{:S(2)}, u32[]{:S(2)}) collective-permute-start(bf16[240,384]{1,0:T(8,128)(2,1)} %get-tuple-element.91), channel_id=1, source_target_pairs={{0,8},{1,12},{2,0},{3,4},{4,10},{5,14},{6,2},{7,6},{8,9},{9,13},{1... | collective-permute-start | bytes 552968 | tf_op jit(solution)/shard_map/ppermute | solution.py:553
  30.2 34.8 %collective-permute-start.4 = (bf16[240,384]{1,0:T(8,128)(2,1)}, bf16[240,384]{1,0:T(8,128)(2,1)S(1)}, u32[]{:S(2)}, u32[]{:S(2)}) collective-permute-start(bf16[240,384]{1,0:T(8,128)(2,1)} %get-tuple-element.92), channel_id=1, source_target_pairs={{0,12},{1,8},{2,4},{3,0},{4,14},{5,10},{6,6},{7,2},{8,13},{9,9},{1... | collective-permute-start | bytes 552968 | tf_op jit(solution)/shard_map/ppermute | solution.py:553
  72.1 43.5 %collective-permute-start.9 = (bf16[960,640]{1,0:T(8,128)(2,1)}, bf16[960,640]{1,0:T(8,128)(2,1)S(1)}, u32[]{:S(2)}, u32[]{:S(2)}) collective-permute-start(bf16[960,640]{1,0:T(8,128)(2,1)} %all-gather.4.cloned.1.call-done.refs_4_), channel_id=1, source_target_pairs={{0,8},{4,12},{8,0},{12,4},{1,9},{5,13},{9,1},{13,5},{2,10},{6,14},... | collective-permute-start | bytes 3686408 | tf_op jit(solution)/shard_map/ppermute | solution.py:499
  77.1 124.5 %all-gather.8.cloned.1.call-start = ((), (), s32[]{:S(2)}) async-start(), calls=%async_computation.4 | async-start | bytes 1536000 | tf_op jit(solution)/shard_map/all_gather | solution.py:637
  79.6 6.9 %collective-permute-start.10 = (bf16[240,384]{1,0:T(8,128)(2,1)}, bf16[240,384]{1,0:T(8,128)(2,1)S(1)}, u32[]{:S(2)}, u32[]{:S(2)}) collective-permute-start(bf16[240,384]{1,0:T(8,128)(2,1)} %get-tuple-element.95), channel_id=1, source_target_pairs={{0,0},{1,4},{2,8},{3,12},{4,2},{5,6},{6,10},{7,14},{8,1},{9,5},{10... | collective-permute-start | bytes 552968 | tf_op jit(solution)/shard_map/ppermute | solution.py:553
  81.2 26.0 %collective-permute-start.11 = (bf16[240,384]{1,0:T(8,128)(2,1)}, bf16[240,384]{1,0:T(8,128)(2,1)S(1)}, u32[]{:S(2)}, u32[]{:S(2)}) collective-permute-start(bf16[240,384]{1,0:T(8,128)(2,1)} %get-tuple-element.96), channel_id=1, source_target_pairs={{0,4},{1,0},{2,12},{3,8},{4,6},{5,2},{6,14},{7,10},{8,5},{9,1},{10... | collective-permute-start | bytes 552968 | tf_op jit(solution)/shard_map/ppermute | solution.py:553
  81.2 34.4 %collective-permute-start.12 = (bf16[240,384]{1,0:T(8,128)(2,1)}, bf16[240,384]{1,0:T(8,128)(2,1)S(1)}, u32[]{:S(2)}, u32[]{:S(2)}) collective-permute-start(bf16[240,384]{1,0:T(8,128)(2,1)} %get-tuple-element.97), channel_id=1, source_target_pairs={{0,8},{1,12},{2,0},{3,4},{4,10},{5,14},{6,2},{7,6},{8,9},{9,13},{1... | collective-permute-start | bytes 552968 | tf_op jit(solution)/shard_map/ppermute | solution.py:553
  83.9 31.7 %collective-permute-start.13 = (bf16[240,384]{1,0:T(8,128)(2,1)}, bf16[240,384]{1,0:T(8,128)(2,1)S(1)}, u32[]{:S(2)}, u32[]{:S(2)}) collective-permute-start(bf16[240,384]{1,0:T(8,128)(2,1)} %get-tuple-element.98), channel_id=1, source_target_pairs={{0,12},{1,8},{2,4},{3,0},{4,14},{5,10},{6,6},{7,2},{8,13},{9,9},{1... | collective-permute-start | bytes 552968 | tf_op jit(solution)/shard_map/ppermute | solution.py:553
  86.6 40.5 %collective-permute-start.8 = (bf16[960,640]{1,0:T(8,128)(2,1)S(1)}, bf16[960,640]{1,0:T(8,128)(2,1)}, u32[]{:S(2)}, u32[]{:S(2)}) collective-permute-start(bf16[960,640]{1,0:T(8,128)(2,1)S(1)} %copy-done.9), channel_id=1, source_target_pairs={{0,4},{4,0},{8,12},{12,8},{1,5},{5,1},{9,13},{13,9},{2,6},{6,2},{1... | collective-permute-start | bytes 3686408 | tf_op jit(solution)/shard_map/ppermute | solution.py:499
  115.6 11.4 %collective-permute-start.14 = (bf16[960,640]{1,0:T(8,128)(2,1)S(1)}, bf16[960,640]{1,0:T(8,128)(2,1)}, u32[]{:S(2)}, u32[]{:S(2)}) collective-permute-start(bf16[960,640]{1,0:T(8,128)(2,1)S(1)} %collective-permute-done.9.refs_6_), channel_id=1, source_target_pairs={{0,4},{4,0},{8,12},{12,8},{1,5},{5,1},{9,13},{13,9},{2,6},{6,2},{1... | collective-permute-start | bytes 3686408 | tf_op jit(solution)/shard_map/ppermute | solution.py:499
  134.0 19.3 %collective-permute-start.16 = (bf16[5,128,384]{2,1,0:T(8,128)(2,1)}, bf16[5,128,384]{2,1,0:T(8,128)(2,1)S(1)}, u32[]{:S(2)}, u32[]{:S(2)}) collective-permute-start(bf16[5,128,384]{2,1,0:T(8,128)(2,1)} %get-tuple-element.101.kv0), channel_id=1, source_target_pairs={{0,8},{4,12},{8,0},{12,4},{1,9},{5,13},{9,1},{13,5},{2,10},{6,14},... | collective-permute-start | bytes 1474568 | tf_op jit(solution)/shard_map/ppermute | solution.py:499
  141.2 174.2 %reduce-scatter.3.cloned.1.call-start = ((), (), s32[]{:S(2)}) async-start(), calls=%async_computation.5 | async-start | bytes 2457600 | tf_op jit(solution)/shard_map/reduce_scatter | solution.py:700
  147.4 13.3 %collective-permute-start.15 = (bf16[5,128,384]{2,1,0:T(8,128)(2,1)}, bf16[5,128,384]{2,1,0:T(8,128)(2,1)}, u32[]{:S(2)}, u32[]{:S(2)}) collective-permute-start(bf16[5,128,384]{2,1,0:T(8,128)(2,1)} %get-tuple-element.101.kv0), channel_id=1, source_target_pairs={{0,4},{4,0},{8,12},{12,8},{1,5},{5,1},{9,13},{13,9},{2,6},{6,2},{1... | collective-permute-start | bytes 1474568 | tf_op jit(solution)/shard_map/ppermute | solution.py:499
  153.2 7.4 %collective-permute-start.17 = (bf16[5,128,384]{2,1,0:T(8,128)(2,1)S(1)}, bf16[5,128,384]{2,1,0:T(8,128)(2,1)}, u32[]{:S(2)}, u32[]{:S(2)}) collective-permute-start(bf16[5,128,384]{2,1,0:T(8,128)(2,1)S(1)} %collective-permute-done.16.kv2), channel_id=1, source_target_pairs={{0,4},{4,0},{8,12},{12,8},{1,5},{5,1},{9,13},{13,9},{2,6},{6,2},{1... | collective-permute-start | bytes 1474568 | tf_op jit(solution)/shard_map/ppermute | solution.py:499
  158.9 30.6 %collective-permute-start.21 = (bf16[960,384]{1,0:T(8,128)(2,1)}, bf16[960,384]{1,0:T(8,128)(2,1)S(1)}, u32[]{:S(2)}, u32[]{:S(2)}) collective-permute-start(bf16[960,384]{1,0:T(8,128)(2,1)} %join.1.refs_5_.refs_4_.dy_ref), channel_id=1, source_target_pairs={{0,8},{4,12},{8,0},{12,4},{1,9},{5,13},{9,1},{13,5},{2,10},{6,14},... | collective-permute-start | bytes 2211848 | tf_op jit(solution)/shard_map/ppermute | solution.py:499
  175.9 25.7 %collective-permute-start.19 = (bf16[960,384]{1,0:T(8,128)(2,1)}, bf16[960,384]{1,0:T(8,128)(2,1)}, u32[]{:S(2)}, u32[]{:S(2)}) collective-permute-start(bf16[960,384]{1,0:T(8,128)(2,1)} %get-tuple-element.115.refs_3_.refs_0_), channel_id=1, source_target_pairs={{0,8},{4,12},{8,0},{12,4},{1,9},{5,13},{9,1},{13,5},{2,10},{6,14},... | collective-permute-start | bytes 2211848 | tf_op jit(solution)/shard_map/ppermute | solution.py:499
  189.6 24.3 %collective-permute-start.18 = (bf16[512,1280]{1,0:T(8,128)(2,1)}, bf16[512,1280]{1,0:T(8,128)(2,1)S(1)}, u32[]{:S(2)}, u32[]{:S(2)}) collective-permute-start(bf16[512,1280]{1,0:T(8,128)(2,1)} %all-gather.6.cloned.1.call-done.refs_0_), channel_id=1, source_target_pairs={{0,16},{16,0},{1,17},{17,1},{2,18},{18,2},{3,19},{19,3},{4,20},{20... | collective-permute-start | bytes 3932168 | tf_op jit(solution)/shard_map/ppermute | solution.py:625
  189.6 24.3 %collective-permute-start.22 = (bf16[960,384]{1,0:T(8,128)(2,1)S(1)}, bf16[960,384]{1,0:T(8,128)(2,1)}, u32[]{:S(2)}, u32[]{:S(2)}) collective-permute-start(bf16[960,384]{1,0:T(8,128)(2,1)S(1)} %collective-permute-done.21.refs_5_.refs_6_), channel_id=1, source_target_pairs={{0,4},{4,0},{8,12},{12,8},{1,5},{5,1},{9,13},{13,9},{2,6},{6,2},{1... | collective-permute-start | bytes 2211848 | tf_op jit(solution)/shard_map/ppermute | solution.py:499
  201.6 12.3 %collective-permute-start.20 = (bf16[960,384]{1,0:T(8,128)(2,1)}, bf16[960,384]{1,0:T(8,128)(2,1)}, u32[]{:S(2)}, u32[]{:S(2)}) collective-permute-start(bf16[960,384]{1,0:T(8,128)(2,1)} %collective-permute-done.19.refs_3_.refs_2_), channel_id=1, source_target_pairs={{0,4},{4,0},{8,12},{12,8},{1,5},{5,1},{9,13},{13,9},{2,6},{6,2},{1... | collective-permute-start | bytes 2211848 | tf_op jit(solution)/shard_map/ppermute | solution.py:499
  231.6 18.6 %collective-permute-start.27 = (bf16[960,384]{1,0:T(8,128)(2,1)S(1)}, bf16[960,384]{1,0:T(8,128)(2,1)S(1)}, u32[]{:S(2)}, u32[]{:S(2)}) collective-permute-start(bf16[960,384]{1,0:T(8,128)(2,1)S(1)} %add_convert_fusion.3), channel_id=1, source_target_pairs={{0,8},{4,12},{8,0},{12,4},{1,9},{5,13},{9,1},{13,5},{2,10},{6,14},... | collective-permute-start | bytes 2211848 | tf_op jit(solution)/shard_map/ppermute | solution.py:499
  268.0 152.6 %reduce-scatter.5.cloned.1.call-start = ((), (), s32[]{:S(2)}) async-start(), calls=%async_computation.6 | async-start | bytes 2150400 | tf_op jit(solution)/shard_map/reduce_scatter | solution.py:700
  271.5 38.5 %collective-permute-start.30 = (bf16[960,384]{1,0:T(8,128)(2,1)S(1)}, bf16[960,384]{1,0:T(8,128)(2,1)}, u32[]{:S(2)}, u32[]{:S(2)}) collective-permute-start(bf16[960,384]{1,0:T(8,128)(2,1)S(1)} %add_convert_fusion.2), channel_id=1, source_target_pairs={{0,8},{4,12},{8,0},{12,4},{1,9},{5,13},{9,1},{13,5},{2,10},{6,14},... | collective-permute-start | bytes 2211848 | tf_op jit(solution)/shard_map/ppermute | solution.py:499
  302.2 13.2 %collective-permute-start.31 = (bf16[5,128,384]{2,1,0:T(8,128)(2,1)}, bf16[5,128,384]{2,1,0:T(8,128)(2,1)S(1)}, u32[]{:S(2)}, u32[]{:S(2)}) collective-permute-start(bf16[5,128,384]{2,1,0:T(8,128)(2,1)} %get-tuple-element.141), channel_id=1, source_target_pairs={{0,4},{4,0},{8,12},{12,8},{1,5},{5,1},{9,13},{13,9},{2,6},{6,2},{1... | collective-permute-start | bytes 1474568 | tf_op jit(solution)/shard_map/ppermute | solution.py:499
  309.9 12.5 %collective-permute-start.29 = (bf16[4,480,240]{2,1,0:T(8,128)(2,1)}, bf16[4,480,240]{2,1,0:T(8,128)(2,1)S(1)}, u32[]{:S(2)}, u32[]{:S(2)}) collective-permute-start(bf16[4,480,240]{2,1,0:T(8,128)(2,1)} %get-tuple-element.138), channel_id=1, source_target_pairs={{0,4},{4,0},{8,12},{12,8},{1,5},{5,1},{9,13},{13,9},{2,6},{6,2},{1... | collective-permute-start | bytes 2764808 | tf_op jit(solution)/shard_map/ppermute | solution.py:499
  316.7 16.6 %collective-permute-start.32 = (bf16[5,128,384]{2,1,0:T(8,128)(2,1)S(1)}, bf16[5,128,384]{2,1,0:T(8,128)(2,1)S(1)}, u32[]{:S(2)}, u32[]{:S(2)}) collective-permute-start(bf16[5,128,384]{2,1,0:T(8,128)(2,1)S(1)} %add_convert_fusion.4), channel_id=1, source_target_pairs={{0,8},{4,12},{8,0},{12,4},{1,9},{5,13},{9,1},{13,5},{2,10},{6,14},... | collective-permute-start | bytes 1474568 | tf_op jit(solution)/shard_map/ppermute | solution.py:499
  321.7 13.3 %collective-permute-start.34 = (bf16[960,384]{1,0:T(8,128)(2,1)}, bf16[960,384]{1,0:T(8,128)(2,1)}, u32[]{:S(2)}, u32[]{:S(2)}) collective-permute-start(bf16[960,384]{1,0:T(8,128)(2,1)} %get-tuple-element.150), channel_id=1, source_target_pairs={{0,4},{4,0},{8,12},{12,8},{1,5},{5,1},{9,13},{13,9},{2,6},{6,2},{1... | collective-permute-start | bytes 2211848 | tf_op jit(solution)/shard_map/ppermute | solution.py:499
  321.7 13.2 %collective-permute-start.33 = (bf16[5,128,384]{2,1,0:T(8,128)(2,1)S(1)}, bf16[5,128,384]{2,1,0:T(8,128)(2,1)S(1)}, u32[]{:S(2)}, u32[]{:S(2)}) collective-permute-start(bf16[5,128,384]{2,1,0:T(8,128)(2,1)S(1)} %copy-done.38), channel_id=1, source_target_pairs={{0,4},{4,0},{8,12},{12,8},{1,5},{5,1},{9,13},{13,9},{2,6},{6,2},{1... | collective-permute-start | bytes 1474568 | tf_op jit(solution)/shard_map/ppermute | solution.py:499
  333.2 23.3 %collective-permute-start.40 = (bf16[4,480,240]{2,1,0:T(8,128)(2,1)S(1)}, bf16[4,480,240]{2,1,0:T(8,128)(2,1)S(1)}, u32[]{:S(2)}, u32[]{:S(2)}) collective-permute-start(bf16[4,480,240]{2,1,0:T(8,128)(2,1)S(1)} %add_convert_fusion.1), channel_id=1, source_target_pairs={{0,8},{4,12},{8,0},{12,4},{1,9},{5,13},{9,1},{13,5},{2,10},{6,14},... | collective-permute-start | bytes 2764808 | tf_op jit(solution)/shard_map/ppermute | solution.py:499
  335.0 36.5 %collective-permute-start.39 = (bf16[4,480,240]{2,1,0:T(8,128)(2,1)}, bf16[4,480,240]{2,1,0:T(8,128)(2,1)S(1)}, u32[]{:S(2)}, u32[]{:S(2)}) collective-permute-start(bf16[4,480,240]{2,1,0:T(8,128)(2,1)} %get-tuple-element.158), channel_id=1, source_target_pairs={{0,4},{4,0},{8,12},{12,8},{1,5},{5,1},{9,13},{13,9},{2,6},{6,2},{1... | collective-permute-start | bytes 2764808 | tf_op jit(solution)/shard_map/ppermute | solution.py:499
  355.5 16.4 %collective-permute-start.41 = (bf16[4,176,240]{2,1,0:T(8,128)(2,1)}, bf16[4,176,240]{2,1,0:T(8,128)(2,1)}, u32[]{:S(2)}, u32[]{:S(2)}) collective-permute-start(bf16[4,176,240]{2,1,0:T(8,128)(2,1)} %get-tuple-element.160), channel_id=1, source_target_pairs={{0,4},{4,0},{8,12},{12,8},{1,5},{5,1},{9,13},{13,9},{2,6},{6,2},{1... | collective-permute-start | bytes 1013768 | tf_op jit(solution)/shard_map/ppermute | solution.py:499
  358.8 13.1 %collective-permute-start.43 = (bf16[4,176,240]{2,1,0:T(8,128)(2,1)}, bf16[4,176,240]{2,1,0:T(8,128)(2,1)}, u32[]{:S(2)}, u32[]{:S(2)}) collective-permute-start(bf16[4,176,240]{2,1,0:T(8,128)(2,1)} %add_convert_fusion.6), channel_id=1, source_target_pairs={{0,8},{4,12},{8,0},{12,4},{1,9},{5,13},{9,1},{13,5},{2,10},{6,14},... | collective-permute-start | bytes 1013768 | tf_op jit(solution)/shard_map/ppermute | solution.py:499
  359.8 14.2 %collective-permute-start.35 = (bf16[480,384]{1,0:T(8,128)(2,1)}, bf16[480,384]{1,0:T(8,128)(2,1)S(1)}, u32[]{:S(2)}, u32[]{:S(2)}) collective-permute-start(bf16[480,384]{1,0:T(8,128)(2,1)} %get-tuple-element.151), channel_id=1, source_target_pairs={{0,0},{1,8},{2,4},{3,12},{4,1},{5,9},{6,5},{7,13},{8,2},{9,10},{10... | collective-permute-start | bytes 1105928 | tf_op jit(solution)/shard_map/ppermute | solution.py:561
  361.4 18.7 %collective-permute-start.36 = (bf16[480,384]{1,0:T(8,128)(2,1)}, bf16[480,384]{1,0:T(8,128)(2,1)}, u32[]{:S(2)}, u32[]{:S(2)}) collective-permute-start(bf16[480,384]{1,0:T(8,128)(2,1)} %get-tuple-element.152), channel_id=1, source_target_pairs={{0,1},{1,9},{2,5},{3,13},{4,0},{5,8},{6,4},{7,12},{8,3},{9,11},{10... | collective-permute-start | bytes 1105928 | tf_op jit(solution)/shard_map/ppermute | solution.py:561
  380.1 17.5 %collective-permute-start.44 = (bf16[656,240]{1,0:T(8,128)(2,1)S(1)}, bf16[656,240]{1,0:T(8,128)(2,1)S(1)}, u32[]{:S(2)}, u32[]{:S(2)}) collective-permute-start(bf16[656,240]{1,0:T(8,128)(2,1)S(1)} %dynamic-slice_bitcast_fusion), channel_id=1, source_target_pairs={{0,1},{1,2},{2,3},{3,0},{4,5},{5,6},{6,7},{7,4},{8,9},{9,10},{10,1... | collective-permute-start | bytes 944648 | tf_op jit(solution)/shard_map/ppermute | solution.py:530
  397.7 19.6 %collective-permute-start.45 = (bf16[656,240]{1,0:T(8,128)(2,1)S(1)}, bf16[656,240]{1,0:T(8,128)(2,1)S(1)}, u32[]{:S(2)}, u32[]{:S(2)}) collective-permute-start(bf16[656,240]{1,0:T(8,128)(2,1)S(1)} %fusion.2), channel_id=1, source_target_pairs={{0,1},{1,2},{2,3},{3,0},{4,5},{5,6},{6,7},{7,4},{8,9},{9,10},{10,1... | collective-permute-start | bytes 944648 | tf_op jit(solution)/shard_map/ppermute | solution.py:530
  418.2 12.3 %collective-permute-start.46 = (bf16[656,240]{1,0:T(8,128)(2,1)}, bf16[656,240]{1,0:T(8,128)(2,1)}, u32[]{:S(2)}, u32[]{:S(2)}) collective-permute-start(bf16[656,240]{1,0:T(8,128)(2,1)} %fusion.1), channel_id=1, source_target_pairs={{0,1},{1,2},{2,3},{3,0},{4,5},{5,6},{6,7},{7,4},{8,9},{9,10},{10,1... | collective-permute-start | bytes 944648 | tf_op jit(solution)/shard_map/ppermute | solution.py:530
  420.6 25.6 %collective-permute-start.52 = (bf16[240,896]{1,0:T(8,128)(2,1)}, bf16[240,896]{1,0:T(8,128)(2,1)S(1)}, u32[]{:S(2)}, u32[]{:S(2)}) collective-permute-start(bf16[240,896]{1,0:T(8,128)(2,1)} %reduce-scatter.5.cloned.1.call-done), channel_id=1, source_target_pairs={{0,16},{16,0},{1,17},{17,1},{2,18},{18,2},{3,19},{19,3},{4,20},{20... | collective-permute-start | bytes 1290248 | tf_op jit(solution)/shard_map/ppermute | solution.py:545
  422.7 14.4 %collective-permute-start.37 = (bf16[480,384]{1,0:T(8,128)(2,1)}, bf16[480,384]{1,0:T(8,128)(2,1)S(1)}, u32[]{:S(2)}, u32[]{:S(2)}) collective-permute-start(bf16[480,384]{1,0:T(8,128)(2,1)} %get-tuple-element.153), channel_id=1, source_target_pairs={{0,2},{1,10},{2,6},{3,14},{4,3},{5,11},{6,7},{7,15},{8,0},{9,8},{1... | collective-permute-start | bytes 1105928 | tf_op jit(solution)/shard_map/ppermute | solution.py:561
  424.5 19.8 %collective-permute-start.38 = (bf16[480,384]{1,0:T(8,128)(2,1)}, bf16[480,384]{1,0:T(8,128)(2,1)}, u32[]{:S(2)}, u32[]{:S(2)}) collective-permute-start(bf16[480,384]{1,0:T(8,128)(2,1)} %get-tuple-element.154), channel_id=1, source_target_pairs={{0,3},{1,11},{2,7},{3,15},{4,2},{5,10},{6,6},{7,14},{8,1},{9,9},{1... | collective-permute-start | bytes 1105928 | tf_op jit(solution)/shard_map/ppermute | solution.py:561
  426.8 20.5 %collective-permute-start.51 = (bf16[240,1024]{1,0:T(8,128)(2,1)S(1)}, bf16[240,1024]{1,0:T(8,128)(2,1)S(1)}, u32[]{:S(2)}, u32[]{:S(2)}) collective-permute-start(bf16[240,1024]{1,0:T(8,128)(2,1)S(1)} %copy-done.19), channel_id=1, source_target_pairs={{0,16},{16,0},{1,17},{17,1},{2,18},{18,2},{3,19},{19,3},{4,20},{20... | collective-permute-start | bytes 1474568 | tf_op jit(solution)/shard_map/ppermute | solution.py:545
  444.3 7.2 %collective-permute-start.47 = (bf16[656,240]{1,0:T(8,128)(2,1)S(1)}, bf16[656,240]{1,0:T(8,128)(2,1)S(1)}, u32[]{:S(2)}, u32[]{:S(2)}) collective-permute-start(bf16[656,240]{1,0:T(8,128)(2,1)S(1)} %fusion), channel_id=1, source_target_pairs={{0,16},{16,0},{1,17},{17,1},{2,18},{18,2},{3,19},{19,3},{4,20},{20... | collective-permute-start | bytes 944648 | tf_op jit(solution)/shard_map/ppermute | solution.py:545
  451.6 15.7 %collective-permute-start.49 = (f32[128,240]{1,0:T(8,128)S(1)}, f32[128,240]{1,0:T(8,128)S(1)}, u32[]{:S(2)}, u32[]{:S(2)}) collective-permute-start(f32[128,240]{1,0:T(8,128)S(1)} %pad_maximum_fusion.5.o0), channel_id=1, source_target_pairs={{0,8},{4,12},{8,0},{12,4},{1,9},{5,13},{9,1},{13,5},{2,10},{6,14},... | collective-permute-start | bytes 368648 | tf_op jit(solution)/shard_map/ppermute | solution.py:499
  453.4 21.3 %collective-permute-start.48 = (f32[128,240]{1,0:T(8,128)S(1)}, f32[128,240]{1,0:T(8,128)S(1)}, u32[]{:S(2)}, u32[]{:S(2)}) collective-permute-start(f32[128,240]{1,0:T(8,128)S(1)} %pad_maximum_fusion.5.o0), channel_id=1, source_target_pairs={{0,4},{4,0},{8,12},{12,8},{1,5},{5,1},{9,13},{13,9},{2,6},{6,2},{1... | collective-permute-start | bytes 368648 | tf_op jit(solution)/shard_map/ppermute | solution.py:499
  467.4 7.3 %collective-permute-start.50 = (f32[128,240]{1,0:T(8,128)S(1)}, f32[128,240]{1,0:T(8,128)S(1)}, u32[]{:S(2)}, u32[]{:S(2)}) collective-permute-start(f32[128,240]{1,0:T(8,128)S(1)} %collective-permute-done.49.o2), channel_id=1, source_target_pairs={{0,4},{4,0},{8,12},{12,8},{1,5},{5,1},{9,13},{13,9},{2,6},{6,2},{1... | collective-permute-start | bytes 368648 | tf_op jit(solution)/shard_map/ppermute | solution.py:499
  (50 other events, 774.9 us)
Sparse Core Ops, SparseCore 0:
  19.3 52.7 all-gather.3
  77.2 50.3 all-gather.5
  141.3 34.0 all-gather.7
  268.1 47.2 reduce-scatter.2
  321.9 43.0 reduce-scatter.4

commit v2 on v1

--- a/solution.py
+++ b/solution.py
@@ -57,34 +57,28 @@
     return a * cos_a - b * sin_a, b * cos_a + a * sin_a
 
 
-def split_kernel(with_tail, sc, *refs):
-    t_ref = refs[0]
-    outs = refs[-ROWS:]
+def split_kernel(sc, t_ref, dy_ref, gain_one, gain_two, *outs):
     iy = sc[1]
-    if with_tail:
-        lane = lax.broadcasted_iota(jnp.int32, (FB, CP - CH), 1)
-        tail = jnp.zeros((FB, CP - CH), F32)
-        for i in range(2):
-            rest = refs[1 + i][...]
-            for part in range(3):
-                piece = rest.astype(BF).astype(F32)
-                rest = rest - piece
-                tail = jnp.where(lane == 3 * i + part, piece, tail)
-        tail = tail.astype(BF)
-    else:
-        tail = jnp.zeros((FB, CP - CH), BF)
+    lane = lax.broadcasted_iota(jnp.int32, (FB, CP - CH), 1)
+    tail = jnp.zeros((FB, CP - CH), F32)
+    for i, gain in enumerate((gain_one, gain_two)):
+        rest = gain[...]
+        for part in range(3):
+            piece = rest.astype(BF).astype(F32)
+            rest = rest - piece
+            tail = jnp.where(lane == 3 * i + part, piece, tail)
+    tail = tail.astype(BF)
+    blank = jnp.zeros((FB, CP - CH), BF)
     for q in range(ROWS):
-        block = jnp.concatenate([t_ref[:, q * CH : (q + 1) * CH], tail], axis=1)
+        cols = slice(q * CH, (q + 1) * CH)
+        block = jnp.concatenate([t_ref[:, cols], tail], axis=1)
+        below = jnp.concatenate([dy_ref[:, cols], blank], axis=1)
         for k in range(ROWS):
 
             @pl.when((iy ^ k) == q)
-            def _(k=k, block=block):
-                outs[k][...] = block
-
-
-def join_kernel(sc, *refs):
-    for k in range(ROWS):
-        refs[ROWS][rows_at(sc[0] ^ k)] = refs[k][...]
+            def _(k=k, block=block, below=below):
+                outs[k][:FB] = block
+                outs[k][FB:] = below
 
 
 def merge_kernel(sc, *refs):
@@ -104,12 +98,13 @@
     toks = refs[:4]
     w_rows = refs[4:8]
     cos_ref, sin_ref = refs[8:10]
-    x_ref, n1_ref, r1_ref, g1_ref, g2_ref, w5_ref, qs_ref, kv_ref = refs[10:]
+    x_ref, dy_ref, n1_ref, r1_ref, g1_ref, g2_ref, w5_ref, qs_ref, kv_ref = refs[10:]
     ix = sc[0]
     lane = lax.broadcasted_iota(jnp.int32, (FB, CP), 1)
     for k in range(ROWS):
         rows = rows_at(ix ^ k)
-        piece = toks[k][...].astype(F32)
+        piece = toks[k][:FB].astype(F32)
+        dy_ref[rows] = toks[k][FB:]
         x_ref[rows] = jnp.where(lane < CH, piece, 0.0).astype(BF)
         for i, out in enumerate((g1_ref, g2_ref)):
             here = (lane >= CH + 3 * i) & (lane < CH + 3 * i + 3)
@@ -119,9 +114,11 @@
     r1_ref[...] = r1
     n1_ref[...] = (x * r1 * g1_ref[...]).astype(BF)
     for k in range(ROWS):
-        w5_ref[k] = w_rows[k][:, :PACK]
         lanes = pl.ds(pl.multiple_of((ix ^ k) * ODD, ODD), ODD)
-        w5_ref[GROUPS - 1, :, lanes] = w_rows[k][:, PACK:]
+        for j in range(ROWS):
+            rows = rows_at((sc[1] + ROWS - j) % ROWS)
+            w5_ref[k, rows] = w_rows[k][j * FB : (j + 1) * FB, :PACK]
+            w5_ref[GROUPS - 1, rows, lanes] = w_rows[k][j * FB : (j + 1) * FB, PACK:]
     cos_a = cos_ref[...]
     sin_a = sin_ref[...]
     for g in range(GROUPS):
@@ -450,7 +447,7 @@
 
 
 MICROSECONDS = {
-    "split_tokens": 3, "split_grad": 3, "join": 2, "qkv": 7, "attend": 18, "mlp_near": 13, "mlp_far": 13,
+    "split": 5, "qkv": 7, "attend": 18, "mlp_near": 13, "mlp_far": 13,
     "mlp_grad": 18, "attend_back": 30, "final": 19, "merge": 2, "grads": 3,
 }
 
@@ -596,44 +593,37 @@
     at = jnp.stack([ix, iy, odd_row, idp]).astype(jnp.int32)
     sc = jnp.concatenate([at, jnp.stack(flags).astype(jnp.int32)])
 
-    piece = sds((FB, CP), BF)
     pieces = simple(
-        functools.partial(split_kernel, True), "split_tokens", [piece] * ROWS,
-        tokens, gain_attn[:, None], gain_mlp[:, None], scalars=at,
-    )
-    toks = to_tokens(pieces)
+        split_kernel, "split", [sds((2 * FB, CP), BF)] * ROWS,
+        tokens, cotangent, gain_attn[:, None], gain_mlp[:, None], scalars=at,
+    )
     odd = jnp.concatenate([w_qkv[:, SLOT_W:], w_out[:, QW:]], axis=1)
     odd = jnp.where(ix == odd_row, odd, jnp.zeros_like(odd))
     quarter = row_scatter([lax.dynamic_slice(odd, (0, ODD * (ix ^ k)), (FB, ODD)) for k in range(ROWS)])
-    w_own = lax.all_gather(
-        jnp.concatenate([w_qkv[:, :SLOT_W], w_out[:, :QW], quarter], axis=1), "gy", axis=0, tiled=True
-    )
-    dy_pieces = simple(
-        functools.partial(split_kernel, False), "split_grad", [piece] * ROWS,
-        after(cotangent, pieces[0]), scalars=at,
-    )
-    dy_pieces = to_tokens(dy_pieces)
-    w_own = after(w_own, *toks)
-    w_far = after(swap(w_own, 2), *dy_pieces)
+    w_pieces = [after(jnp.concatenate([w_qkv[:, :SLOT_W], w_out[:, :QW], quarter], axis=1), pieces[0])]
+    toks = to_tokens(pieces)
+    for _ in range(ROWS - 1):
+        w_pieces.append(ring(w_pieces[-1]))
+    w_own = jnp.concatenate(w_pieces, axis=0)
+    w_far = jnp.concatenate([swap(w, 2) for w in w_pieces], axis=0)
     w_rows = [w_own, swap(w_own, 1), w_far, swap(w_far, 1)]
     w_gu = jnp.concatenate([w_gate_up[:, 0], w_gate_up[:, 1]], axis=1)
     halves = lax.axis_size("dp") == 2
     if halves:
         w_gu = lax.dynamic_slice(w_gu, ((FB - 128) * idp, 0), (128, 2 * ff))
-    w_gu = [lax.all_gather(w_gu, "gy", axis=0, tiled=True)]
+    w_gu = [lax.all_gather(after(w_gu, *toks), "gy", axis=0, tiled=True)]
     if halves:
         w_gu.append(lax.ppermute(w_gu[0], "dp", [(0, 1), (1, 0)]))
-    x, n1, r1, gain_one, gain_two, w5, qs, kv = simple(
+    x, dy, n1, r1, gain_one, gain_two, w5, qs, kv = simple(
         qkv_kernel, "qkv",
         [
-            sds((D, CP), BF), sds((D, CP), BF), sds((1, CP), F32), sds((D, 1), F32), sds((D, 1), F32),
+            sds((D, CP), BF), sds((D, CP), BF), sds((D, CP), BF), sds((1, CP), F32), sds((D, 1), F32), sds((D, 1), F32),
             sds((GROUPS, D, PACK), BF), sds((GROUPS, QW, CP), BF), sds((GROUPS, KV, CP), BF),
         ],
         *toks, *w_rows, cos_a, sin_a,
         scalars=at,
     )
 
-    dy = simple(join_kernel, "join", [sds((D, CP), BF)], *dy_pieces, scalars=at)[0]
     w_d = lax.all_gather(w_down, "gy", axis=0, tiled=True)
 
     kvs = row_gather(kv)
@@ -648,7 +638,7 @@
         ],
         [per_group(QW, CP), per_group(8, CP), whole(D, CP), whole(D, CP), whole(1, CP)],
         [pltpu.VMEM((8, CP), F32), pltpu.VMEM((8, CP), F32), pltpu.VMEM((QW, CP), F32)],
-        sc, qs, *kvs, bias, w5, x, gain_two,
+        sc, after(qs, w_gu[0]), *kvs, bias, w5, x, gain_two,
     )
 
     n2s = row_gather(n2)
@@ -723,9 +713,10 @@
     g_a = sum(term.astype(F32) for term in a_terms).astype(BF)
     packs_b = list(packs_b)
     packs_b[2] = after(packs_b[2], a_terms[2])
-    g_all = jnp.concatenate([g_a, row_scatter(packs_b)], axis=1)
-    g_all = ring_scatter(after(g_all, *back[:2]), iy)
-    g_all = dp_sum(after(g_all, *back[2:]))
+    g_a = lax.psum_scatter(g_a.reshape(ROWS * AP, FB), "gy", scatter_dimension=0, tiled=True)
+    g_b = after(row_scatter(packs_b).reshape(ROWS * BP, FB), *back)
+    g_b = lax.psum_scatter(g_b, "gy", scatter_dimension=0, tiled=True)
+    g_all = dp_sum(jnp.concatenate([g_a, g_b], axis=0))
     odds = jnp.concatenate([g_all[AW:AP], g_all[AP + KV : AP + KV + KV // ROWS]], axis=0)
     grad_qkv, grad_out, grad_gains = simple(
         grads_kernel, "grads",

time: 496 us -> 470 us (0.948)
  starting transfers between devices: 141 us -> 111 us
  waiting for transfers between devices: 161 us -> 170 us
    reduce_scatter x0 -> x2, waiting for transfers between devices: none -> 34.7 us  [the longest x1 34.7 us: per_device(): g_b = lax.psum_scatter(g_b, 'gy', scatter_dimension=0, tiled=True)]
    ppermute x8 -> x4, waiting for transfers between devices: 58.2 us -> 34.3 us  [to_tokens(): out.append(lax.ppermute(pieces[k], ('gx', 'gy'), pairs))]
    ppermute x3, starting transfers between devices: 27 us -> 4.86 us  [ring(): lax.ppermute(values, 'gy', [(i, (i + 1) % ROWS) for i in range(ROWS)])]
    ppermute x33 -> x36, waiting for transfers between devices: 38.9 us -> 59.2 us  [swap(): return lax.ppermute(values, 'gx', [(i, i ^ bit) for i in range(ROWS)])]
    ppermute x3, waiting for transfers between devices: 16.1 us -> 5.97 us  [ring(): lax.ppermute(values, 'gy', [(i, (i + 1) % ROWS) for i in range(ROWS)])]
    ppermute x8 -> x4, starting transfers between devices: 16.3 us -> 7.83 us  [to_tokens(): out.append(lax.ppermute(pieces[k], ('gx', 'gy'), pairs))]
    ppermute x4, waiting for transfers between devices: 19 us -> 10.9 us  [to_features(): back.append(lax.ppermute(pieces[k], ('gx', 'gy'), pairs))]
    all_gather x2 -> x1, waiting for transfers between devices: 7.05 us -> 0.01 us  [per_device(): w_gu = [lax.all_gather(after(w_gu, *toks), 'gy', axis=0, tiled=True)]]
  transfers between devices with their start and end apart: 58 -> 58, of which waited for: 24 -> 20; matrix products, arithmetic and copies ran while one was open for 5% -> 6% of each run, Pallas kernels for 19% -> 19%
where the time goes in v2:
time: 470 us; the launch traced here: 465 us
  waiting for transfers between devices  170 us (36%)
  Pallas kernels  124 us (26%)
  starting transfers between devices  111 us (24%)
  local copies, waits for them, and re-layouts  21.5 us (5%)
  between operations  21.2 us (5%)
  other arithmetic  18.6 us (4%)
    ppermute x36, starting transfers between devices, swap(): return lax.ppermute(values, 'gx', [(i, i ^ bit) for i in range(ROWS)])  71 us
    pallas_call x3, Pallas kernels, grouped(): pl.pallas_call(kernel, grid_spec=pltpu.PrefetchScalarGridSpec(num_scalar_...  62.6 us
    pallas_call x7, Pallas kernels, simple(): pl.pallas_call(kernel, in_specs=specs, out_specs=[pl.BlockSpec(memory_spa...  61 us
    ppermute x36, waiting for transfers between devices, swap(): return lax.ppermute(values, 'gx', [(i, i ^ bit) for i in range(ROWS)])  59.2 us
    reduce_scatter x1, waiting for transfers between devices, per_device(): g_b = lax.psum_scatter(g_b, 'gy', scatter_dimension=0, tiled=True)  34.7 us
    ppermute x4, waiting for transfers between devices, to_tokens(): out.append(lax.ppermute(pieces[k], ('gx', 'gy'), pairs))  34.3 us
    ppermute x4, starting transfers between devices, to_features(): back.append(lax.ppermute(pieces[k], ('gx', 'gy'), pairs))  21.3 us
    unnamed x84, local copies, waits for them, and re-layouts  12.4 us
  transfers between devices with their start and end apart: 58, of which 20 were waited for; matrix products, arithmetic and copies ran while one was open for 6% of the time, Pallas kernels for 19%

profile of v2, /device:TPU:0, one launch (start us, length us, event | category | flops | bytes accessed | tf_op | source)
XLA Modules:
  0.0 465.2 jit_solution(17692942210931511568)
XLA Ops:
  13.0 2.9 collective-permute-start.7
  18.8 3.5 split.1
  22.3 2.5 collective-permute-start.3
  24.8 3.6 collective-permute-start.4
  28.5 1.6 collective-permute-start.1
  30.3 2.6 collective-permute-start.8
  33.9 34.3 %collective-permute-done.2.refs_1_ = bf16[480,384]{1,0:T(8,128)(2,1)S(1)} collective-permute-done((bf16[480,384]{1,0:T(8,128)(2,1)}, bf16[480,384]{1,0:T(8,128)(2,1)S(1)}, u32[]{:S(2)}, u32[]{:S(2)}) %collective-permute-start.2) | collective-permute-done | bytes 368672 | tf_op jit(solution)/shard_map/ppermute | solution.py:550
  69.2 15.1 %collective-permute-start.13 = (bf16[240,640]{1,0:T(8,128)(2,1)S(1)}, bf16[240,640]{1,0:T(8,128)(2,1)S(1)}, u32[]{:S(2)}, u32[]{:S(2)}) collective-permute-start(bf16[240,640]{1,0:T(8,128)(2,1)S(1)} %collective-permute-done.8), channel_id=1, source_target_pairs={{0,8},{4,12},{8,0},{12,4},{1,9},{5,13},{9,1},{13,5},{2,10},{6,14},... | collective-permute-start | bytes 921608 | tf_op jit(solution)/shard_map/ppermute | solution.py:496
  84.3 2.2 collective-permute-start.10
  87.6 2.0 collective-permute-start.14
  90.6 6.0 %collective-permute-done.10 = bf16[240,640]{1,0:T(8,128)(2,1)S(1)} collective-permute-done((bf16[240,640]{1,0:T(8,128)(2,1)}, bf16[240,640]{1,0:T(8,128)(2,1)S(1)}, u32[]{:S(2)}, u32[]{:S(2)}) %collective-permute-start.10) | collective-permute-done | bytes 307232 | tf_op jit(solution)/shard_map/ppermute | solution.py:527
  96.7 4.2 collective-permute-start.11
  100.9 4.0 collective-permute-done.15
  105.0 2.0 collective-permute-start.16
  108.6 2.6 select_add_fusion
  112.1 9.0 %qkv.1 = (bf16[960,384]{1,0:T(8,128)(2,1)}, bf16[960,384]{1,0:T(8,128)(2,1)}, bf16[960,384]{1,0:T(8,128)(2,1)}, f32[1,384]{1,0:T(1,128)}, f32[960,1]{1,0:T(8,128...) custom-call(s32[4]{0:T(128)} %pad_add_fusion.sc, ...), custom_call_target="tpu_custom_call" | custom-call | flops 700000000 | bytes 2100000 | tf_op jit(solution)/shard_map/qkv/pallas_call | solution.py:466
  128.3 6.3 %collective-permute-done.18.kv2 = bf16[5,128,384]{2,1,0:T(8,128)(2,1)} collective-permute-done((bf16[5,128,384]{2,1,0:T(8,128)(2,1)}, bf16[5,128,384]{2,1,0:T(8,128)(2,1)}, u32[]{:S(2)}, u32[]{:S(2)}) %collective-permute-start.18) | collective-permute-done | bytes 491552 | tf_op jit(solution)/shard_map/ppermute | solution.py:496
  138.9 15.3 %attend.1 = (bf16[5,192,384]{2,1,0:T(8,128)(2,1)}, f32[5,8,384]{2,1,0:T(8,128)}, f32[960,384]{1,0:T(8,128)}, bf16[960,384]{1,0:T(8,128)(2,1)}, f32[1,384]{1,0:T(1,128)}) custom-call(s32[8]{0:T(128)} %concatenate.28.sc, bf16[5,192,384]{2,1,0:T(8,128)(2,1)} %get-tuple-element.94.qs_ref, bf16[5,128,384]{2,1,0:T(8,128)(2,1)} %get-tuple-element.91.kv0, ...), custom_call_target="tpu_custom_call" | custom-call | flops 1800000000 | bytes 5400000 | tf_op jit(solution)/shard_map/attend/pallas_call | solution.py:479
  154.3 7.9 %collective-permute-start.21 = (bf16[960,384]{1,0:T(8,128)(2,1)}, bf16[960,384]{1,0:T(8,128)(2,1)}, u32[]{:S(2)}, u32[]{:S(2)}) collective-permute-start(bf16[960,384]{1,0:T(8,128)(2,1)} %get-tuple-element.108.refs_3_.refs_0_), channel_id=1, source_target_pairs={{0,8},{4,12},{8,0},{12,4},{1,9},{5,13},{9,1},{13,5},{2,10},{6,14},... | collective-permute-start | bytes 2211848 | tf_op jit(solution)/shard_map/ppermute | solution.py:496
  163.4 6.3 %collective-permute-start.24 = (bf16[960,384]{1,0:T(8,128)(2,1)}, bf16[960,384]{1,0:T(8,128)(2,1)}, u32[]{:S(2)}, u32[]{:S(2)}) collective-permute-start(bf16[960,384]{1,0:T(8,128)(2,1)} %collective-permute-done.23.refs_5_.refs_6_), channel_id=1, source_target_pairs={{0,4},{4,0},{8,12},{12,8},{1,5},{5,1},{9,13},{13,9},{2,6},{6,2},{1... | collective-permute-start | bytes 2211848 | tf_op jit(solution)/shard_map/ppermute | solution.py:496
  169.7 3.8 collective-permute-done.21.refs_3_.refs_2_
  173.5 6.3 %collective-permute-start.22 = (bf16[960,384]{1,0:T(8,128)(2,1)}, bf16[960,384]{1,0:T(8,128)(2,1)}, u32[]{:S(2)}, u32[]{:S(2)}) collective-permute-start(bf16[960,384]{1,0:T(8,128)(2,1)} %collective-permute-done.21.refs_3_.refs_2_), channel_id=1, source_target_pairs={{0,4},{4,0},{8,12},{12,8},{1,5},{5,1},{9,13},{13,9},{2,6},{6,2},{1... | collective-permute-start | bytes 2211848 | tf_op jit(solution)/shard_map/ppermute | solution.py:496
  179.8 8.3 %collective-permute-done.20.refs_1_ = bf16[512,1280]{1,0:T(8,128)(2,1)S(1)} collective-permute-done((bf16[512,1280]{1,0:T(8,128)(2,1)S(1)}, bf16[512,1280]{1,0:T(8,128)(2,1)S(1)}, u32[]{:S(2)}, u32[]{:S(2)}) %collective-permute-start.20) | collective-permute-done | bytes 1310752 | tf_op jit(solution)/shard_map/ppermute | solution.py:616
  189.2 12.7 %mlp_far.1 = (bf16[640,384]{1,0:T(8,128)(2,1)}, bf16[640,384]{1,0:T(8,128)(2,1)}, bf16[640,384]{1,0:T(8,128)(2,1)}, bf16[960,384]{1,0:T(8,128)(2,1)}, bf16[960,3...) custom-call(s32[4]{0:T(128)} %pad_add_fusion.sc, ...), custom_call_target="tpu_custom_call" | custom-call | flops 1300000000 | bytes 3900000 | tf_op jit(solution)/shard_map/mlp_far/pallas_call | solution.py:466
  201.9 5.5 %collective-permute-start.28 = (bf16[960,384]{1,0:T(8,128)(2,1)}, bf16[960,384]{1,0:T(8,128)(2,1)S(1)}, u32[]{:S(2)}, u32[]{:S(2)}) collective-permute-start(bf16[960,384]{1,0:T(8,128)(2,1)} %get-tuple-element.103), channel_id=1, source_target_pairs={{0,4},{4,0},{8,12},{12,8},{1,5},{5,1},{9,13},{13,9},{2,6},{6,2},{1... | collective-permute-start | bytes 2211848 | tf_op jit(solution)/shard_map/ppermute | solution.py:496
  207.9 1.8 collective-permute-done.28
  213.0 12.9 %mlp_near.1 = (bf16[640,384]{1,0:T(8,128)(2,1)}, bf16[640,384]{1,0:T(8,128)(2,1)}, bf16[640,384]{1,0:T(8,128)(2,1)}, bf16[960,384]{1,0:T(8,128)(2,1)}, bf16[960,...) custom-call(s32[4]{0:T(128)} %pad_add_fusion.sc, ...), custom_call_target="tpu_custom_call" | custom-call | flops 1300000000 | bytes 3900000 | tf_op jit(solution)/shard_map/mlp_near/pallas_call | solution.py:466
  225.9 4.0 collective-permute-done.29.dn_c
  229.9 17.8 %mlp_grad.1 = (bf16[960,1024]{1,0:T(8,128)(2,1)}, bf16[960,896]{1,0:T(8,128)(2,1)}) custom-call(bf16[960,384]{1,0:T(8,128)(2,1)} %get-tuple-element.108.refs_3_.refs_0_, bf16[960,384]{1,0:T(8,128)(2,1)} %copy-done.6, bf16[960,384]{1,0:T(8,128)(2,1)} %collective-permute-done.21.refs_3_.refs_2_, bf16[960,384]{1,0:T(8,128)(2,1)} %collective-permute-done.22.refs_4_.refs_3_, ...), custom_call_target="tpu_custom_call" | custom-call | flops 1800000000 | bytes 5400000 | tf_op jit(solution)/shard_map/mlp_grad/pallas_call | solution.py:466
  249.3 2.7 collective-permute-done.30
  253.4 28.2 %attend_back.1 = (bf16[5,192,384]{2,1,0:T(8,128)(2,1)}, f32[5,128,384]{2,1,0:T(8,128)}, bf16[5,128,384]{2,1,0:T(8,128)(2,1)}, bf16[5,128,384]{2,1,0:T(8,128)(2,1...) custom-call(s32[8]{0:T(128)} %concatenate.28.sc, ...), custom_call_target="tpu_custom_call" | custom-call | flops 3000000000 | bytes 9000000 | tf_op jit(solution)/shard_map/attend_back/pallas_call | solution.py:479
  281.7 7.6 %collective-permute-start.33 = (bf16[5,128,384]{2,1,0:T(8,128)(2,1)}, bf16[5,128,384]{2,1,0:T(8,128)(2,1)S(1)}, u32[]{:S(2)}, u32[]{:S(2)}) collective-permute-start(bf16[5,128,384]{2,1,0:T(8,128)(2,1)} %get-tuple-element.134), channel_id=1, source_target_pairs={{0,4},{4,0},{8,12},{12,8},{1,5},{5,1},{9,13},{13,9},{2,6},{6,2},{1... | collective-permute-start | bytes 1474568 | tf_op jit(solution)/shard_map/ppermute | solution.py:496
  289.4 10.6 %reduce-scatter.5.cloned.1.call-done = bf16[240,1024]{1,0:T(8,128)(2,1)} async-done(((bf16[960,1024]{1,0:T(8,128)(2,1)}), bf16[240,1024]{1,0:T(8,128)(2,1)}) %reduce-scatter.5.cloned.1.call-update) | async-done | bytes 491536 | tf_op jit(solution)/shard_map/reduce_scatter | solution.py:690
  302.9 11.0 %collective-permute-done.34.d2 = bf16[5,128,384]{2,1,0:T(8,128)(2,1)S(1)} collective-permute-done((bf16[5,128,384]{2,1,0:T(8,128)(2,1)S(1)}, bf16[5,128,384]{2,1,0:T(8,128)(2,1)S(1)}, u32[]{:S(2)}, u32[]{:S(2)}) %collective-permute-start.34) | collective-permute-done | bytes 491552 | tf_op jit(solution)/shard_map/ppermute | solution.py:496
  316.0 20.6 %collective-permute-done.42 = bf16[4,480,240]{2,1,0:T(8,128)(2,1)S(1)} collective-permute-done((bf16[4,480,240]{2,1,0:T(8,128)(2,1)S(1)}, bf16[4,480,240]{2,1,0:T(8,128)(2,1)S(1)}, u32[]{:S(2)}, u32[]{:S(2)}) %collective-permute-start.42) | collective-permute-done | bytes 921632 | tf_op jit(solution)/shard_map/ppermute | solution.py:496
  339.0 19.1 %final.1 = (bf16[4,176,240]{2,1,0:T(8,128)(2,1)}, bf16[4,176,240]{2,1,0:T(8,128)(2,1)}, bf16[4,176,240]{2,1,0:T(8,128)(2,1)}, bf16[4,176,240]{2,1,0:T(8,128)(2,1...) custom-call(s32[8]{0:T(128)} %concatenate.28.sc, ...), custom_call_target="tpu_custom_call" | custom-call | flops 1900000000 | bytes 5700000 | tf_op jit(solution)/shard_map/final/pallas_call | solution.py:479
  362.6 1.6 collective-permute-start.37
  364.3 2.4 collective-permute-start.38
  366.7 13.3 %collective-permute-start.39 = (bf16[480,384]{1,0:T(8,128)(2,1)}, bf16[480,384]{1,0:T(8,128)(2,1)S(1)}, u32[]{:S(2)}, u32[]{:S(2)}) collective-permute-start(bf16[480,384]{1,0:T(8,128)(2,1)} %get-tuple-element.146), channel_id=1, source_target_pairs={{0,2},{1,10},{2,6},{3,14},{4,3},{5,11},{6,7},{7,15},{8,0},{9,8},{1... | collective-permute-start | bytes 1105928 | tf_op jit(solution)/shard_map/ppermute | solution.py:558
  380.0 3.9 collective-permute-start.40
  384.8 9.5 %collective-permute-done.39.refs_2_ = bf16[480,384]{1,0:T(8,128)(2,1)S(1)} collective-permute-done((bf16[480,384]{1,0:T(8,128)(2,1)}, bf16[480,384]{1,0:T(8,128)(2,1)S(1)}, u32[]{:S(2)}, u32[]{:S(2)}) %collective-permute-start.39) | collective-permute-done | bytes 368672 | tf_op jit(solution)/shard_map/ppermute | solution.py:558
  395.8 1.8 collective-permute-start.51
  398.9 34.7 %reduce-scatter.9.cloned.1.call-done = bf16[176,240]{1,0:T(8,128)(2,1)} async-done(((bf16[704,240]{1,0:T(8,128)(2,1)}), bf16[176,240]{1,0:T(8,128)(2,1)}) %reduce-scatter.9.cloned.1.call-update) | async-done | bytes 84496 | tf_op jit(solution)/shard_map/reduce_scatter | solution.py:718
  437.3 5.4 %collective-permute-done.46 = bf16[656,240]{1,0:T(8,128)(2,1)S(1)} collective-permute-done((bf16[656,240]{1,0:T(8,128)(2,1)S(1)}, bf16[656,240]{1,0:T(8,128)(2,1)S(1)}, u32[]{:S(2)}, u32[]{:S(2)}) %collective-permute-start.46) | collective-permute-done | bytes 314912 | tf_op jit(solution)/shard_map/ppermute | solution.py:542
  445.3 2.5 collective-permute-done.48.o2
  448.5 1.7 copy.25
  450.2 2.7 merge.1
  454.1 2.5 grads.1
  (219 shorter events, 55.2 us)
Async XLA Ops:
  7.2 130.8 %all-gather.3.cloned.1.call-start = ((), (), s32[]{:S(2)}) async-start(), calls=%async_computation.4 | async-start | bytes 1638400 | tf_op jit(solution)/shard_map/all_gather | solution.py:614
  12.1 16.4 %collective-permute-start.5 = (bf16[240,128]{1,0:T(8,128)(2,1)S(1)}, bf16[240,128]{1,0:T(8,128)(2,1)S(1)}, u32[]{:S(2)}, u32[]{:S(2)}) collective-permute-start(bf16[240,128]{1,0:T(8,128)(2,1)S(1)} %get-tuple-element.194), channel_id=1, source_target_pairs={{0,4},{4,0},{8,12},{12,8},{1,5},{5,1},{9,13},{13,9},{2,6},{6,2},{1... | collective-permute-start | bytes 184328 | tf_op jit(solution)/shard_map/ppermute | solution.py:496
  13.0 17.1 %collective-permute-start.7 = (bf16[240,128]{1,0:T(8,128)(2,1)S(1)}, bf16[240,128]{1,0:T(8,128)(2,1)S(1)}, u32[]{:S(2)}, u32[]{:S(2)}) collective-permute-start(bf16[240,128]{1,0:T(8,128)(2,1)S(1)} %add_convert_fusion.8), channel_id=1, source_target_pairs={{0,8},{4,12},{8,0},{12,4},{1,9},{5,13},{9,1},{13,5},{2,10},{6,14},... | collective-permute-start | bytes 184328 | tf_op jit(solution)/shard_map/ppermute | solution.py:496
  22.3 45.9 %collective-permute-start.2 = (bf16[480,384]{1,0:T(8,128)(2,1)}, bf16[480,384]{1,0:T(8,128)(2,1)S(1)}, u32[]{:S(2)}, u32[]{:S(2)}) collective-permute-start(bf16[480,384]{1,0:T(8,128)(2,1)} %get-tuple-element.86), channel_id=1, source_target_pairs={{0,4},{1,0},{2,12},{3,8},{4,6},{5,2},{6,14},{7,10},{8,5},{9,1},{10... | collective-permute-start | bytes 1105928 | tf_op jit(solution)/shard_map/ppermute | solution.py:550
  22.3 46.8 %collective-permute-start.3 = (bf16[480,384]{1,0:T(8,128)(2,1)}, bf16[480,384]{1,0:T(8,128)(2,1)S(1)}, u32[]{:S(2)}, u32[]{:S(2)}) collective-permute-start(bf16[480,384]{1,0:T(8,128)(2,1)} %get-tuple-element.87), channel_id=1, source_target_pairs={{0,8},{1,12},{2,0},{3,4},{4,10},{5,14},{6,2},{7,6},{8,9},{9,13},{1... | collective-permute-start | bytes 1105928 | tf_op jit(solution)/shard_map/ppermute | solution.py:550
  24.8 44.3 %collective-permute-start.4 = (bf16[480,384]{1,0:T(8,128)(2,1)}, bf16[480,384]{1,0:T(8,128)(2,1)S(1)}, u32[]{:S(2)}, u32[]{:S(2)}) collective-permute-start(bf16[480,384]{1,0:T(8,128)(2,1)} %get-tuple-element.88), channel_id=1, source_target_pairs={{0,12},{1,8},{2,4},{3,0},{4,14},{5,10},{6,6},{7,2},{8,13},{9,9},{1... | collective-permute-start | bytes 1105928 | tf_op jit(solution)/shard_map/ppermute | solution.py:550
  28.5 40.6 %collective-permute-start.1 = (bf16[480,384]{1,0:T(8,128)(2,1)}, bf16[480,384]{1,0:T(8,128)(2,1)S(1)}, u32[]{:S(2)}, u32[]{:S(2)}) collective-permute-start(bf16[480,384]{1,0:T(8,128)(2,1)} %get-tuple-element.85), channel_id=1, source_target_pairs={{0,0},{1,4},{2,8},{3,12},{4,2},{5,6},{6,10},{7,14},{8,1},{9,5},{10... | collective-permute-start | bytes 1105928 | tf_op jit(solution)/shard_map/ppermute | solution.py:550
  30.3 37.9 %collective-permute-start.8 = (bf16[240,640]{1,0:T(8,128)(2,1)S(1)}, bf16[240,640]{1,0:T(8,128)(2,1)S(1)}, u32[]{:S(2)}, u32[]{:S(2)}) collective-permute-start(bf16[240,640]{1,0:T(8,128)(2,1)S(1)} %pad_maximum_fusion.3), channel_id=1, source_target_pairs={{0,1},{1,2},{2,3},{3,0},{4,5},{5,6},{6,7},{7,4},{8,9},{9,10},{10,1... | collective-permute-start | bytes 921608 | tf_op jit(solution)/shard_map/ppermute | solution.py:527
  68.2 18.3 %collective-permute-start.12 = (bf16[240,640]{1,0:T(8,128)(2,1)S(1)}, bf16[240,640]{1,0:T(8,128)(2,1)}, u32[]{:S(2)}, u32[]{:S(2)}) collective-permute-start(bf16[240,640]{1,0:T(8,128)(2,1)S(1)} %pad_maximum_fusion.3), channel_id=1, source_target_pairs={{0,8},{4,12},{8,0},{12,4},{1,9},{5,13},{9,1},{13,5},{2,10},{6,14},... | collective-permute-start | bytes 921608 | tf_op jit(solution)/shard_map/ppermute | solution.py:496
  68.2 16.1 %collective-permute-start.9 = (bf16[240,640]{1,0:T(8,128)(2,1)S(1)}, bf16[240,640]{1,0:T(8,128)(2,1)}, u32[]{:S(2)}, u32[]{:S(2)}) collective-permute-start(bf16[240,640]{1,0:T(8,128)(2,1)S(1)} %collective-permute-done.8), channel_id=1, source_target_pairs={{0,1},{1,2},{2,3},{3,0},{4,5},{5,6},{6,7},{7,4},{8,9},{9,10},{10,1... | collective-permute-start | bytes 921608 | tf_op jit(solution)/shard_map/ppermute | solution.py:527
  69.2 110.6 %all-gather.5.cloned.1.call-start = ((), (), s32[]{:S(2)}) async-start(), calls=%async_computation.5 | async-start | bytes 1536000 | tf_op jit(solution)/shard_map/all_gather | solution.py:627
  69.2 27.4 %collective-permute-start.13 = (bf16[240,640]{1,0:T(8,128)(2,1)S(1)}, bf16[240,640]{1,0:T(8,128)(2,1)S(1)}, u32[]{:S(2)}, u32[]{:S(2)}) collective-permute-start(bf16[240,640]{1,0:T(8,128)(2,1)S(1)} %collective-permute-done.8), channel_id=1, source_target_pairs={{0,8},{4,12},{8,0},{12,4},{1,9},{5,13},{9,1},{13,5},{2,10},{6,14},... | collective-permute-start | bytes 921608 | tf_op jit(solution)/shard_map/ppermute | solution.py:496
  84.3 12.3 %collective-permute-start.10 = (bf16[240,640]{1,0:T(8,128)(2,1)}, bf16[240,640]{1,0:T(8,128)(2,1)S(1)}, u32[]{:S(2)}, u32[]{:S(2)}) collective-permute-start(bf16[240,640]{1,0:T(8,128)(2,1)} %collective-permute-done.9), channel_id=1, source_target_pairs={{0,1},{1,2},{2,3},{3,0},{4,5},{5,6},{6,7},{7,4},{8,9},{9,10},{10,1... | collective-permute-start | bytes 921608 | tf_op jit(solution)/shard_map/ppermute | solution.py:527
  87.6 13.3 %collective-permute-start.14 = (bf16[240,640]{1,0:T(8,128)(2,1)}, bf16[240,640]{1,0:T(8,128)(2,1)S(1)}, u32[]{:S(2)}, u32[]{:S(2)}) collective-permute-start(bf16[240,640]{1,0:T(8,128)(2,1)} %collective-permute-done.9), channel_id=1, source_target_pairs={{0,8},{4,12},{8,0},{12,4},{1,9},{5,13},{9,1},{13,5},{2,10},{6,14},... | collective-permute-start | bytes 921608 | tf_op jit(solution)/shard_map/ppermute | solution.py:496
  96.6 8.4 %collective-permute-start.15 = (bf16[240,640]{1,0:T(8,128)(2,1)S(1)}, bf16[240,640]{1,0:T(8,128)(2,1)S(1)}, u32[]{:S(2)}, u32[]{:S(2)}) collective-permute-start(bf16[240,640]{1,0:T(8,128)(2,1)S(1)} %collective-permute-done.10), channel_id=1, source_target_pairs={{0,8},{4,12},{8,0},{12,4},{1,9},{5,13},{9,1},{13,5},{2,10},{6,14},... | collective-permute-start | bytes 921608 | tf_op jit(solution)/shard_map/ppermute | solution.py:496
  96.7 15.4 %collective-permute-start.11 = (bf16[960,640]{1,0:T(8,128)(2,1)S(1)}, bf16[960,640]{1,0:T(8,128)(2,1)}, u32[]{:S(2)}, u32[]{:S(2)}) collective-permute-start(bf16[960,640]{1,0:T(8,128)(2,1)S(1)} %constant_dynamic-update-slice_fusion.refs_4_), channel_id=1, source_target_pairs={{0,4},{4,0},{8,12},{12,8},{1,5},{5,1},{9,13},{13,9},{2,6},{6,2},{1... | collective-permute-start | bytes 3686408 | tf_op jit(solution)/shard_map/ppermute | solution.py:496
  105.0 7.1 %collective-permute-start.16 = (bf16[960,640]{1,0:T(8,128)(2,1)S(1)}, bf16[960,640]{1,0:T(8,128)(2,1)}, u32[]{:S(2)}, u32[]{:S(2)}) collective-permute-start(bf16[960,640]{1,0:T(8,128)(2,1)S(1)} %constant_dynamic-update-slice_fusion.4.refs_6_), channel_id=1, source_target_pairs={{0,4},{4,0},{8,12},{12,8},{1,5},{5,1},{9,13},{13,9},{2,6},{6,2},{1... | collective-permute-start | bytes 3686408 | tf_op jit(solution)/shard_map/ppermute | solution.py:496
  121.2 13.5 %collective-permute-start.18 = (bf16[5,128,384]{2,1,0:T(8,128)(2,1)}, bf16[5,128,384]{2,1,0:T(8,128)(2,1)}, u32[]{:S(2)}, u32[]{:S(2)}) collective-permute-start(bf16[5,128,384]{2,1,0:T(8,128)(2,1)} %get-tuple-element.91.kv0), channel_id=1, source_target_pairs={{0,8},{4,12},{8,0},{12,4},{1,9},{5,13},{9,1},{13,5},{2,10},{6,14},... | collective-permute-start | bytes 1474568 | tf_op jit(solution)/shard_map/ppermute | solution.py:496
  122.0 177.9 %reduce-scatter.5.cloned.1.call-start = ((), (), s32[]{:S(2)}) async-start(), calls=%async_computation.6 | async-start | bytes 2457600 | tf_op jit(solution)/shard_map/reduce_scatter | solution.py:690
  128.3 10.6 %collective-permute-start.17 = (bf16[5,128,384]{2,1,0:T(8,128)(2,1)}, bf16[5,128,384]{2,1,0:T(8,128)(2,1)}, u32[]{:S(2)}, u32[]{:S(2)}) collective-permute-start(bf16[5,128,384]{2,1,0:T(8,128)(2,1)} %get-tuple-element.91.kv0), channel_id=1, source_target_pairs={{0,4},{4,0},{8,12},{12,8},{1,5},{5,1},{9,13},{13,9},{2,6},{6,2},{1... | collective-permute-start | bytes 1474568 | tf_op jit(solution)/shard_map/ppermute | solution.py:496
  138.0 25.4 %collective-permute-start.23 = (bf16[960,384]{1,0:T(8,128)(2,1)S(1)}, bf16[960,384]{1,0:T(8,128)(2,1)}, u32[]{:S(2)}, u32[]{:S(2)}) collective-permute-start(bf16[960,384]{1,0:T(8,128)(2,1)S(1)} %copy-done), channel_id=1, source_target_pairs={{0,8},{4,12},{8,0},{12,4},{1,9},{5,13},{9,1},{13,5},{2,10},{6,14},... | collective-permute-start | bytes 2211848 | tf_op jit(solution)/shard_map/ppermute | solution.py:496
  154.3 19.3 %collective-permute-start.21 = (bf16[960,384]{1,0:T(8,128)(2,1)}, bf16[960,384]{1,0:T(8,128)(2,1)}, u32[]{:S(2)}, u32[]{:S(2)}) collective-permute-start(bf16[960,384]{1,0:T(8,128)(2,1)} %get-tuple-element.108.refs_3_.refs_0_), channel_id=1, source_target_pairs={{0,8},{4,12},{8,0},{12,4},{1,9},{5,13},{9,1},{13,5},{2,10},{6,14},... | collective-permute-start | bytes 2211848 | tf_op jit(solution)/shard_map/ppermute | solution.py:496
  162.1 26.0 %collective-permute-start.20 = (bf16[512,1280]{1,0:T(8,128)(2,1)S(1)}, bf16[512,1280]{1,0:T(8,128)(2,1)S(1)}, u32[]{:S(2)}, u32[]{:S(2)}) collective-permute-start(bf16[512,1280]{1,0:T(8,128)(2,1)S(1)} %copy-done.1), channel_id=1, source_target_pairs={{0,16},{16,0},{1,17},{17,1},{2,18},{18,2},{3,19},{19,3},{4,20},{20... | collective-permute-start | bytes 3932168 | tf_op jit(solution)/shard_map/ppermute | solution.py:616
  163.4 24.7 %collective-permute-start.24 = (bf16[960,384]{1,0:T(8,128)(2,1)}, bf16[960,384]{1,0:T(8,128)(2,1)}, u32[]{:S(2)}, u32[]{:S(2)}) collective-permute-start(bf16[960,384]{1,0:T(8,128)(2,1)} %collective-permute-done.23.refs_5_.refs_6_), channel_id=1, source_target_pairs={{0,4},{4,0},{8,12},{12,8},{1,5},{5,1},{9,13},{13,9},{2,6},{6,2},{1... | collective-permute-start | bytes 2211848 | tf_op jit(solution)/shard_map/ppermute | solution.py:496
  173.5 14.6 %collective-permute-start.22 = (bf16[960,384]{1,0:T(8,128)(2,1)}, bf16[960,384]{1,0:T(8,128)(2,1)}, u32[]{:S(2)}, u32[]{:S(2)}) collective-permute-start(bf16[960,384]{1,0:T(8,128)(2,1)} %collective-permute-done.21.refs_3_.refs_2_), channel_id=1, source_target_pairs={{0,4},{4,0},{8,12},{12,8},{1,5},{5,1},{9,13},{13,9},{2,6},{6,2},{1... | collective-permute-start | bytes 2211848 | tf_op jit(solution)/shard_map/ppermute | solution.py:496
  201.9 7.9 %collective-permute-start.28 = (bf16[960,384]{1,0:T(8,128)(2,1)}, bf16[960,384]{1,0:T(8,128)(2,1)S(1)}, u32[]{:S(2)}, u32[]{:S(2)}) collective-permute-start(bf16[960,384]{1,0:T(8,128)(2,1)} %get-tuple-element.103), channel_id=1, source_target_pairs={{0,4},{4,0},{8,12},{12,8},{1,5},{5,1},{9,13},{13,9},{2,6},{6,2},{1... | collective-permute-start | bytes 2211848 | tf_op jit(solution)/shard_map/ppermute | solution.py:496
  211.0 18.8 %collective-permute-start.29 = (bf16[960,384]{1,0:T(8,128)(2,1)S(1)}, bf16[960,384]{1,0:T(8,128)(2,1)S(1)}, u32[]{:S(2)}, u32[]{:S(2)}) collective-permute-start(bf16[960,384]{1,0:T(8,128)(2,1)S(1)} %add_convert_fusion.3), channel_id=1, source_target_pairs={{0,8},{4,12},{8,0},{12,4},{1,9},{5,13},{9,1},{13,5},{2,10},{6,14},... | collective-permute-start | bytes 2211848 | tf_op jit(solution)/shard_map/ppermute | solution.py:496
  247.7 148.1 %reduce-scatter.11.cloned.1.call-start = ((), (), s32[]{:S(2)}) async-start(), calls=%async_computation.9 | async-start | bytes 2150400 | tf_op jit(solution)/shard_map/reduce_scatter | solution.py:690
  249.3 148.6 %reduce-scatter.7.cloned.1.call-start = ((), (), s32[]{:S(2)}) async-start(), calls=%async_computation.7 | async-start | bytes 1228800 | tf_op jit(solution)/shard_map/reduce_scatter | solution.py:716
  252.2 37.2 %collective-permute-start.32 = (bf16[960,384]{1,0:T(8,128)(2,1)S(1)}, bf16[960,384]{1,0:T(8,128)(2,1)S(1)}, u32[]{:S(2)}, u32[]{:S(2)}) collective-permute-start(bf16[960,384]{1,0:T(8,128)(2,1)S(1)} %add_convert_fusion.2), channel_id=1, source_target_pairs={{0,8},{4,12},{8,0},{12,4},{1,9},{5,13},{9,1},{13,5},{2,10},{6,14},... | collective-permute-start | bytes 2211848 | tf_op jit(solution)/shard_map/ppermute | solution.py:496
  281.7 18.3 %collective-permute-start.33 = (bf16[5,128,384]{2,1,0:T(8,128)(2,1)}, bf16[5,128,384]{2,1,0:T(8,128)(2,1)S(1)}, u32[]{:S(2)}, u32[]{:S(2)}) collective-permute-start(bf16[5,128,384]{2,1,0:T(8,128)(2,1)} %get-tuple-element.134), channel_id=1, source_target_pairs={{0,4},{4,0},{8,12},{12,8},{1,5},{5,1},{9,13},{13,9},{2,6},{6,2},{1... | collective-permute-start | bytes 1474568 | tf_op jit(solution)/shard_map/ppermute | solution.py:496
  289.3 13.4 %collective-permute-start.31 = (bf16[4,480,240]{2,1,0:T(8,128)(2,1)}, bf16[4,480,240]{2,1,0:T(8,128)(2,1)S(1)}, u32[]{:S(2)}, u32[]{:S(2)}) collective-permute-start(bf16[4,480,240]{2,1,0:T(8,128)(2,1)} %get-tuple-element.131), channel_id=1, source_target_pairs={{0,4},{4,0},{8,12},{12,8},{1,5},{5,1},{9,13},{13,9},{2,6},{6,2},{1... | collective-permute-start | bytes 2764808 | tf_op jit(solution)/shard_map/ppermute | solution.py:496
  301.1 12.9 %collective-permute-start.34 = (bf16[5,128,384]{2,1,0:T(8,128)(2,1)S(1)}, bf16[5,128,384]{2,1,0:T(8,128)(2,1)S(1)}, u32[]{:S(2)}, u32[]{:S(2)}) collective-permute-start(bf16[5,128,384]{2,1,0:T(8,128)(2,1)S(1)} %add_convert_fusion.4), channel_id=1, source_target_pairs={{0,8},{4,12},{8,0},{12,4},{1,9},{5,13},{9,1},{13,5},{2,10},{6,14},... | collective-permute-start | bytes 1474568 | tf_op jit(solution)/shard_map/ppermute | solution.py:496
  302.7 13.3 %collective-permute-start.41 = (bf16[4,480,240]{2,1,0:T(8,128)(2,1)}, bf16[4,480,240]{2,1,0:T(8,128)(2,1)S(1)}, u32[]{:S(2)}, u32[]{:S(2)}) collective-permute-start(bf16[4,480,240]{2,1,0:T(8,128)(2,1)} %get-tuple-element.151), channel_id=1, source_target_pairs={{0,4},{4,0},{8,12},{12,8},{1,5},{5,1},{9,13},{13,9},{2,6},{6,2},{1... | collective-permute-start | bytes 2764808 | tf_op jit(solution)/shard_map/ppermute | solution.py:496
  314.0 22.5 %collective-permute-start.42 = (bf16[4,480,240]{2,1,0:T(8,128)(2,1)S(1)}, bf16[4,480,240]{2,1,0:T(8,128)(2,1)S(1)}, u32[]{:S(2)}, u32[]{:S(2)}) collective-permute-start(bf16[4,480,240]{2,1,0:T(8,128)(2,1)S(1)} %add_convert_fusion.1), channel_id=1, source_target_pairs={{0,8},{4,12},{8,0},{12,4},{1,9},{5,13},{9,1},{13,5},{2,10},{6,14},... | collective-permute-start | bytes 2764808 | tf_op jit(solution)/shard_map/ppermute | solution.py:496
  315.4 22.6 %collective-permute-start.36 = (bf16[960,384]{1,0:T(8,128)(2,1)S(1)}, bf16[960,384]{1,0:T(8,128)(2,1)S(1)}, u32[]{:S(2)}, u32[]{:S(2)}) collective-permute-start(bf16[960,384]{1,0:T(8,128)(2,1)S(1)} %copy-done.35), channel_id=1, source_target_pairs={{0,4},{4,0},{8,12},{12,8},{1,5},{5,1},{9,13},{13,9},{2,6},{6,2},{1... | collective-permute-start | bytes 2211848 | tf_op jit(solution)/shard_map/ppermute | solution.py:496
  315.4 22.6 %collective-permute-start.35 = (bf16[5,128,384]{2,1,0:T(8,128)(2,1)}, bf16[5,128,384]{2,1,0:T(8,128)(2,1)S(1)}, u32[]{:S(2)}, u32[]{:S(2)}) collective-permute-start(bf16[5,128,384]{2,1,0:T(8,128)(2,1)} %get-tuple-element.137), channel_id=1, source_target_pairs={{0,4},{4,0},{8,12},{12,8},{1,5},{5,1},{9,13},{13,9},{2,6},{6,2},{1... | collective-permute-start | bytes 1474568 | tf_op jit(solution)/shard_map/ppermute | solution.py:496
  337.9 95.6 %reduce-scatter.9.cloned.1.call-start = ((), (), s32[]{:S(2)}) async-start(), calls=%async_computation.8 | async-start | bytes 450560 | tf_op jit(solution)/shard_map/reduce_scatter | solution.py:718
  358.2 21.8 %collective-permute-start.43 = (bf16[4,176,240]{2,1,0:T(8,128)(2,1)}, bf16[4,176,240]{2,1,0:T(8,128)(2,1)S(1)}, u32[]{:S(2)}, u32[]{:S(2)}) collective-permute-start(bf16[4,176,240]{2,1,0:T(8,128)(2,1)} %get-tuple-element.153), channel_id=1, source_target_pairs={{0,4},{4,0},{8,12},{12,8},{1,5},{5,1},{9,13},{13,9},{2,6},{6,2},{1... | collective-permute-start | bytes 1013768 | tf_op jit(solution)/shard_map/ppermute | solution.py:496
  361.2 22.8 %collective-permute-start.45 = (bf16[4,176,240]{2,1,0:T(8,128)(2,1)S(1)}, bf16[4,176,240]{2,1,0:T(8,128)(2,1)S(1)}, u32[]{:S(2)}, u32[]{:S(2)}) collective-permute-start(bf16[4,176,240]{2,1,0:T(8,128)(2,1)S(1)} %add_convert_fusion.6), channel_id=1, source_target_pairs={{0,8},{4,12},{8,0},{12,4},{1,9},{5,13},{9,1},{13,5},{2,10},{6,14},... | collective-permute-start | bytes 1013768 | tf_op jit(solution)/shard_map/ppermute | solution.py:496
  362.6 22.2 %collective-permute-start.37 = (bf16[480,384]{1,0:T(8,128)(2,1)}, bf16[480,384]{1,0:T(8,128)(2,1)S(1)}, u32[]{:S(2)}, u32[]{:S(2)}) collective-permute-start(bf16[480,384]{1,0:T(8,128)(2,1)} %get-tuple-element.144), channel_id=1, source_target_pairs={{0,0},{1,8},{2,4},{3,12},{4,1},{5,9},{6,5},{7,13},{8,2},{9,10},{10... | collective-permute-start | bytes 1105928 | tf_op jit(solution)/shard_map/ppermute | solution.py:558
  364.3 20.5 %collective-permute-start.38 = (bf16[480,384]{1,0:T(8,128)(2,1)}, bf16[480,384]{1,0:T(8,128)(2,1)S(1)}, u32[]{:S(2)}, u32[]{:S(2)}) collective-permute-start(bf16[480,384]{1,0:T(8,128)(2,1)} %get-tuple-element.145), channel_id=1, source_target_pairs={{0,1},{1,9},{2,5},{3,13},{4,0},{5,8},{6,4},{7,12},{8,3},{9,11},{10... | collective-permute-start | bytes 1105928 | tf_op jit(solution)/shard_map/ppermute | solution.py:558
  366.7 27.7 %collective-permute-start.39 = (bf16[480,384]{1,0:T(8,128)(2,1)}, bf16[480,384]{1,0:T(8,128)(2,1)S(1)}, u32[]{:S(2)}, u32[]{:S(2)}) collective-permute-start(bf16[480,384]{1,0:T(8,128)(2,1)} %get-tuple-element.146), channel_id=1, source_target_pairs={{0,2},{1,10},{2,6},{3,14},{4,3},{5,11},{6,7},{7,15},{8,0},{9,8},{1... | collective-permute-start | bytes 1105928 | tf_op jit(solution)/shard_map/ppermute | solution.py:558
  380.0 15.8 %collective-permute-start.40 = (bf16[480,384]{1,0:T(8,128)(2,1)}, bf16[480,384]{1,0:T(8,128)(2,1)S(1)}, u32[]{:S(2)}, u32[]{:S(2)}) collective-permute-start(bf16[480,384]{1,0:T(8,128)(2,1)} %get-tuple-element.147), channel_id=1, source_target_pairs={{0,3},{1,11},{2,7},{3,15},{4,2},{5,10},{6,6},{7,14},{8,1},{9,9},{1... | collective-permute-start | bytes 1105928 | tf_op jit(solution)/shard_map/ppermute | solution.py:558
  395.8 40.1 %collective-permute-start.51 = (bf16[240,896]{1,0:T(8,128)(2,1)}, bf16[240,896]{1,0:T(8,128)(2,1)S(1)}, u32[]{:S(2)}, u32[]{:S(2)}) collective-permute-start(bf16[240,896]{1,0:T(8,128)(2,1)} %reduce-scatter.11.cloned.1.call-done), channel_id=1, source_target_pairs={{0,16},{16,0},{1,17},{17,1},{2,18},{18,2},{3,19},{19,3},{4,20},{20... | collective-permute-start | bytes 1290248 | tf_op jit(solution)/shard_map/ppermute | solution.py:542
  397.6 39.4 %collective-permute-start.50 = (bf16[240,1024]{1,0:T(8,128)(2,1)S(1)}, bf16[240,1024]{1,0:T(8,128)(2,1)S(1)}, u32[]{:S(2)}, u32[]{:S(2)}) collective-permute-start(bf16[240,1024]{1,0:T(8,128)(2,1)S(1)} %copy-done.20), channel_id=1, source_target_pairs={{0,16},{16,0},{1,17},{17,1},{2,18},{18,2},{3,19},{19,3},{4,20},{20... | collective-permute-start | bytes 1474568 | tf_op jit(solution)/shard_map/ppermute | solution.py:542
  434.5 8.2 %collective-permute-start.46 = (bf16[656,240]{1,0:T(8,128)(2,1)S(1)}, bf16[656,240]{1,0:T(8,128)(2,1)S(1)}, u32[]{:S(2)}, u32[]{:S(2)}) collective-permute-start(bf16[656,240]{1,0:T(8,128)(2,1)S(1)} %constant_dynamic-update-slice_fusion.8), channel_id=1, source_target_pairs={{0,16},{16,0},{1,17},{17,1},{2,18},{18,2},{3,19},{19,3},{4,20},{20... | collective-permute-start | bytes 944648 | tf_op jit(solution)/shard_map/ppermute | solution.py:542
  445.3 7.5 %collective-permute-start.47 = (f32[128,240]{1,0:T(8,128)S(1)}, f32[128,240]{1,0:T(8,128)S(1)}, u32[]{:S(2)}, u32[]{:S(2)}) collective-permute-start(f32[128,240]{1,0:T(8,128)S(1)} %pad_maximum_fusion.4.o0), channel_id=1, source_target_pairs={{0,4},{4,0},{8,12},{12,8},{1,5},{5,1},{9,13},{13,9},{2,6},{6,2},{1... | collective-permute-start | bytes 368648 | tf_op jit(solution)/shard_map/ppermute | solution.py:496
  (48 other events, 635.4 us)
Sparse Core Ops, SparseCore 0:
  69.3 48.7 all-gather.2
  122.2 37.8 all-gather.4
  247.8 52.1 reduce-scatter.4
  302.1 36.9 reduce-scatter.10
  341.4 40.9 reduce-scatter.6
  395.9 37.6 reduce-scatter.8

commit v3 on v2

--- a/solution.py
+++ b/solution.py
@@ -379,7 +379,7 @@
         n2 = refs[i]
         dy = refs[count + i]
         a_ref, dg_ref, du_ref, mlp_ref, dn_ref = refs[2 * count + 5 * i : 2 * count + 5 * i + 5]
-        step = 128
+        step = width
         for f in range(0, width, step):
             cols = slice(f, f + step)
             gate = tn(w[:, f : f + step], n2[...])
@@ -399,15 +399,14 @@
     outs = refs[-2:]
     width = acts[0].shape[0]
     edge = outs[0].shape[1]
-    step = 128
     for part, (left, right) in enumerate(((n2s, gates), (n2s, ups), (dys, acts))):
-        for f in range(0, width, step):
-            total = nt(left[0][...], right[0][f : f + step])
+        begin = part * width
+        cuts = [begin] + ([edge] if begin < edge < begin + width else []) + [begin + width]
+        for low, high in zip(cuts[:-1], cuts[1:]):
+            total = nt(left[0][...], right[0][low - begin : high - begin])
             for k in range(1, ROWS):
-                total = total + nt(left[k][...], right[k][f : f + step])
-            col = part * width + f
-            out = outs[col // edge]
-            out[:, col % edge : col % edge + step] = total.astype(BF)
+                total = total + nt(left[k][...], right[k][low - begin : high - begin])
+            outs[low // edge][:, low % edge : low % edge + high - low] = total.astype(BF)
 
 
 def grads_kernel(sc, g_ref, o0, o1, o2, o3, qkv_ref, out_ref, gains_ref, oa_s, ob_s):
@@ -543,12 +542,9 @@
     return lax.psum(values, "dp").astype(F32)
 
 
-def to_tokens(pieces):
-    out = []
-    for k in range(ROWS):
-        pairs = [(a * ROWS + b, (b ^ k) * ROWS + SEQ_MAP[a]) for a in range(ROWS) for b in range(ROWS)]
-        out.append(lax.ppermute(pieces[k], ("gx", "gy"), pairs))
-    return out
+def to_token(k, piece):
+    pairs = [(a * ROWS + b, (b ^ k) * ROWS + SEQ_MAP[a]) for a in range(ROWS) for b in range(ROWS)]
+    return lax.ppermute(piece, ("gx", "gy"), pairs)
 
 
 def to_features(pieces):
@@ -601,12 +597,14 @@
     odd = jnp.where(ix == odd_row, odd, jnp.zeros_like(odd))
     quarter = row_scatter([lax.dynamic_slice(odd, (0, ODD * (ix ^ k)), (FB, ODD)) for k in range(ROWS)])
     w_pieces = [after(jnp.concatenate([w_qkv[:, :SLOT_W], w_out[:, :QW], quarter], axis=1), pieces[0])]
-    toks = to_tokens(pieces)
-    for _ in range(ROWS - 1):
-        w_pieces.append(ring(w_pieces[-1]))
+    toks = []
+    for k in range(ROWS):
+        toks.append(to_token(k, after(pieces[k], *w_pieces[1:])))
+        if k < ROWS - 1:
+            w_pieces.append(ring(after(w_pieces[-1], *toks[:k])))
     w_own = jnp.concatenate(w_pieces, axis=0)
     w_far = jnp.concatenate([swap(w, 2) for w in w_pieces], axis=0)
-    w_rows = [w_own, swap(w_own, 1), w_far, swap(w_far, 1)]
+    w_rows = [w_own, swap(after(w_own, toks[2]), 1), w_far, swap(after(w_far, toks[2], toks[3]), 1)]
     w_gu = jnp.concatenate([w_gate_up[:, 0], w_gate_up[:, 1]], axis=1)
     halves = lax.axis_size("dp") == 2
     if halves:
@@ -710,13 +708,16 @@
 
     g_mlp = jnp.concatenate([dp_sum(g) for g in g_mlp], axis=1)
     grad_down = g_mlp[:, 2 * ff :]
-    g_a = sum(term.astype(F32) for term in a_terms).astype(BF)
+    a_terms[0] = after(a_terms[0], packs_b[0])
+    g_a = (
+        (a_terms[0].astype(F32) + a_terms[1].astype(F32)) + a_terms[2].astype(F32)
+    ).astype(BF)
     packs_b = list(packs_b)
-    packs_b[2] = after(packs_b[2], a_terms[2])
+    packs_b[3] = after(packs_b[3], g_a)
     g_a = lax.psum_scatter(g_a.reshape(ROWS * AP, FB), "gy", scatter_dimension=0, tiled=True)
-    g_b = after(row_scatter(packs_b).reshape(ROWS * BP, FB), *back)
+    g_b = row_scatter(packs_b).reshape(ROWS * BP, FB)
     g_b = lax.psum_scatter(g_b, "gy", scatter_dimension=0, tiled=True)
-    g_all = dp_sum(jnp.concatenate([g_a, g_b], axis=0))
+    g_all = dp_sum(after(jnp.concatenate([g_a, g_b], axis=0), *back))
     odds = jnp.concatenate([g_all[AW:AP], g_all[AP + KV : AP + KV + KV // ROWS]], axis=0)
     grad_qkv, grad_out, grad_gains = simple(
         grads_kernel, "grads",

time: 470 us -> 463 us (0.985)
  starting transfers between devices: 111 us -> 88.5 us
  waiting for transfers between devices: 170 us -> 183 us
    reduce_scatter x1, waiting for transfers between devices: 0.01 us -> 39 us  [per_device(): lax.psum_scatter(g_a.reshape(ROWS * AP, FB), 'gy', scatter_dimension=0, t...]
    ppermute x3, waiting for transfers between devices: 5.97 us -> 38.9 us  [ring(): lax.ppermute(values, 'gy', [(i, (i + 1) % ROWS) for i in range(ROWS)])]
    ppermute x4, waiting for transfers between devices: 34.3 us -> 11.1 us  [to_token(): return lax.ppermute(piece, ('gx', 'gy'), pairs)]
    reduce_scatter x1, waiting for transfers between devices: 34.7 us -> 14.9 us  [per_device(): g_b = lax.psum_scatter(g_b, 'gy', scatter_dimension=0, tiled=True)]
    ppermute x4, starting transfers between devices: 21.3 us -> 6.55 us  [to_features(): back.append(lax.ppermute(pieces[k], ('gx', 'gy'), pairs))]
    ppermute x4, waiting for transfers between devices: 10.9 us -> 0.01 us  [to_features(): back.append(lax.ppermute(pieces[k], ('gx', 'gy'), pairs))]
    reduce_scatter x2, waiting for transfers between devices: 10.6 us -> 0.04 us  [per_device(): lax.psum_scatter(g, 'gy', scatter_dimension=0, tiled=True)]
    ppermute x1, waiting for transfers between devices: 8.29 us -> 18.3 us  [per_device(): w_gu.append(lax.ppermute(w_gu[0], 'dp', [(0, 1), (1, 0)]))]
  transfers between devices with their start and end apart: 58 -> 58, of which waited for: 20 -> 23; matrix products, arithmetic and copies ran while one was open for 6% -> 6% of each run, Pallas kernels for 19% -> 20%
where the time goes in v3:
time: 463 us; the launch traced here: 455 us
  waiting for transfers between devices  183 us (40%)
  Pallas kernels  120 us (26%)
  starting transfers between devices  88.5 us (19%)
  local copies, waits for them, and re-layouts  22.3 us (5%)
  between operations  21.3 us (5%)
  other arithmetic  18.8 us (4%)
    ppermute x36, starting transfers between devices, swap(): return lax.ppermute(values, 'gx', [(i, i ^ bit) for i in range(ROWS)])  64.7 us
    pallas_call x3, Pallas kernels, grouped(): pl.pallas_call(kernel, grid_spec=pltpu.PrefetchScalarGridSpec(num_scalar_...  62.5 us
    pallas_call x7, Pallas kernels, simple(): pl.pallas_call(kernel, in_specs=specs, out_specs=[pl.BlockSpec(memory_spa...  57.9 us
    ppermute x36, waiting for transfers between devices, swap(): return lax.ppermute(values, 'gx', [(i, i ^ bit) for i in range(ROWS)])  53.8 us
    reduce_scatter x1, waiting for transfers between devices, per_device(): lax.psum_scatter(g_a.reshape(ROWS * AP, FB), 'gy', scatter_dimension=0, t...  39 us
    ppermute x3, waiting for transfers between devices, ring(): lax.ppermute(values, 'gy', [(i, (i + 1) % ROWS) for i in range(ROWS)])  38.9 us
    ppermute x1, waiting for transfers between devices, per_device(): w_gu.append(lax.ppermute(w_gu[0], 'dp', [(0, 1), (1, 0)]))  18.3 us
    reduce_scatter x1, waiting for transfers between devices, per_device(): g_b = lax.psum_scatter(g_b, 'gy', scatter_dimension=0, tiled=True)  14.9 us
  transfers between devices with their start and end apart: 58, of which 23 were waited for; matrix products, arithmetic and copies ran while one was open for 6% of the time, Pallas kernels for 20%

profile of v3, /device:TPU:0, one launch (start us, length us, event | category | flops | bytes accessed | tf_op | source)
XLA Modules:
  0.0 454.7 jit_solution(8384745122175759131)
XLA Ops:
  13.0 2.9 collective-permute-start.4
  18.8 3.5 split.1
  22.3 1.6 collective-permute-start.1
  24.1 1.9 collective-permute-start.5
  26.0 17.3 %collective-permute-done.5 = bf16[240,640]{1,0:T(8,128)(2,1)S(1)} collective-permute-done((bf16[240,640]{1,0:T(8,128)(2,1)S(1)}, bf16[240,640]{1,0:T(8,128)(2,1)S(1)}, u32[]{:S(2)}, u32[]{:S(2)}) %collective-permute-start.5) | collective-permute-done | bytes 307232 | tf_op jit(solution)/shard_map/ppermute | solution.py:526
  43.4 2.2 collective-permute-start.7
  45.6 15.5 %collective-permute-done.7 = bf16[240,640]{1,0:T(8,128)(2,1)} collective-permute-done((bf16[240,640]{1,0:T(8,128)(2,1)S(1)}, bf16[240,640]{1,0:T(8,128)(2,1)}, u32[]{:S(2)}, u32[]{:S(2)}) %collective-permute-start.7) | collective-permute-done | bytes 307232 | tf_op jit(solution)/shard_map/ppermute | solution.py:526
  61.1 4.0 collective-permute-done.6.refs_1_
  66.2 2.0 collective-permute-start.8
  68.2 6.1 %collective-permute-done.9 = bf16[240,640]{1,0:T(8,128)(2,1)} collective-permute-done((bf16[240,640]{1,0:T(8,128)(2,1)}, bf16[240,640]{1,0:T(8,128)(2,1)}, u32[]{:S(2)}, u32[]{:S(2)}) %collective-permute-start.9) | collective-permute-done | bytes 307232 | tf_op jit(solution)/shard_map/ppermute | solution.py:526
  74.3 4.4 collective-permute-start.10
  80.5 2.1 collective-permute-start.14
  82.7 7.1 %collective-permute-done.10.refs_3_ = bf16[480,384]{1,0:T(8,128)(2,1)S(1)} collective-permute-done((bf16[480,384]{1,0:T(8,128)(2,1)}, bf16[480,384]{1,0:T(8,128)(2,1)S(1)}, u32[]{:S(2)}, u32[]{:S(2)}) %collective-permute-start.10) | collective-permute-done | bytes 368672 | tf_op jit(solution)/shard_map/ppermute | solution.py:547
  90.9 8.0 %collective-permute-start.15 = (bf16[240,640]{1,0:T(8,128)(2,1)}, bf16[240,640]{1,0:T(8,128)(2,1)S(1)}, u32[]{:S(2)}, u32[]{:S(2)}) collective-permute-start(bf16[240,640]{1,0:T(8,128)(2,1)} %collective-permute-done.9), channel_id=1, source_target_pairs={{0,8},{4,12},{8,0},{12,4},{1,9},{5,13},{9,1},{13,5},{2,10},{6,14},... | collective-permute-start | bytes 921608 | tf_op jit(solution)/shard_map/ppermute | solution.py:495
  102.0 6.6 %collective-permute-start.11 = (bf16[960,640]{1,0:T(8,128)(2,1)S(1)}, bf16[960,640]{1,0:T(8,128)(2,1)}, u32[]{:S(2)}, u32[]{:S(2)}) collective-permute-start(bf16[960,640]{1,0:T(8,128)(2,1)S(1)} %constant_dynamic-update-slice_fusion.refs_4_), channel_id=1, source_target_pairs={{0,4},{4,0},{8,12},{12,8},{1,5},{5,1},{9,13},{13,9},{2,6},{6,2},{1... | collective-permute-start | bytes 3686408 | tf_op jit(solution)/shard_map/ppermute | solution.py:495
  111.8 2.6 select_add_fusion
  115.4 9.0 %qkv.1 = (bf16[960,384]{1,0:T(8,128)(2,1)}, bf16[960,384]{1,0:T(8,128)(2,1)}, bf16[960,384]{1,0:T(8,128)(2,1)}, f32[1,384]{1,0:T(1,128)}, f32[960,1]{1,0:T(8,128...) custom-call(s32[4]{0:T(128)} %pad_add_fusion.sc, ...), custom_call_target="tpu_custom_call" | custom-call | flops 700000000 | bytes 2100000 | tf_op jit(solution)/shard_map/qkv/pallas_call | solution.py:465
  124.4 2.5 collective-permute-start.18
  133.2 5.5 %collective-permute-done.18.kv2 = bf16[5,128,384]{2,1,0:T(8,128)(2,1)} collective-permute-done((bf16[5,128,384]{2,1,0:T(8,128)(2,1)}, bf16[5,128,384]{2,1,0:T(8,128)(2,1)}, u32[]{:S(2)}, u32[]{:S(2)}) %collective-permute-start.18) | collective-permute-done | bytes 491552 | tf_op jit(solution)/shard_map/ppermute | solution.py:495
  140.5 1.6 pad_maximum_fusion.bias_ref
  142.1 1.7 collective-permute-start.23
  143.9 15.3 %attend.1 = (bf16[5,192,384]{2,1,0:T(8,128)(2,1)}, f32[5,8,384]{2,1,0:T(8,128)}, f32[960,384]{1,0:T(8,128)}, bf16[960,384]{1,0:T(8,128)(2,1)}, f32[1,384]{1,0:T(1,128)}) custom-call(s32[8]{0:T(128)} %concatenate.28.sc, bf16[5,192,384]{2,1,0:T(8,128)(2,1)} %get-tuple-element.109.qs_ref, bf16[5,128,384]{2,1,0:T(8,128)(2,1)} %get-tuple-element.106.kv0, ...), custom_call_target="tpu_custom_call" | custom-call | flops 1800000000 | bytes 5400000 | tf_op jit(solution)/shard_map/attend/pallas_call | solution.py:478
  159.2 13.6 %collective-permute-start.21 = (bf16[960,384]{1,0:T(8,128)(2,1)}, bf16[960,384]{1,0:T(8,128)(2,1)}, u32[]{:S(2)}, u32[]{:S(2)}) collective-permute-start(bf16[960,384]{1,0:T(8,128)(2,1)} %get-tuple-element.123.refs_3_.refs_0_), channel_id=1, source_target_pairs={{0,8},{4,12},{8,0},{12,4},{1,9},{5,13},{9,1},{13,5},{2,10},{6,14},... | collective-permute-start | bytes 2211848 | tf_op jit(solution)/shard_map/ppermute | solution.py:495
  174.0 10.9 %collective-permute-done.21.refs_3_.refs_2_ = bf16[960,384]{1,0:T(8,128)(2,1)} collective-permute-done((bf16[960,384]{1,0:T(8,128)(2,1)}, bf16[960,384]{1,0:T(8,128)(2,1)}, u32[]{:S(2)}, u32[]{:S(2)}) %collective-permute-start.21) | collective-permute-done | bytes 737312 | tf_op jit(solution)/shard_map/ppermute | solution.py:495
  184.9 18.3 %collective-permute-done.20.refs_1_ = bf16[512,1280]{1,0:T(8,128)(2,1)S(1)} collective-permute-done((bf16[512,1280]{1,0:T(8,128)(2,1)S(1)}, bf16[512,1280]{1,0:T(8,128)(2,1)S(1)}, u32[]{:S(2)}, u32[]{:S(2)}) %collective-permute-start.20) | collective-permute-done | bytes 1310752 | tf_op jit(solution)/shard_map/ppermute | solution.py:614
  204.3 12.8 %mlp_far.1 = (bf16[640,384]{1,0:T(8,128)(2,1)}, bf16[640,384]{1,0:T(8,128)(2,1)}, bf16[640,384]{1,0:T(8,128)(2,1)}, bf16[960,384]{1,0:T(8,128)(2,1)}, bf16[960,3...) custom-call(s32[4]{0:T(128)} %pad_add_fusion.sc, ...), custom_call_target="tpu_custom_call" | custom-call | flops 1300000000 | bytes 3900000 | tf_op jit(solution)/shard_map/mlp_far/pallas_call | solution.py:465
  217.7 2.1 collective-permute-done.28
  223.3 13.0 %mlp_near.1 = (bf16[640,384]{1,0:T(8,128)(2,1)}, bf16[640,384]{1,0:T(8,128)(2,1)}, bf16[640,384]{1,0:T(8,128)(2,1)}, bf16[960,384]{1,0:T(8,128)(2,1)}, bf16[960,...) custom-call(s32[4]{0:T(128)} %pad_add_fusion.sc, ...), custom_call_target="tpu_custom_call" | custom-call | flops 1300000000 | bytes 3900000 | tf_op jit(solution)/shard_map/mlp_near/pallas_call | solution.py:465
  236.3 3.5 collective-permute-done.29.dn_c
  239.8 14.4 %mlp_grad.1 = (bf16[960,1024]{1,0:T(8,128)(2,1)}, bf16[960,896]{1,0:T(8,128)(2,1)}) custom-call(bf16[960,384]{1,0:T(8,128)(2,1)} %get-tuple-element.123.refs_3_.refs_0_, bf16[960,384]{1,0:T(8,128)(2,1)} %copy-done.6, bf16[960,384]{1,0:T(8,128)(2,1)} %collective-permute-done.21.refs_3_.refs_2_, bf16[960,384]{1,0:T(8,128)(2,1)} %collective-permute-done.22.refs_4_.refs_3_, ...), custom_call_target="tpu_custom_call" | custom-call | flops 1800000000 | bytes 5400000 | tf_op jit(solution)/shard_map/mlp_grad/pallas_call | solution.py:465
  255.8 1.7 collective-permute-done.30
  259.5 28.2 %attend_back.1 = (bf16[5,192,384]{2,1,0:T(8,128)(2,1)}, f32[5,128,384]{2,1,0:T(8,128)}, bf16[5,128,384]{2,1,0:T(8,128)(2,1)}, bf16[5,128,384]{2,1,0:T(8,128)(2,1...) custom-call(s32[8]{0:T(128)} %concatenate.28.sc, ...), custom_call_target="tpu_custom_call" | custom-call | flops 3000000000 | bytes 9000000 | tf_op jit(solution)/shard_map/attend_back/pallas_call | solution.py:478
  287.7 7.9 %collective-permute-start.33 = (bf16[5,128,384]{2,1,0:T(8,128)(2,1)}, bf16[5,128,384]{2,1,0:T(8,128)(2,1)}, u32[]{:S(2)}, u32[]{:S(2)}) collective-permute-start(bf16[5,128,384]{2,1,0:T(8,128)(2,1)} %get-tuple-element.149), channel_id=1, source_target_pairs={{0,4},{4,0},{8,12},{12,8},{1,5},{5,1},{9,13},{13,9},{2,6},{6,2},{1... | collective-permute-start | bytes 1474568 | tf_op jit(solution)/shard_map/ppermute | solution.py:495
  298.7 9.1 %collective-permute-start.34 = (bf16[5,128,384]{2,1,0:T(8,128)(2,1)S(1)}, bf16[5,128,384]{2,1,0:T(8,128)(2,1)S(1)}, u32[]{:S(2)}, u32[]{:S(2)}) collective-permute-start(bf16[5,128,384]{2,1,0:T(8,128)(2,1)S(1)} %add_convert_fusion.4), channel_id=1, source_target_pairs={{0,8},{4,12},{8,0},{12,4},{1,9},{5,13},{9,1},{13,5},{2,10},{6,14},... | collective-permute-start | bytes 1474568 | tf_op jit(solution)/shard_map/ppermute | solution.py:495
  308.1 11.2 %collective-permute-done.34.d2 = bf16[5,128,384]{2,1,0:T(8,128)(2,1)S(1)} collective-permute-done((bf16[5,128,384]{2,1,0:T(8,128)(2,1)S(1)}, bf16[5,128,384]{2,1,0:T(8,128)(2,1)S(1)}, u32[]{:S(2)}, u32[]{:S(2)}) %collective-permute-start.34) | collective-permute-done | bytes 491552 | tf_op jit(solution)/shard_map/ppermute | solution.py:495
  319.4 1.7 collective-permute-start.42
  321.6 1.7 collective-permute-done.36.mlp_b
  324.8 19.0 %final.1 = (bf16[4,176,240]{2,1,0:T(8,128)(2,1)}, bf16[4,176,240]{2,1,0:T(8,128)(2,1)}, bf16[4,176,240]{2,1,0:T(8,128)(2,1)}, bf16[4,176,240]{2,1,0:T(8,128)(2,1...) custom-call(s32[8]{0:T(128)} %concatenate.28.sc, ...), custom_call_target="tpu_custom_call" | custom-call | flops 1900000000 | bytes 5700000 | tf_op jit(solution)/shard_map/final/pallas_call | solution.py:478
  347.4 10.1 %collective-permute-done.45 = bf16[4,176,240]{2,1,0:T(8,128)(2,1)S(1)} collective-permute-done((bf16[4,176,240]{2,1,0:T(8,128)(2,1)S(1)}, bf16[4,176,240]{2,1,0:T(8,128)(2,1)S(1)}, u32[]{:S(2)}, u32[]{:S(2)}) %collective-permute-start.45) | collective-permute-done | bytes 337952 | tf_op jit(solution)/shard_map/ppermute | solution.py:495
  360.1 3.2 collective-permute-start.38
  363.4 2.6 collective-permute-start.40
  367.6 14.9 %reduce-scatter.9.cloned.1.call-done = bf16[176,240]{1,0:T(8,128)(2,1)} async-done(((bf16[704,240]{1,0:T(8,128)(2,1)}), bf16[176,240]{1,0:T(8,128)(2,1)}) %reduce-scatter.9.cloned.1.call-update) | async-done | bytes 84496 | tf_op jit(solution)/shard_map/reduce_scatter | solution.py:719
  382.5 39.0 %reduce-scatter.7.cloned.1.call-done = bf16[480,240]{1,0:T(8,128)(2,1)} async-done(((bf16[1920,240]{1,0:T(8,128)(2,1)}), bf16[480,240]{1,0:T(8,128)(2,1)}) %reduce-scatter.7.cloned.1.call-update) | async-done | bytes 230416 | tf_op jit(solution)/shard_map/reduce_scatter | solution.py:717
  425.4 6.7 %collective-permute-done.46 = bf16[656,240]{1,0:T(8,128)(2,1)S(1)} collective-permute-done((bf16[656,240]{1,0:T(8,128)(2,1)S(1)}, bf16[656,240]{1,0:T(8,128)(2,1)S(1)}, u32[]{:S(2)}, u32[]{:S(2)}) %collective-permute-start.46) | collective-permute-done | bytes 314912 | tf_op jit(solution)/shard_map/ppermute | solution.py:541
  434.8 2.5 collective-permute-done.48.o2
  437.9 1.7 copy.25
  439.6 2.7 merge.1
  443.6 2.5 grads.1
  (236 shorter events, 54.6 us)
Async XLA Ops:
  7.2 136.7 %all-gather.3.cloned.1.call-start = ((), (), s32[]{:S(2)}) async-start(), calls=%async_computation.4 | async-start | bytes 1638400 | tf_op jit(solution)/shard_map/all_gather | solution.py:612
  12.1 11.8 %collective-permute-start.2 = (bf16[240,128]{1,0:T(8,128)(2,1)S(1)}, bf16[240,128]{1,0:T(8,128)(2,1)S(1)}, u32[]{:S(2)}, u32[]{:S(2)}) collective-permute-start(bf16[240,128]{1,0:T(8,128)(2,1)S(1)} %get-tuple-element.210), channel_id=1, source_target_pairs={{0,4},{4,0},{8,12},{12,8},{1,5},{5,1},{9,13},{13,9},{2,6},{6,2},{1... | collective-permute-start | bytes 184328 | tf_op jit(solution)/shard_map/ppermute | solution.py:495
  13.0 10.9 %collective-permute-start.4 = (bf16[240,128]{1,0:T(8,128)(2,1)S(1)}, bf16[240,128]{1,0:T(8,128)(2,1)S(1)}, u32[]{:S(2)}, u32[]{:S(2)}) collective-permute-start(bf16[240,128]{1,0:T(8,128)(2,1)S(1)} %add_convert_fusion.8), channel_id=1, source_target_pairs={{0,8},{4,12},{8,0},{12,4},{1,9},{5,13},{9,1},{13,5},{2,10},{6,14},... | collective-permute-start | bytes 184328 | tf_op jit(solution)/shard_map/ppermute | solution.py:495
  22.3 21.1 %collective-permute-start.1 = (bf16[480,384]{1,0:T(8,128)(2,1)}, bf16[480,384]{1,0:T(8,128)(2,1)S(1)}, u32[]{:S(2)}, u32[]{:S(2)}) collective-permute-start(bf16[480,384]{1,0:T(8,128)(2,1)} %get-tuple-element.93), channel_id=1, source_target_pairs={{0,0},{1,4},{2,8},{3,12},{4,2},{5,6},{6,10},{7,14},{8,1},{9,5},{10... | collective-permute-start | bytes 1105928 | tf_op jit(solution)/shard_map/ppermute | solution.py:547
  24.1 19.3 %collective-permute-start.5 = (bf16[240,640]{1,0:T(8,128)(2,1)S(1)}, bf16[240,640]{1,0:T(8,128)(2,1)S(1)}, u32[]{:S(2)}, u32[]{:S(2)}) collective-permute-start(bf16[240,640]{1,0:T(8,128)(2,1)S(1)} %pad_maximum_fusion.4), channel_id=1, source_target_pairs={{0,1},{1,2},{2,3},{3,0},{4,5},{5,6},{6,7},{7,4},{8,9},{9,10},{10,1... | collective-permute-start | bytes 921608 | tf_op jit(solution)/shard_map/ppermute | solution.py:526
  43.4 21.7 %collective-permute-start.6 = (bf16[480,384]{1,0:T(8,128)(2,1)}, bf16[480,384]{1,0:T(8,128)(2,1)S(1)}, u32[]{:S(2)}, u32[]{:S(2)}) collective-permute-start(bf16[480,384]{1,0:T(8,128)(2,1)} %get-tuple-element.96), channel_id=1, source_target_pairs={{0,4},{1,0},{2,12},{3,8},{4,6},{5,2},{6,14},{7,10},{8,5},{9,1},{10... | collective-permute-start | bytes 1105928 | tf_op jit(solution)/shard_map/ppermute | solution.py:547
  43.4 17.7 %collective-permute-start.7 = (bf16[240,640]{1,0:T(8,128)(2,1)S(1)}, bf16[240,640]{1,0:T(8,128)(2,1)}, u32[]{:S(2)}, u32[]{:S(2)}) collective-permute-start(bf16[240,640]{1,0:T(8,128)(2,1)S(1)} %collective-permute-done.5), channel_id=1, source_target_pairs={{0,1},{1,2},{2,3},{3,0},{4,5},{5,6},{6,7},{7,4},{8,9},{9,10},{10,1... | collective-permute-start | bytes 921608 | tf_op jit(solution)/shard_map/ppermute | solution.py:526
  65.1 9.2 %collective-permute-start.9 = (bf16[240,640]{1,0:T(8,128)(2,1)}, bf16[240,640]{1,0:T(8,128)(2,1)}, u32[]{:S(2)}, u32[]{:S(2)}) collective-permute-start(bf16[240,640]{1,0:T(8,128)(2,1)} %collective-permute-done.7), channel_id=1, source_target_pairs={{0,1},{1,2},{2,3},{3,0},{4,5},{5,6},{6,7},{7,4},{8,9},{9,10},{10,1... | collective-permute-start | bytes 921608 | tf_op jit(solution)/shard_map/ppermute | solution.py:526
  66.1 13.4 %collective-permute-start.12 = (bf16[240,640]{1,0:T(8,128)(2,1)S(1)}, bf16[240,640]{1,0:T(8,128)(2,1)}, u32[]{:S(2)}, u32[]{:S(2)}) collective-permute-start(bf16[240,640]{1,0:T(8,128)(2,1)S(1)} %pad_maximum_fusion.4), channel_id=1, source_target_pairs={{0,8},{4,12},{8,0},{12,4},{1,9},{5,13},{9,1},{13,5},{2,10},{6,14},... | collective-permute-start | bytes 921608 | tf_op jit(solution)/shard_map/ppermute | solution.py:495
  66.2 16.5 %collective-permute-start.8 = (bf16[480,384]{1,0:T(8,128)(2,1)}, bf16[480,384]{1,0:T(8,128)(2,1)S(1)}, u32[]{:S(2)}, u32[]{:S(2)}) collective-permute-start(bf16[480,384]{1,0:T(8,128)(2,1)} %get-tuple-element.99), channel_id=1, source_target_pairs={{0,8},{1,12},{2,0},{3,4},{4,10},{5,14},{6,2},{7,6},{8,9},{9,13},{1... | collective-permute-start | bytes 1105928 | tf_op jit(solution)/shard_map/ppermute | solution.py:547
  74.3 15.5 %collective-permute-start.10 = (bf16[480,384]{1,0:T(8,128)(2,1)}, bf16[480,384]{1,0:T(8,128)(2,1)S(1)}, u32[]{:S(2)}, u32[]{:S(2)}) collective-permute-start(bf16[480,384]{1,0:T(8,128)(2,1)} %get-tuple-element.102), channel_id=1, source_target_pairs={{0,12},{1,8},{2,4},{3,0},{4,14},{5,10},{6,6},{7,2},{8,13},{9,9},{1... | collective-permute-start | bytes 1105928 | tf_op jit(solution)/shard_map/ppermute | solution.py:547
  79.4 19.5 %collective-permute-start.13 = (bf16[240,640]{1,0:T(8,128)(2,1)S(1)}, bf16[240,640]{1,0:T(8,128)(2,1)}, u32[]{:S(2)}, u32[]{:S(2)}) collective-permute-start(bf16[240,640]{1,0:T(8,128)(2,1)S(1)} %copy-done.32), channel_id=1, source_target_pairs={{0,8},{4,12},{8,0},{12,4},{1,9},{5,13},{9,1},{13,5},{2,10},{6,14},... | collective-permute-start | bytes 921608 | tf_op jit(solution)/shard_map/ppermute | solution.py:495
  80.5 19.4 %collective-permute-start.14 = (bf16[240,640]{1,0:T(8,128)(2,1)}, bf16[240,640]{1,0:T(8,128)(2,1)}, u32[]{:S(2)}, u32[]{:S(2)}) collective-permute-start(bf16[240,640]{1,0:T(8,128)(2,1)} %collective-permute-done.7), channel_id=1, source_target_pairs={{0,8},{4,12},{8,0},{12,4},{1,9},{5,13},{9,1},{13,5},{2,10},{6,14},... | collective-permute-start | bytes 921608 | tf_op jit(solution)/shard_map/ppermute | solution.py:495
  89.8 95.1 %all-gather.5.cloned.1.call-start = ((), (), s32[]{:S(2)}) async-start(), calls=%async_computation.5 | async-start | bytes 1536000 | tf_op jit(solution)/shard_map/all_gather | solution.py:625
  90.9 17.8 %collective-permute-start.15 = (bf16[240,640]{1,0:T(8,128)(2,1)}, bf16[240,640]{1,0:T(8,128)(2,1)S(1)}, u32[]{:S(2)}, u32[]{:S(2)}) collective-permute-start(bf16[240,640]{1,0:T(8,128)(2,1)} %collective-permute-done.9), channel_id=1, source_target_pairs={{0,8},{4,12},{8,0},{12,4},{1,9},{5,13},{9,1},{13,5},{2,10},{6,14},... | collective-permute-start | bytes 921608 | tf_op jit(solution)/shard_map/ppermute | solution.py:495
  102.0 13.4 %collective-permute-start.11 = (bf16[960,640]{1,0:T(8,128)(2,1)S(1)}, bf16[960,640]{1,0:T(8,128)(2,1)}, u32[]{:S(2)}, u32[]{:S(2)}) collective-permute-start(bf16[960,640]{1,0:T(8,128)(2,1)S(1)} %constant_dynamic-update-slice_fusion.refs_4_), channel_id=1, source_target_pairs={{0,4},{4,0},{8,12},{12,8},{1,5},{5,1},{9,13},{13,9},{2,6},{6,2},{1... | collective-permute-start | bytes 3686408 | tf_op jit(solution)/shard_map/ppermute | solution.py:495
  108.7 6.7 %collective-permute-start.16 = (bf16[960,640]{1,0:T(8,128)(2,1)S(1)}, bf16[960,640]{1,0:T(8,128)(2,1)}, u32[]{:S(2)}, u32[]{:S(2)}) collective-permute-start(bf16[960,640]{1,0:T(8,128)(2,1)S(1)} %constant_dynamic-update-slice_fusion.4.refs_6_), channel_id=1, source_target_pairs={{0,4},{4,0},{8,12},{12,8},{1,5},{5,1},{9,13},{13,9},{2,6},{6,2},{1... | collective-permute-start | bytes 3686408 | tf_op jit(solution)/shard_map/ppermute | solution.py:495
  124.4 14.2 %collective-permute-start.18 = (bf16[5,128,384]{2,1,0:T(8,128)(2,1)}, bf16[5,128,384]{2,1,0:T(8,128)(2,1)}, u32[]{:S(2)}, u32[]{:S(2)}) collective-permute-start(bf16[5,128,384]{2,1,0:T(8,128)(2,1)} %get-tuple-element.106.kv0), channel_id=1, source_target_pairs={{0,8},{4,12},{8,0},{12,4},{1,9},{5,13},{9,1},{13,5},{2,10},{6,14},... | collective-permute-start | bytes 1474568 | tf_op jit(solution)/shard_map/ppermute | solution.py:495
  126.9 169.1 %reduce-scatter.5.cloned.1.call-start = ((), (), s32[]{:S(2)}) async-start(), calls=%async_computation.6 | async-start | bytes 2457600 | tf_op jit(solution)/shard_map/reduce_scatter | solution.py:688
  133.1 10.7 %collective-permute-start.17 = (bf16[5,128,384]{2,1,0:T(8,128)(2,1)}, bf16[5,128,384]{2,1,0:T(8,128)(2,1)}, u32[]{:S(2)}, u32[]{:S(2)}) collective-permute-start(bf16[5,128,384]{2,1,0:T(8,128)(2,1)} %get-tuple-element.106.kv0), channel_id=1, source_target_pairs={{0,4},{4,0},{8,12},{12,8},{1,5},{5,1},{9,13},{13,9},{2,6},{6,2},{1... | collective-permute-start | bytes 1474568 | tf_op jit(solution)/shard_map/ppermute | solution.py:495
  138.7 5.2 %collective-permute-start.19 = (bf16[5,128,384]{2,1,0:T(8,128)(2,1)}, bf16[5,128,384]{2,1,0:T(8,128)(2,1)}, u32[]{:S(2)}, u32[]{:S(2)}) collective-permute-start(bf16[5,128,384]{2,1,0:T(8,128)(2,1)} %collective-permute-done.18.kv2), channel_id=1, source_target_pairs={{0,4},{4,0},{8,12},{12,8},{1,5},{5,1},{9,13},{13,9},{2,6},{6,2},{1... | collective-permute-start | bytes 1474568 | tf_op jit(solution)/shard_map/ppermute | solution.py:495
  142.1 30.7 %collective-permute-start.23 = (bf16[960,384]{1,0:T(8,128)(2,1)S(1)}, bf16[960,384]{1,0:T(8,128)(2,1)}, u32[]{:S(2)}, u32[]{:S(2)}) collective-permute-start(bf16[960,384]{1,0:T(8,128)(2,1)S(1)} %copy-done), channel_id=1, source_target_pairs={{0,8},{4,12},{8,0},{12,4},{1,9},{5,13},{9,1},{13,5},{2,10},{6,14},... | collective-permute-start | bytes 2211848 | tf_op jit(solution)/shard_map/ppermute | solution.py:495
  159.2 25.7 %collective-permute-start.21 = (bf16[960,384]{1,0:T(8,128)(2,1)}, bf16[960,384]{1,0:T(8,128)(2,1)}, u32[]{:S(2)}, u32[]{:S(2)}) collective-permute-start(bf16[960,384]{1,0:T(8,128)(2,1)} %get-tuple-element.123.refs_3_.refs_0_), channel_id=1, source_target_pairs={{0,8},{4,12},{8,0},{12,4},{1,9},{5,13},{9,1},{13,5},{2,10},{6,14},... | collective-permute-start | bytes 2211848 | tf_op jit(solution)/shard_map/ppermute | solution.py:495
  172.8 30.4 %collective-permute-start.20 = (bf16[512,1280]{1,0:T(8,128)(2,1)S(1)}, bf16[512,1280]{1,0:T(8,128)(2,1)S(1)}, u32[]{:S(2)}, u32[]{:S(2)}) collective-permute-start(bf16[512,1280]{1,0:T(8,128)(2,1)S(1)} %copy-done.1), channel_id=1, source_target_pairs={{0,16},{16,0},{1,17},{17,1},{2,18},{18,2},{3,19},{19,3},{4,20},{20... | collective-permute-start | bytes 3932168 | tf_op jit(solution)/shard_map/ppermute | solution.py:614
  172.8 12.1 %collective-permute-start.24 = (bf16[960,384]{1,0:T(8,128)(2,1)}, bf16[960,384]{1,0:T(8,128)(2,1)}, u32[]{:S(2)}, u32[]{:S(2)}) collective-permute-start(bf16[960,384]{1,0:T(8,128)(2,1)} %collective-permute-done.23.refs_5_.refs_6_), channel_id=1, source_target_pairs={{0,4},{4,0},{8,12},{12,8},{1,5},{5,1},{9,13},{13,9},{2,6},{6,2},{1... | collective-permute-start | bytes 2211848 | tf_op jit(solution)/shard_map/ppermute | solution.py:495
  184.9 18.3 %collective-permute-start.22 = (bf16[960,384]{1,0:T(8,128)(2,1)}, bf16[960,384]{1,0:T(8,128)(2,1)}, u32[]{:S(2)}, u32[]{:S(2)}) collective-permute-start(bf16[960,384]{1,0:T(8,128)(2,1)} %collective-permute-done.21.refs_3_.refs_2_), channel_id=1, source_target_pairs={{0,4},{4,0},{8,12},{12,8},{1,5},{5,1},{9,13},{13,9},{2,6},{6,2},{1... | collective-permute-start | bytes 2211848 | tf_op jit(solution)/shard_map/ppermute | solution.py:495
  217.1 4.5 collective-permute-start.26
  221.2 18.6 %collective-permute-start.29 = (bf16[960,384]{1,0:T(8,128)(2,1)S(1)}, bf16[960,384]{1,0:T(8,128)(2,1)S(1)}, u32[]{:S(2)}, u32[]{:S(2)}) collective-permute-start(bf16[960,384]{1,0:T(8,128)(2,1)S(1)} %add_convert_fusion.3), channel_id=1, source_target_pairs={{0,8},{4,12},{8,0},{12,4},{1,9},{5,13},{9,1},{13,5},{2,10},{6,14},... | collective-permute-start | bytes 2211848 | tf_op jit(solution)/shard_map/ppermute | solution.py:495
  254.2 105.5 %reduce-scatter.11.cloned.1.call-start = ((), (), s32[]{:S(2)}) async-start(), calls=%async_computation.9 | async-start | bytes 2150400 | tf_op jit(solution)/shard_map/reduce_scatter | solution.py:688
  257.7 38.3 %collective-permute-start.32 = (bf16[960,384]{1,0:T(8,128)(2,1)S(1)}, bf16[960,384]{1,0:T(8,128)(2,1)S(1)}, u32[]{:S(2)}, u32[]{:S(2)}) collective-permute-start(bf16[960,384]{1,0:T(8,128)(2,1)S(1)} %add_convert_fusion.2), channel_id=1, source_target_pairs={{0,8},{4,12},{8,0},{12,4},{1,9},{5,13},{9,1},{13,5},{2,10},{6,14},... | collective-permute-start | bytes 2211848 | tf_op jit(solution)/shard_map/ppermute | solution.py:495
  287.7 9.7 %collective-permute-start.33 = (bf16[5,128,384]{2,1,0:T(8,128)(2,1)}, bf16[5,128,384]{2,1,0:T(8,128)(2,1)}, u32[]{:S(2)}, u32[]{:S(2)}) collective-permute-start(bf16[5,128,384]{2,1,0:T(8,128)(2,1)} %get-tuple-element.149), channel_id=1, source_target_pairs={{0,4},{4,0},{8,12},{12,8},{1,5},{5,1},{9,13},{13,9},{2,6},{6,2},{1... | collective-permute-start | bytes 1474568 | tf_op jit(solution)/shard_map/ppermute | solution.py:495
  295.6 12.3 %collective-permute-start.31 = (bf16[4,480,240]{2,1,0:T(8,128)(2,1)}, bf16[4,480,240]{2,1,0:T(8,128)(2,1)S(1)}, u32[]{:S(2)}, u32[]{:S(2)}) collective-permute-start(bf16[4,480,240]{2,1,0:T(8,128)(2,1)} %get-tuple-element.146), channel_id=1, source_target_pairs={{0,4},{4,0},{8,12},{12,8},{1,5},{5,1},{9,13},{13,9},{2,6},{6,2},{1... | collective-permute-start | bytes 2764808 | tf_op jit(solution)/shard_map/ppermute | solution.py:495
  295.7 86.8 %reduce-scatter.9.cloned.1.call-start = ((), (), s32[]{:S(2)}) async-start(), calls=%async_computation.8 | async-start | bytes 450560 | tf_op jit(solution)/shard_map/reduce_scatter | solution.py:719
  298.7 20.7 %collective-permute-start.34 = (bf16[5,128,384]{2,1,0:T(8,128)(2,1)S(1)}, bf16[5,128,384]{2,1,0:T(8,128)(2,1)S(1)}, u32[]{:S(2)}, u32[]{:S(2)}) collective-permute-start(bf16[5,128,384]{2,1,0:T(8,128)(2,1)S(1)} %add_convert_fusion.4), channel_id=1, source_target_pairs={{0,8},{4,12},{8,0},{12,4},{1,9},{5,13},{9,1},{13,5},{2,10},{6,14},... | collective-permute-start | bytes 1474568 | tf_op jit(solution)/shard_map/ppermute | solution.py:495
  307.9 36.0 %collective-permute-start.41 = (bf16[4,480,240]{2,1,0:T(8,128)(2,1)}, bf16[4,480,240]{2,1,0:T(8,128)(2,1)S(1)}, u32[]{:S(2)}, u32[]{:S(2)}) collective-permute-start(bf16[4,480,240]{2,1,0:T(8,128)(2,1)} %get-tuple-element.168), channel_id=1, source_target_pairs={{0,4},{4,0},{8,12},{12,8},{1,5},{5,1},{9,13},{13,9},{2,6},{6,2},{1... | collective-permute-start | bytes 2764808 | tf_op jit(solution)/shard_map/ppermute | solution.py:495
  319.4 24.5 %collective-permute-start.42 = (bf16[4,480,240]{2,1,0:T(8,128)(2,1)S(1)}, bf16[4,480,240]{2,1,0:T(8,128)(2,1)S(1)}, u32[]{:S(2)}, u32[]{:S(2)}) collective-permute-start(bf16[4,480,240]{2,1,0:T(8,128)(2,1)S(1)} %add_convert_fusion.1), channel_id=1, source_target_pairs={{0,8},{4,12},{8,0},{12,4},{1,9},{5,13},{9,1},{13,5},{2,10},{6,14},... | collective-permute-start | bytes 2764808 | tf_op jit(solution)/shard_map/ppermute | solution.py:495
  347.0 10.5 %collective-permute-start.45 = (bf16[4,176,240]{2,1,0:T(8,128)(2,1)S(1)}, bf16[4,176,240]{2,1,0:T(8,128)(2,1)S(1)}, u32[]{:S(2)}, u32[]{:S(2)}) collective-permute-start(bf16[4,176,240]{2,1,0:T(8,128)(2,1)S(1)} %add_convert_fusion.6), channel_id=1, source_target_pairs={{0,8},{4,12},{8,0},{12,4},{1,9},{5,13},{9,1},{13,5},{2,10},{6,14},... | collective-permute-start | bytes 1013768 | tf_op jit(solution)/shard_map/ppermute | solution.py:495
  358.4 63.1 %reduce-scatter.7.cloned.1.call-start = ((), (), s32[]{:S(2)}) async-start(), calls=%async_computation.7 | async-start | bytes 1228800 | tf_op jit(solution)/shard_map/reduce_scatter | solution.py:717
  359.0 7.0 %collective-permute-start.37 = (bf16[480,384]{1,0:T(8,128)(2,1)S(1)}, bf16[480,384]{1,0:T(8,128)(2,1)S(1)}, u32[]{:S(2)}, u32[]{:S(2)}) collective-permute-start(bf16[480,384]{1,0:T(8,128)(2,1)S(1)} %copy-done.43), channel_id=1, source_target_pairs={{0,0},{1,8},{2,4},{3,12},{4,1},{5,9},{6,5},{7,13},{8,2},{9,10},{10... | collective-permute-start | bytes 1105928 | tf_op jit(solution)/shard_map/ppermute | solution.py:554
  359.7 64.4 %collective-permute-start.51 = (bf16[240,896]{1,0:T(8,128)(2,1)}, bf16[240,896]{1,0:T(8,128)(2,1)S(1)}, u32[]{:S(2)}, u32[]{:S(2)}) collective-permute-start(bf16[240,896]{1,0:T(8,128)(2,1)} %reduce-scatter.11.cloned.1.call-done), channel_id=1, source_target_pairs={{0,16},{16,0},{1,17},{17,1},{2,18},{18,2},{3,19},{19,3},{4,20},{20... | collective-permute-start | bytes 1290248 | tf_op jit(solution)/shard_map/ppermute | solution.py:541
  360.1 62.4 %collective-permute-start.38 = (bf16[480,384]{1,0:T(8,128)(2,1)}, bf16[480,384]{1,0:T(8,128)(2,1)S(1)}, u32[]{:S(2)}, u32[]{:S(2)}) collective-permute-start(bf16[480,384]{1,0:T(8,128)(2,1)} %get-tuple-element.160), channel_id=1, source_target_pairs={{0,1},{1,9},{2,5},{3,13},{4,0},{5,8},{6,4},{7,12},{8,3},{9,11},{10... | collective-permute-start | bytes 1105928 | tf_op jit(solution)/shard_map/ppermute | solution.py:554
  363.4 59.2 %collective-permute-start.39 = (bf16[480,384]{1,0:T(8,128)(2,1)}, bf16[480,384]{1,0:T(8,128)(2,1)S(1)}, u32[]{:S(2)}, u32[]{:S(2)}) collective-permute-start(bf16[480,384]{1,0:T(8,128)(2,1)} %get-tuple-element.161), channel_id=1, source_target_pairs={{0,2},{1,10},{2,6},{3,14},{4,3},{5,11},{6,7},{7,15},{8,0},{9,8},{1... | collective-permute-start | bytes 1105928 | tf_op jit(solution)/shard_map/ppermute | solution.py:554
  363.4 59.2 %collective-permute-start.40 = (bf16[480,384]{1,0:T(8,128)(2,1)S(1)}, bf16[480,384]{1,0:T(8,128)(2,1)S(1)}, u32[]{:S(2)}, u32[]{:S(2)}) collective-permute-start(bf16[480,384]{1,0:T(8,128)(2,1)S(1)} %copy-done.42), channel_id=1, source_target_pairs={{0,3},{1,11},{2,7},{3,15},{4,2},{5,10},{6,6},{7,14},{8,1},{9,9},{1... | collective-permute-start | bytes 1105928 | tf_op jit(solution)/shard_map/ppermute | solution.py:554
  366.1 59.2 %collective-permute-start.50 = (bf16[240,1024]{1,0:T(8,128)(2,1)S(1)}, bf16[240,1024]{1,0:T(8,128)(2,1)S(1)}, u32[]{:S(2)}, u32[]{:S(2)}) collective-permute-start(bf16[240,1024]{1,0:T(8,128)(2,1)S(1)} %copy-done.20), channel_id=1, source_target_pairs={{0,16},{16,0},{1,17},{17,1},{2,18},{18,2},{3,19},{19,3},{4,20},{20... | collective-permute-start | bytes 1474568 | tf_op jit(solution)/shard_map/ppermute | solution.py:541
  422.6 9.5 %collective-permute-start.46 = (bf16[656,240]{1,0:T(8,128)(2,1)S(1)}, bf16[656,240]{1,0:T(8,128)(2,1)S(1)}, u32[]{:S(2)}, u32[]{:S(2)}) collective-permute-start(bf16[656,240]{1,0:T(8,128)(2,1)S(1)} %pad_maximum_fusion.3), channel_id=1, source_target_pairs={{0,16},{16,0},{1,17},{17,1},{2,18},{18,2},{3,19},{19,3},{4,20},{20... | collective-permute-start | bytes 944648 | tf_op jit(solution)/shard_map/ppermute | solution.py:541
  432.3 5.0 %collective-permute-start.48 = (f32[128,240]{1,0:T(8,128)S(1)}, f32[128,240]{1,0:T(8,128)S(1)}, u32[]{:S(2)}, u32[]{:S(2)}) collective-permute-start(f32[128,240]{1,0:T(8,128)S(1)} %pad_maximum_fusion.5.o0), channel_id=1, source_target_pairs={{0,8},{4,12},{8,0},{12,4},{1,9},{5,13},{9,1},{13,5},{2,10},{6,14},... | collective-permute-start | bytes 368648 | tf_op jit(solution)/shard_map/ppermute | solution.py:495
  434.8 7.5 %collective-permute-start.47 = (f32[128,240]{1,0:T(8,128)S(1)}, f32[128,240]{1,0:T(8,128)S(1)}, u32[]{:S(2)}, u32[]{:S(2)}) collective-permute-start(f32[128,240]{1,0:T(8,128)S(1)} %pad_maximum_fusion.5.o0), channel_id=1, source_target_pairs={{0,4},{4,0},{8,12},{12,8},{1,5},{5,1},{9,13},{13,9},{2,6},{6,2},{1... | collective-permute-start | bytes 368648 | tf_op jit(solution)/shard_map/ppermute | solution.py:495
  437.3 5.0 %collective-permute-start.49 = (f32[128,240]{1,0:T(8,128)S(1)}, f32[128,240]{1,0:T(8,128)S(1)}, u32[]{:S(2)}, u32[]{:S(2)}) collective-permute-start(f32[128,240]{1,0:T(8,128)S(1)} %collective-permute-done.48.o2), channel_id=1, source_target_pairs={{0,4},{4,0},{8,12},{12,8},{1,5},{5,1},{9,13},{13,9},{2,6},{6,2},{1... | collective-permute-start | bytes 368648 | tf_op jit(solution)/shard_map/ppermute | solution.py:495
  (57 other events, 537.8 us)
Sparse Core Ops, SparseCore 0:
  89.9 42.7 all-gather.2
  134.2 30.1 all-gather.4
  254.3 37.8 reduce-scatter.4
  295.8 42.6 reduce-scatter.10
  358.5 23.9 reduce-scatter.8
  385.4 36.0 reduce-scatter.6

commit v4 on v3

--- a/solution.py
+++ b/solution.py
@@ -365,12 +365,16 @@
     if halves:
         w = refs[-1]
         part = refs[0].shape[0] // ROWS
-        for h in range(2):
-            shift = (FB - part) * (sc[3] if h == 0 else 1 - sc[3])
-            for b in range(ROWS):
-                w[pl.ds(pl.multiple_of(b * FB + shift, 16), part)] = refs[h][b * part : (b + 1) * part]
-        wd = refs[2]
-        refs = refs[3:-1]
+        wd = refs[3]
+        width = wd.shape[1]
+        for b in range(ROWS):
+            rows = slice(b * part, (b + 1) * part)
+            mine = pl.ds(pl.multiple_of(b * FB + (FB - part) * sc[3], 16), part)
+            theirs = pl.ds(pl.multiple_of(b * FB + (FB - part) * (1 - sc[3]), 16), part)
+            w[mine] = refs[0][rows]
+            w[theirs, :width] = refs[1][rows]
+            w[theirs, width:] = refs[2][rows]
+        refs = refs[4:-1]
     else:
         w, wd = refs[:2]
         refs = refs[2:]
@@ -611,7 +615,7 @@
         w_gu = lax.dynamic_slice(w_gu, ((FB - 128) * idp, 0), (128, 2 * ff))
     w_gu = [lax.all_gather(after(w_gu, *toks), "gy", axis=0, tiled=True)]
     if halves:
-        w_gu.append(lax.ppermute(w_gu[0], "dp", [(0, 1), (1, 0)]))
+        w_gu += [lax.ppermute(w_gu[0][:, at : at + ff], "dp", [(0, 1), (1, 0)]) for at in (0, ff)]
     x, dy, n1, r1, gain_one, gain_two, w5, qs, kv = simple(
         qkv_kernel, "qkv",
         [
@@ -636,7 +640,7 @@
         ],
         [per_group(QW, CP), per_group(8, CP), whole(D, CP), whole(D, CP), whole(1, CP)],
         [pltpu.VMEM((8, CP), F32), pltpu.VMEM((8, CP), F32), pltpu.VMEM((QW, CP), F32)],
-        sc, after(qs, w_gu[0]), *kvs, bias, w5, x, gain_two,
+        sc, after(qs, *w_gu[:2]), *kvs, bias, w5, x, gain_two,
     )
 
     n2s = row_gather(n2)
@@ -714,10 +718,9 @@
     ).astype(BF)
     packs_b = list(packs_b)
     packs_b[3] = after(packs_b[3], g_a)
-    g_a = lax.psum_scatter(g_a.reshape(ROWS * AP, FB), "gy", scatter_dimension=0, tiled=True)
-    g_b = row_scatter(packs_b).reshape(ROWS * BP, FB)
-    g_b = lax.psum_scatter(g_b, "gy", scatter_dimension=0, tiled=True)
-    g_all = dp_sum(after(jnp.concatenate([g_a, g_b], axis=0), *back))
+    g_all = jnp.concatenate([g_a, row_scatter(packs_b)], axis=1).reshape(ROWS * (AP + BP), FB)
+    g_all = lax.psum_scatter(g_all, "gy", scatter_dimension=0, tiled=True)
+    g_all = dp_sum(after(g_all, *back))
     odds = jnp.concatenate([g_all[AW:AP], g_all[AP + KV : AP + KV + KV // ROWS]], axis=0)
     grad_qkv, grad_out, grad_gains = simple(
         grads_kernel, "grads",

time: 463 us -> 472 us (1.019)
  waiting for transfers between devices: 183 us -> 192 us
    reduce_scatter x2 -> x1, waiting for transfers between devices: 53.9 us -> 0.01 us  [per_device(): g_all = lax.psum_scatter(g_all, 'gy', scatter_dimension=0, tiled=True)]
    ppermute x4, waiting for transfers between devices: 0.01 us -> 39.1 us  [to_features(): back.append(lax.ppermute(pieces[k], ('gx', 'gy'), pairs))]
    ppermute x36, waiting for transfers between devices: 53.8 us -> 71.2 us  [swap(): return lax.ppermute(values, 'gx', [(i, i ^ bit) for i in range(ROWS)])]
    ppermute x36, starting transfers between devices: 64.7 us -> 53.1 us  [swap(): return lax.ppermute(values, 'gx', [(i, i ^ bit) for i in range(ROWS)])]
    ppermute x3, starting transfers between devices: 3.43 us -> 14.5 us  [dp_sum(): lax.ppermute(values, 'dp', [(0, 1), (1, 0)]).astype(F32)]
    ppermute x1 -> x2, starting transfers between devices: 0.01 us -> 7.89 us  [per_device(): lax.ppermute(w_gu[0][:, at:at + ff], 'dp', [(0, 1), (1, 0)])]
    unnamed x101 -> x111, local copies, waits for them, and re-layouts: 13.1 us -> 10 us
    ppermute x1 -> x2, waiting for transfers between devices: 18.3 us -> 21.3 us  [per_device(): lax.ppermute(w_gu[0][:, at:at + ff], 'dp', [(0, 1), (1, 0)])]
  transfers between devices with their start and end apart: 58 -> 58, of which waited for: 23 -> 30; matrix products, arithmetic and copies ran while one was open for 6% -> 6% of each run, Pallas kernels for 20% -> 20%
where the time goes in v4:
time: 472 us; the launch traced here: 464 us
  waiting for transfers between devices  192 us (41%)
  Pallas kernels  120 us (25%)
  starting transfers between devices  91.7 us (19%)
  local copies, waits for them, and re-layouts  20.7 us (4%)
  between operations  20.6 us (4%)
  other arithmetic  19.3 us (4%)
    ppermute x36, waiting for transfers between devices, swap(): return lax.ppermute(values, 'gx', [(i, i ^ bit) for i in range(ROWS)])  71.2 us
    pallas_call x3, Pallas kernels, grouped(): pl.pallas_call(kernel, grid_spec=pltpu.PrefetchScalarGridSpec(num_scalar_...  62.2 us
    pallas_call x7, Pallas kernels, simple(): pl.pallas_call(kernel, in_specs=specs, out_specs=[pl.BlockSpec(memory_spa...  58.1 us
    ppermute x36, starting transfers between devices, swap(): return lax.ppermute(values, 'gx', [(i, i ^ bit) for i in range(ROWS)])  53.1 us
    ppermute x3, waiting for transfers between devices, ring(): lax.ppermute(values, 'gy', [(i, (i + 1) % ROWS) for i in range(ROWS)])  42.7 us
    ppermute x4, waiting for transfers between devices, to_features(): back.append(lax.ppermute(pieces[k], ('gx', 'gy'), pairs))  39.1 us
    ppermute x2, waiting for transfers between devices, per_device(): lax.ppermute(w_gu[0][:, at:at + ff], 'dp', [(0, 1), (1, 0)])  21.3 us
    ppermute x3, starting transfers between devices, dp_sum(): lax.ppermute(values, 'dp', [(0, 1), (1, 0)]).astype(F32)  14.5 us
  transfers between devices with their start and end apart: 58, of which 30 were waited for; matrix products, arithmetic and copies ran while one was open for 6% of the time, Pallas kernels for 20%

profile of v4, /device:TPU:0, one launch (start us, length us, event | category | flops | bytes accessed | tf_op | source)
XLA Modules:
  0.0 464.2 jit_solution(9797879382497131096)
XLA Ops:
  13.0 2.9 collective-permute-start.4
  18.8 3.5 split.1
  26.1 17.3 %collective-permute-done.5 = bf16[240,640]{1,0:T(8,128)(2,1)S(1)} collective-permute-done((bf16[240,640]{1,0:T(8,128)(2,1)S(1)}, bf16[240,640]{1,0:T(8,128)(2,1)S(1)}, u32[]{:S(2)}, u32[]{:S(2)}) %collective-permute-start.5) | collective-permute-done | bytes 307232 | tf_op jit(solution)/shard_map/ppermute | solution.py:530
  43.4 2.2 collective-permute-start.7
  45.6 15.4 %collective-permute-done.7 = bf16[240,640]{1,0:T(8,128)(2,1)S(1)} collective-permute-done((bf16[240,640]{1,0:T(8,128)(2,1)S(1)}, bf16[240,640]{1,0:T(8,128)(2,1)S(1)}, u32[]{:S(2)}, u32[]{:S(2)}) %collective-permute-start.7) | collective-permute-done | bytes 307232 | tf_op jit(solution)/shard_map/ppermute | solution.py:530
  61.0 4.1 collective-permute-done.6.refs_1_
  66.0 10.0 %collective-permute-done.9 = bf16[240,640]{1,0:T(8,128)(2,1)S(1)} collective-permute-done((bf16[240,640]{1,0:T(8,128)(2,1)S(1)}, bf16[240,640]{1,0:T(8,128)(2,1)S(1)}, u32[]{:S(2)}, u32[]{:S(2)}) %collective-permute-start.9) | collective-permute-done | bytes 307232 | tf_op jit(solution)/shard_map/ppermute | solution.py:530
  81.8 6.9 %collective-permute-done.10.refs_3_ = bf16[480,384]{1,0:T(8,128)(2,1)S(1)} collective-permute-done((bf16[480,384]{1,0:T(8,128)(2,1)S(1)}, bf16[480,384]{1,0:T(8,128)(2,1)S(1)}, u32[]{:S(2)}, u32[]{:S(2)}) %collective-permute-start.10) | collective-permute-done | bytes 368672 | tf_op jit(solution)/shard_map/ppermute | solution.py:551
  89.4 8.6 %collective-permute-start.12 = (bf16[240,640]{1,0:T(8,128)(2,1)S(1)}, bf16[240,640]{1,0:T(8,128)(2,1)S(1)}, u32[]{:S(2)}, u32[]{:S(2)}) collective-permute-start(bf16[240,640]{1,0:T(8,128)(2,1)S(1)} %pad_maximum_fusion.4), channel_id=1, source_target_pairs={{0,8},{4,12},{8,0},{12,4},{1,9},{5,13},{9,1},{13,5},{2,10},{6,14},... | collective-permute-start | bytes 921608 | tf_op jit(solution)/shard_map/ppermute | solution.py:499
  98.1 8.0 %collective-permute-done.12 = bf16[240,640]{1,0:T(8,128)(2,1)S(1)} collective-permute-done((bf16[240,640]{1,0:T(8,128)(2,1)S(1)}, bf16[240,640]{1,0:T(8,128)(2,1)S(1)}, u32[]{:S(2)}, u32[]{:S(2)}) %collective-permute-start.12) | collective-permute-done | bytes 307232 | tf_op jit(solution)/shard_map/ppermute | solution.py:499
  106.2 2.1 collective-permute-start.14
  108.5 4.2 collective-permute-done.13
  112.8 6.5 %collective-permute-done.14 = bf16[240,640]{1,0:T(8,128)(2,1)S(1)} collective-permute-done((bf16[240,640]{1,0:T(8,128)(2,1)S(1)}, bf16[240,640]{1,0:T(8,128)(2,1)S(1)}, u32[]{:S(2)}, u32[]{:S(2)}) %collective-permute-start.14) | collective-permute-done | bytes 307232 | tf_op jit(solution)/shard_map/ppermute | solution.py:499
  119.5 5.3 %collective-permute-done.15 = bf16[240,640]{1,0:T(8,128)(2,1)S(1)} collective-permute-done((bf16[240,640]{1,0:T(8,128)(2,1)S(1)}, bf16[240,640]{1,0:T(8,128)(2,1)S(1)}, u32[]{:S(2)}, u32[]{:S(2)}) %collective-permute-start.15) | collective-permute-done | bytes 307232 | tf_op jit(solution)/shard_map/ppermute | solution.py:499
  127.2 2.5 select_add_fusion
  130.6 9.0 %qkv.1 = (bf16[960,384]{1,0:T(8,128)(2,1)}, bf16[960,384]{1,0:T(8,128)(2,1)}, bf16[960,384]{1,0:T(8,128)(2,1)}, f32[1,384]{1,0:T(1,128)}, f32[960,1]{1,0:T(8,128...) custom-call(s32[4]{0:T(128)} %pad_add_fusion.sc, ...), custom_call_target="tpu_custom_call" | custom-call | flops 700000000 | bytes 2100000 | tf_op jit(solution)/shard_map/qkv/pallas_call | solution.py:469
  147.3 2.5 fusion.11
  151.2 2.4 collective-permute-done.18.kv2
  156.2 2.8 pad_maximum_fusion.bias_ref
  160.7 6.1 %collective-permute-done.20.refs_1_ = bf16[512,640]{1,0:T(8,128)(2,1)S(1)} collective-permute-done((bf16[512,640]{1,0:T(8,128)(2,1)}, bf16[512,640]{1,0:T(8,128)(2,1)S(1)}, u32[]{:S(2)}, u32[]{:S(2)}) %collective-permute-start.20) | collective-permute-done | bytes 655392 | tf_op jit(solution)/shard_map/ppermute | solution.py:618
  166.8 14.9 %attend.1 = (bf16[5,192,384]{2,1,0:T(8,128)(2,1)}, f32[5,8,384]{2,1,0:T(8,128)}, f32[960,384]{1,0:T(8,128)}, bf16[960,384]{1,0:T(8,128)(2,1)}, f32[1,384]{1,0:T(1,128)}) custom-call(s32[8]{0:T(128)} %concatenate.28.sc, bf16[5,192,384]{2,1,0:T(8,128)(2,1)} %get-tuple-element.109.qs_ref, bf16[5,128,384]{2,1,0:T(8,128)(2,1)} %get-tuple-element.106.kv0, ...), custom_call_target="tpu_custom_call" | custom-call | flops 1800000000 | bytes 5400000 | tf_op jit(solution)/shard_map/attend/pallas_call | solution.py:482
  182.1 5.8 %collective-permute-start.25 = (bf16[960,384]{1,0:T(8,128)(2,1)S(1)}, bf16[960,384]{1,0:T(8,128)(2,1)}, u32[]{:S(2)}, u32[]{:S(2)}) collective-permute-start(bf16[960,384]{1,0:T(8,128)(2,1)S(1)} %collective-permute-done.24.refs_6_), channel_id=1, source_target_pairs={{0,4},{4,0},{8,12},{12,8},{1,5},{5,1},{9,13},{13,9},{2,6},{6,2},{1... | collective-permute-start | bytes 2211848 | tf_op jit(solution)/shard_map/ppermute | solution.py:499
  188.0 8.3 %collective-permute-done.22.refs_4_.refs_2_ = bf16[960,384]{1,0:T(8,128)(2,1)S(1)} collective-permute-done((bf16[960,384]{1,0:T(8,128)(2,1)}, bf16[960,384]{1,0:T(8,128)(2,1)S(1)}, u32[]{:S(2)}, u32[]{:S(2)}) %collective-permute-start.22) | collective-permute-done | bytes 737312 | tf_op jit(solution)/shard_map/ppermute | solution.py:499
  196.2 5.0 %collective-permute-start.23 = (bf16[960,384]{1,0:T(8,128)(2,1)S(1)}, bf16[960,384]{1,0:T(8,128)(2,1)}, u32[]{:S(2)}, u32[]{:S(2)}) collective-permute-start(bf16[960,384]{1,0:T(8,128)(2,1)S(1)} %collective-permute-done.22.refs_4_.refs_2_), channel_id=1, source_target_pairs={{0,4},{4,0},{8,12},{12,8},{1,5},{5,1},{9,13},{13,9},{2,6},{6,2},{1... | collective-permute-start | bytes 2211848 | tf_op jit(solution)/shard_map/ppermute | solution.py:499
  201.2 6.4 %collective-permute-start.21 = (bf16[512,640]{1,0:T(8,128)(2,1)}, bf16[512,640]{1,0:T(8,128)(2,1)}, u32[]{:S(2)}, u32[]{:S(2)}) collective-permute-start(bf16[512,640]{1,0:T(8,128)(2,1)} %get-tuple-element.203), channel_id=1, source_target_pairs={{0,16},{16,0},{1,17},{17,1},{2,18},{18,2},{3,19},{19,3},{4,20},{20... | collective-permute-start | bytes 1966088 | tf_op jit(solution)/shard_map/ppermute | solution.py:618
  207.6 15.3 %collective-permute-done.21.refs_2_ = bf16[512,640]{1,0:T(8,128)(2,1)} collective-permute-done((bf16[512,640]{1,0:T(8,128)(2,1)}, bf16[512,640]{1,0:T(8,128)(2,1)}, u32[]{:S(2)}, u32[]{:S(2)}) %collective-permute-start.21) | collective-permute-done | bytes 655392 | tf_op jit(solution)/shard_map/ppermute | solution.py:618
  222.9 12.8 %mlp_far.1 = (bf16[640,384]{1,0:T(8,128)(2,1)}, bf16[640,384]{1,0:T(8,128)(2,1)}, bf16[640,384]{1,0:T(8,128)(2,1)}, bf16[960,384]{1,0:T(8,128)(2,1)}, bf16[960,3...) custom-call(s32[4]{0:T(128)} %pad_add_fusion.sc, ...), custom_call_target="tpu_custom_call" | custom-call | flops 1300000000 | bytes 3900000 | tf_op jit(solution)/shard_map/mlp_far/pallas_call | solution.py:469
  236.4 2.1 collective-permute-done.29
  243.7 13.2 %mlp_near.1 = (bf16[640,384]{1,0:T(8,128)(2,1)}, bf16[640,384]{1,0:T(8,128)(2,1)}, bf16[640,384]{1,0:T(8,128)(2,1)}, bf16[960,384]{1,0:T(8,128)(2,1)}, bf16[960,...) custom-call(s32[4]{0:T(128)} %pad_add_fusion.sc, ...), custom_call_target="tpu_custom_call" | custom-call | flops 1300000000 | bytes 3900000 | tf_op jit(solution)/shard_map/mlp_near/pallas_call | solution.py:469
  258.7 14.4 %mlp_grad.1 = (bf16[960,1024]{1,0:T(8,128)(2,1)}, bf16[960,896]{1,0:T(8,128)(2,1)}) custom-call(bf16[960,384]{1,0:T(8,128)(2,1)} %get-tuple-element.123.refs_4_.refs_0_, bf16[960,384]{1,0:T(8,128)(2,1)} %copy-done.6, bf16[960,384]{1,0:T(8,128)(2,1)} %copy-done.4, bf16[960,384]{1,0:T(8,128)(2,1)} %collective-permute-done.23.refs_5_.refs_3_, ...), custom_call_target="tpu_custom_call" | custom-call | flops 1800000000 | bytes 5400000 | tf_op jit(solution)/shard_map/mlp_grad/pallas_call | solution.py:469
  274.7 2.7 collective-permute-done.31
  280.3 28.2 %attend_back.1 = (bf16[5,192,384]{2,1,0:T(8,128)(2,1)}, f32[5,128,384]{2,1,0:T(8,128)}, bf16[5,128,384]{2,1,0:T(8,128)(2,1)}, bf16[5,128,384]{2,1,0:T(8,128)(2,1...) custom-call(s32[8]{0:T(128)} %concatenate.28.sc, ...), custom_call_target="tpu_custom_call" | custom-call | flops 3000000000 | bytes 9000000 | tf_op jit(solution)/shard_map/attend_back/pallas_call | solution.py:482
  308.6 7.6 %collective-permute-start.34 = (bf16[5,128,384]{2,1,0:T(8,128)(2,1)}, bf16[5,128,384]{2,1,0:T(8,128)(2,1)}, u32[]{:S(2)}, u32[]{:S(2)}) collective-permute-start(bf16[5,128,384]{2,1,0:T(8,128)(2,1)} %get-tuple-element.149), channel_id=1, source_target_pairs={{0,4},{4,0},{8,12},{12,8},{1,5},{5,1},{9,13},{13,9},{2,6},{6,2},{1... | collective-permute-start | bytes 1474568 | tf_op jit(solution)/shard_map/ppermute | solution.py:499
  320.1 12.8 %collective-permute-done.35.d2 = bf16[5,128,384]{2,1,0:T(8,128)(2,1)S(1)} collective-permute-done((bf16[5,128,384]{2,1,0:T(8,128)(2,1)S(1)}, bf16[5,128,384]{2,1,0:T(8,128)(2,1)S(1)}, u32[]{:S(2)}, u32[]{:S(2)}) %collective-permute-start.35) | collective-permute-done | bytes 491552 | tf_op jit(solution)/shard_map/ppermute | solution.py:499
  336.9 19.1 %final.1 = (bf16[4,176,240]{2,1,0:T(8,128)(2,1)}, bf16[4,176,240]{2,1,0:T(8,128)(2,1)}, bf16[4,176,240]{2,1,0:T(8,128)(2,1)}, bf16[4,176,240]{2,1,0:T(8,128)(2,1...) custom-call(s32[8]{0:T(128)} %concatenate.28.sc, ...), custom_call_target="tpu_custom_call" | custom-call | flops 1900000000 | bytes 5700000 | tf_op jit(solution)/shard_map/final/pallas_call | solution.py:482
  360.5 8.7 %collective-permute-done.46 = bf16[4,176,240]{2,1,0:T(8,128)(2,1)S(1)} collective-permute-done((bf16[4,176,240]{2,1,0:T(8,128)(2,1)S(1)}, bf16[4,176,240]{2,1,0:T(8,128)(2,1)S(1)}, u32[]{:S(2)}, u32[]{:S(2)}) %collective-permute-start.46) | collective-permute-done | bytes 337952 | tf_op jit(solution)/shard_map/ppermute | solution.py:499
  372.4 9.4 %collective-permute-start.52 = (bf16[240,896]{1,0:T(8,128)(2,1)}, bf16[240,896]{1,0:T(8,128)(2,1)S(1)}, u32[]{:S(2)}, u32[]{:S(2)}) collective-permute-start(bf16[240,896]{1,0:T(8,128)(2,1)} %reduce-scatter.8.cloned.1.call-done), channel_id=1, source_target_pairs={{0,16},{16,0},{1,17},{17,1},{2,18},{18,2},{3,19},{19,3},{4,20},{20... | collective-permute-start | bytes 1290248 | tf_op jit(solution)/shard_map/ppermute | solution.py:545
  381.8 3.0 collective-permute-start.39
  384.9 2.6 collective-permute-start.41
  387.7 14.3 %collective-permute-done.39.refs_1_ = bf16[480,384]{1,0:T(8,128)(2,1)S(1)} collective-permute-done((bf16[480,384]{1,0:T(8,128)(2,1)}, bf16[480,384]{1,0:T(8,128)(2,1)S(1)}, u32[]{:S(2)}, u32[]{:S(2)}) %collective-permute-start.39) | collective-permute-done | bytes 368672 | tf_op jit(solution)/shard_map/ppermute | solution.py:558
  401.9 15.8 %collective-permute-done.40.refs_2_ = bf16[480,384]{1,0:T(8,128)(2,1)S(1)} collective-permute-done((bf16[480,384]{1,0:T(8,128)(2,1)}, bf16[480,384]{1,0:T(8,128)(2,1)S(1)}, u32[]{:S(2)}, u32[]{:S(2)}) %collective-permute-start.40) | collective-permute-done | bytes 368672 | tf_op jit(solution)/shard_map/ppermute | solution.py:558
  417.7 9.1 %collective-permute-done.41.refs_3_ = bf16[480,384]{1,0:T(8,128)(2,1)S(1)} collective-permute-done((bf16[480,384]{1,0:T(8,128)(2,1)S(1)}, bf16[480,384]{1,0:T(8,128)(2,1)S(1)}, u32[]{:S(2)}, u32[]{:S(2)}) %collective-permute-start.41) | collective-permute-done | bytes 368672 | tf_op jit(solution)/shard_map/ppermute | solution.py:558
  426.8 4.9 %collective-permute-start.47 = (bf16[656,240]{1,0:T(8,128)(2,1)}, bf16[656,240]{1,0:T(8,128)(2,1)S(1)}, u32[]{:S(2)}, u32[]{:S(2)}) collective-permute-start(bf16[656,240]{1,0:T(8,128)(2,1)} %reduce-scatter.6.cloned.1.call-done), channel_id=1, source_target_pairs={{0,16},{16,0},{1,17},{17,1},{2,18},{18,2},{3,19},{19,3},{4,20},{20... | collective-permute-start | bytes 944648 | tf_op jit(solution)/shard_map/ppermute | solution.py:545
  433.0 4.0 collective-permute-done.47
  437.2 6.5 %collective-permute-start.49 = (f32[128,240]{1,0:T(8,128)S(1)}, f32[128,240]{1,0:T(8,128)S(1)}, u32[]{:S(2)}, u32[]{:S(2)}) collective-permute-start(f32[128,240]{1,0:T(8,128)S(1)} %pad_maximum_fusion.5.o0), channel_id=1, source_target_pairs={{0,8},{4,12},{8,0},{12,4},{1,9},{5,13},{9,1},{13,5},{2,10},{6,14},... | collective-permute-start | bytes 368648 | tf_op jit(solution)/shard_map/ppermute | solution.py:499
  444.8 2.2 collective-permute-done.49.o2
  449.7 2.7 merge.1
  453.6 2.5 grads.1
  (246 shorter events, 66.9 us)
Async XLA Ops:
  7.2 140.1 %all-gather.3.cloned.1.call-start = ((), (), s32[]{:S(2)}) async-start(), calls=%async_computation.3 | async-start | bytes 1638400 | tf_op jit(solution)/shard_map/all_gather | solution.py:616
  12.1 11.8 %collective-permute-start.2 = (bf16[240,128]{1,0:T(8,128)(2,1)S(1)}, bf16[240,128]{1,0:T(8,128)(2,1)S(1)}, u32[]{:S(2)}, u32[]{:S(2)}) collective-permute-start(bf16[240,128]{1,0:T(8,128)(2,1)S(1)} %get-tuple-element.212), channel_id=1, source_target_pairs={{0,4},{4,0},{8,12},{12,8},{1,5},{5,1},{9,13},{13,9},{2,6},{6,2},{1... | collective-permute-start | bytes 184328 | tf_op jit(solution)/shard_map/ppermute | solution.py:499
  13.0 10.9 %collective-permute-start.4 = (bf16[240,128]{1,0:T(8,128)(2,1)S(1)}, bf16[240,128]{1,0:T(8,128)(2,1)S(1)}, u32[]{:S(2)}, u32[]{:S(2)}) collective-permute-start(bf16[240,128]{1,0:T(8,128)(2,1)S(1)} %add_convert_fusion.8), channel_id=1, source_target_pairs={{0,8},{4,12},{8,0},{12,4},{1,9},{5,13},{9,1},{13,5},{2,10},{6,14},... | collective-permute-start | bytes 184328 | tf_op jit(solution)/shard_map/ppermute | solution.py:499
  22.3 21.1 %collective-permute-start.1 = (bf16[480,384]{1,0:T(8,128)(2,1)}, bf16[480,384]{1,0:T(8,128)(2,1)S(1)}, u32[]{:S(2)}, u32[]{:S(2)}) collective-permute-start(bf16[480,384]{1,0:T(8,128)(2,1)} %get-tuple-element.93), channel_id=1, source_target_pairs={{0,0},{1,4},{2,8},{3,12},{4,2},{5,6},{6,10},{7,14},{8,1},{9,5},{10... | collective-permute-start | bytes 1105928 | tf_op jit(solution)/shard_map/ppermute | solution.py:551
  24.1 19.3 %collective-permute-start.5 = (bf16[240,640]{1,0:T(8,128)(2,1)S(1)}, bf16[240,640]{1,0:T(8,128)(2,1)S(1)}, u32[]{:S(2)}, u32[]{:S(2)}) collective-permute-start(bf16[240,640]{1,0:T(8,128)(2,1)S(1)} %pad_maximum_fusion.4), channel_id=1, source_target_pairs={{0,1},{1,2},{2,3},{3,0},{4,5},{5,6},{6,7},{7,4},{8,9},{9,10},{10,1... | collective-permute-start | bytes 921608 | tf_op jit(solution)/shard_map/ppermute | solution.py:530
  43.4 21.7 %collective-permute-start.6 = (bf16[480,384]{1,0:T(8,128)(2,1)}, bf16[480,384]{1,0:T(8,128)(2,1)S(1)}, u32[]{:S(2)}, u32[]{:S(2)}) collective-permute-start(bf16[480,384]{1,0:T(8,128)(2,1)} %get-tuple-element.96), channel_id=1, source_target_pairs={{0,4},{1,0},{2,12},{3,8},{4,6},{5,2},{6,14},{7,10},{8,5},{9,1},{10... | collective-permute-start | bytes 1105928 | tf_op jit(solution)/shard_map/ppermute | solution.py:551
  43.4 17.6 %collective-permute-start.7 = (bf16[240,640]{1,0:T(8,128)(2,1)S(1)}, bf16[240,640]{1,0:T(8,128)(2,1)S(1)}, u32[]{:S(2)}, u32[]{:S(2)}) collective-permute-start(bf16[240,640]{1,0:T(8,128)(2,1)S(1)} %collective-permute-done.5), channel_id=1, source_target_pairs={{0,1},{1,2},{2,3},{3,0},{4,5},{5,6},{6,7},{7,4},{8,9},{9,10},{10,1... | collective-permute-start | bytes 921608 | tf_op jit(solution)/shard_map/ppermute | solution.py:530
  65.1 11.0 %collective-permute-start.9 = (bf16[240,640]{1,0:T(8,128)(2,1)S(1)}, bf16[240,640]{1,0:T(8,128)(2,1)S(1)}, u32[]{:S(2)}, u32[]{:S(2)}) collective-permute-start(bf16[240,640]{1,0:T(8,128)(2,1)S(1)} %collective-permute-done.7), channel_id=1, source_target_pairs={{0,1},{1,2},{2,3},{3,0},{4,5},{5,6},{6,7},{7,4},{8,9},{9,10},{10,1... | collective-permute-start | bytes 921608 | tf_op jit(solution)/shard_map/ppermute | solution.py:530
  66.0 15.8 %collective-permute-start.8 = (bf16[480,384]{1,0:T(8,128)(2,1)S(1)}, bf16[480,384]{1,0:T(8,128)(2,1)S(1)}, u32[]{:S(2)}, u32[]{:S(2)}) collective-permute-start(bf16[480,384]{1,0:T(8,128)(2,1)S(1)} %copy-done.47), channel_id=1, source_target_pairs={{0,8},{1,12},{2,0},{3,4},{4,10},{5,14},{6,2},{7,6},{8,9},{9,13},{1... | collective-permute-start | bytes 1105928 | tf_op jit(solution)/shard_map/ppermute | solution.py:551
  76.8 11.9 %collective-permute-start.10 = (bf16[480,384]{1,0:T(8,128)(2,1)S(1)}, bf16[480,384]{1,0:T(8,128)(2,1)S(1)}, u32[]{:S(2)}, u32[]{:S(2)}) collective-permute-start(bf16[480,384]{1,0:T(8,128)(2,1)S(1)} %copy-done.46), channel_id=1, source_target_pairs={{0,12},{1,8},{2,4},{3,0},{4,14},{5,10},{6,6},{7,2},{8,13},{9,9},{1... | collective-permute-start | bytes 1105928 | tf_op jit(solution)/shard_map/ppermute | solution.py:551
  88.7 118.9 %all-gather.5.cloned.1.call-start = ((), (), s32[]{:S(2)}) async-start(), calls=%async_computation.4 | async-start | bytes 1536000 | tf_op jit(solution)/shard_map/all_gather | solution.py:629
  89.4 16.7 %collective-permute-start.12 = (bf16[240,640]{1,0:T(8,128)(2,1)S(1)}, bf16[240,640]{1,0:T(8,128)(2,1)S(1)}, u32[]{:S(2)}, u32[]{:S(2)}) collective-permute-start(bf16[240,640]{1,0:T(8,128)(2,1)S(1)} %pad_maximum_fusion.4), channel_id=1, source_target_pairs={{0,8},{4,12},{8,0},{12,4},{1,9},{5,13},{9,1},{13,5},{2,10},{6,14},... | collective-permute-start | bytes 921608 | tf_op jit(solution)/shard_map/ppermute | solution.py:499
  98.0 14.7 %collective-permute-start.13 = (bf16[240,640]{1,0:T(8,128)(2,1)S(1)}, bf16[240,640]{1,0:T(8,128)(2,1)S(1)}, u32[]{:S(2)}, u32[]{:S(2)}) collective-permute-start(bf16[240,640]{1,0:T(8,128)(2,1)S(1)} %collective-permute-done.5), channel_id=1, source_target_pairs={{0,8},{4,12},{8,0},{12,4},{1,9},{5,13},{9,1},{13,5},{2,10},{6,14},... | collective-permute-start | bytes 921608 | tf_op jit(solution)/shard_map/ppermute | solution.py:499
  106.2 13.1 %collective-permute-start.14 = (bf16[240,640]{1,0:T(8,128)(2,1)S(1)}, bf16[240,640]{1,0:T(8,128)(2,1)S(1)}, u32[]{:S(2)}, u32[]{:S(2)}) collective-permute-start(bf16[240,640]{1,0:T(8,128)(2,1)S(1)} %copy-done.36), channel_id=1, source_target_pairs={{0,8},{4,12},{8,0},{12,4},{1,9},{5,13},{9,1},{13,5},{2,10},{6,14},... | collective-permute-start | bytes 921608 | tf_op jit(solution)/shard_map/ppermute | solution.py:499
  108.4 16.4 %collective-permute-start.15 = (bf16[240,640]{1,0:T(8,128)(2,1)S(1)}, bf16[240,640]{1,0:T(8,128)(2,1)S(1)}, u32[]{:S(2)}, u32[]{:S(2)}) collective-permute-start(bf16[240,640]{1,0:T(8,128)(2,1)S(1)} %copy-done.34), channel_id=1, source_target_pairs={{0,8},{4,12},{8,0},{12,4},{1,9},{5,13},{9,1},{13,5},{2,10},{6,14},... | collective-permute-start | bytes 921608 | tf_op jit(solution)/shard_map/ppermute | solution.py:499
  119.4 11.2 %collective-permute-start.11 = (bf16[960,640]{1,0:T(8,128)(2,1)S(1)}, bf16[960,640]{1,0:T(8,128)(2,1)}, u32[]{:S(2)}, u32[]{:S(2)}) collective-permute-start(bf16[960,640]{1,0:T(8,128)(2,1)S(1)} %constant_dynamic-update-slice_fusion.refs_4_), channel_id=1, source_target_pairs={{0,4},{4,0},{8,12},{12,8},{1,5},{5,1},{9,13},{13,9},{2,6},{6,2},{1... | collective-permute-start | bytes 3686408 | tf_op jit(solution)/shard_map/ppermute | solution.py:499
  124.9 5.8 %collective-permute-start.16 = (bf16[960,640]{1,0:T(8,128)(2,1)S(1)}, bf16[960,640]{1,0:T(8,128)(2,1)}, u32[]{:S(2)}, u32[]{:S(2)}) collective-permute-start(bf16[960,640]{1,0:T(8,128)(2,1)S(1)} %constant_dynamic-update-slice_fusion.4.refs_6_), channel_id=1, source_target_pairs={{0,4},{4,0},{8,12},{12,8},{1,5},{5,1},{9,13},{13,9},{2,6},{6,2},{1... | collective-permute-start | bytes 3686408 | tf_op jit(solution)/shard_map/ppermute | solution.py:499
  125.6 190.9 %reduce-scatter.4.cloned.1.call-start = ((), (), s32[]{:S(2)}) async-start(), calls=%async_computation.5 | async-start | bytes 2457600 | tf_op jit(solution)/shard_map/reduce_scatter | solution.py:692
  139.7 13.9 %collective-permute-start.18 = (bf16[5,128,384]{2,1,0:T(8,128)(2,1)}, bf16[5,128,384]{2,1,0:T(8,128)(2,1)}, u32[]{:S(2)}, u32[]{:S(2)}) collective-permute-start(bf16[5,128,384]{2,1,0:T(8,128)(2,1)} %get-tuple-element.106.kv0), channel_id=1, source_target_pairs={{0,8},{4,12},{8,0},{12,4},{1,9},{5,13},{9,1},{13,5},{2,10},{6,14},... | collective-permute-start | bytes 1474568 | tf_op jit(solution)/shard_map/ppermute | solution.py:499
  149.7 17.1 %collective-permute-start.20 = (bf16[512,640]{1,0:T(8,128)(2,1)}, bf16[512,640]{1,0:T(8,128)(2,1)S(1)}, u32[]{:S(2)}, u32[]{:S(2)}) collective-permute-start(bf16[512,640]{1,0:T(8,128)(2,1)} %get-tuple-element.204), channel_id=1, source_target_pairs={{0,16},{16,0},{1,17},{17,1},{2,18},{18,2},{3,19},{19,3},{4,20},{20... | collective-permute-start | bytes 1966088 | tf_op jit(solution)/shard_map/ppermute | solution.py:618
  151.2 15.6 %collective-permute-start.17 = (bf16[5,128,384]{2,1,0:T(8,128)(2,1)}, bf16[5,128,384]{2,1,0:T(8,128)(2,1)}, u32[]{:S(2)}, u32[]{:S(2)}) collective-permute-start(bf16[5,128,384]{2,1,0:T(8,128)(2,1)} %get-tuple-element.106.kv0), channel_id=1, source_target_pairs={{0,4},{4,0},{8,12},{12,8},{1,5},{5,1},{9,13},{13,9},{2,6},{6,2},{1... | collective-permute-start | bytes 1474568 | tf_op jit(solution)/shard_map/ppermute | solution.py:499
  153.6 13.2 %collective-permute-start.19 = (bf16[5,128,384]{2,1,0:T(8,128)(2,1)}, bf16[5,128,384]{2,1,0:T(8,128)(2,1)}, u32[]{:S(2)}, u32[]{:S(2)}) collective-permute-start(bf16[5,128,384]{2,1,0:T(8,128)(2,1)} %collective-permute-done.18.kv2), channel_id=1, source_target_pairs={{0,4},{4,0},{8,12},{12,8},{1,5},{5,1},{9,13},{13,9},{2,6},{6,2},{1... | collective-permute-start | bytes 1474568 | tf_op jit(solution)/shard_map/ppermute | solution.py:499
  159.0 23.1 %collective-permute-start.24 = (bf16[960,384]{1,0:T(8,128)(2,1)S(1)}, bf16[960,384]{1,0:T(8,128)(2,1)S(1)}, u32[]{:S(2)}, u32[]{:S(2)}) collective-permute-start(bf16[960,384]{1,0:T(8,128)(2,1)S(1)} %copy-done), channel_id=1, source_target_pairs={{0,8},{4,12},{8,0},{12,4},{1,9},{5,13},{9,1},{13,5},{2,10},{6,14},... | collective-permute-start | bytes 2211848 | tf_op jit(solution)/shard_map/ppermute | solution.py:499
  181.8 14.5 %collective-permute-start.22 = (bf16[960,384]{1,0:T(8,128)(2,1)}, bf16[960,384]{1,0:T(8,128)(2,1)S(1)}, u32[]{:S(2)}, u32[]{:S(2)}) collective-permute-start(bf16[960,384]{1,0:T(8,128)(2,1)} %get-tuple-element.123.refs_4_.refs_0_), channel_id=1, source_target_pairs={{0,8},{4,12},{8,0},{12,4},{1,9},{5,13},{9,1},{13,5},{2,10},{6,14},... | collective-permute-start | bytes 2211848 | tf_op jit(solution)/shard_map/ppermute | solution.py:499
  182.1 40.8 %collective-permute-start.25 = (bf16[960,384]{1,0:T(8,128)(2,1)S(1)}, bf16[960,384]{1,0:T(8,128)(2,1)}, u32[]{:S(2)}, u32[]{:S(2)}) collective-permute-start(bf16[960,384]{1,0:T(8,128)(2,1)S(1)} %collective-permute-done.24.refs_6_), channel_id=1, source_target_pairs={{0,4},{4,0},{8,12},{12,8},{1,5},{5,1},{9,13},{13,9},{2,6},{6,2},{1... | collective-permute-start | bytes 2211848 | tf_op jit(solution)/shard_map/ppermute | solution.py:499
  196.2 26.7 %collective-permute-start.23 = (bf16[960,384]{1,0:T(8,128)(2,1)S(1)}, bf16[960,384]{1,0:T(8,128)(2,1)}, u32[]{:S(2)}, u32[]{:S(2)}) collective-permute-start(bf16[960,384]{1,0:T(8,128)(2,1)S(1)} %collective-permute-done.22.refs_4_.refs_2_), channel_id=1, source_target_pairs={{0,4},{4,0},{8,12},{12,8},{1,5},{5,1},{9,13},{13,9},{2,6},{6,2},{1... | collective-permute-start | bytes 2211848 | tf_op jit(solution)/shard_map/ppermute | solution.py:499
  201.2 21.7 %collective-permute-start.21 = (bf16[512,640]{1,0:T(8,128)(2,1)}, bf16[512,640]{1,0:T(8,128)(2,1)}, u32[]{:S(2)}, u32[]{:S(2)}) collective-permute-start(bf16[512,640]{1,0:T(8,128)(2,1)} %get-tuple-element.203), channel_id=1, source_target_pairs={{0,16},{16,0},{1,17},{17,1},{2,18},{18,2},{3,19},{19,3},{4,20},{20... | collective-permute-start | bytes 1966088 | tf_op jit(solution)/shard_map/ppermute | solution.py:618
  235.8 6.1 %collective-permute-start.27 = (bf16[960,384]{1,0:T(8,128)(2,1)S(1)}, bf16[960,384]{1,0:T(8,128)(2,1)S(1)}, u32[]{:S(2)}, u32[]{:S(2)}) collective-permute-start(bf16[960,384]{1,0:T(8,128)(2,1)S(1)} %copy-done), channel_id=1, source_target_pairs={{0,4},{4,0},{8,12},{12,8},{1,5},{5,1},{9,13},{13,9},{2,6},{6,2},{1... | collective-permute-start | bytes 2211848 | tf_op jit(solution)/shard_map/ppermute | solution.py:499
  236.3 5.6 %collective-permute-start.26 = (bf16[960,384]{1,0:T(8,128)(2,1)S(1)}, bf16[960,384]{1,0:T(8,128)(2,1)S(1)}, u32[]{:S(2)}, u32[]{:S(2)}) collective-permute-start(bf16[960,384]{1,0:T(8,128)(2,1)S(1)} %copy-done.3), channel_id=1, source_target_pairs={{0,4},{4,0},{8,12},{12,8},{1,5},{5,1},{9,13},{13,9},{2,6},{6,2},{1... | collective-permute-start | bytes 2211848 | tf_op jit(solution)/shard_map/ppermute | solution.py:499
  239.8 18.9 %collective-permute-start.30 = (bf16[960,384]{1,0:T(8,128)(2,1)S(1)}, bf16[960,384]{1,0:T(8,128)(2,1)S(1)}, u32[]{:S(2)}, u32[]{:S(2)}) collective-permute-start(bf16[960,384]{1,0:T(8,128)(2,1)S(1)} %add_convert_fusion.3), channel_id=1, source_target_pairs={{0,8},{4,12},{8,0},{12,4},{1,9},{5,13},{9,1},{13,5},{2,10},{6,14},... | collective-permute-start | bytes 2211848 | tf_op jit(solution)/shard_map/ppermute | solution.py:499
  273.1 99.2 %reduce-scatter.8.cloned.1.call-start = ((), (), s32[]{:S(2)}) async-start(), calls=%async_computation.7 | async-start | bytes 2150400 | tf_op jit(solution)/shard_map/reduce_scatter | solution.py:692
  277.6 38.9 %collective-permute-start.33 = (bf16[960,384]{1,0:T(8,128)(2,1)S(1)}, bf16[960,384]{1,0:T(8,128)(2,1)S(1)}, u32[]{:S(2)}, u32[]{:S(2)}) collective-permute-start(bf16[960,384]{1,0:T(8,128)(2,1)S(1)} %add_convert_fusion.2), channel_id=1, source_target_pairs={{0,8},{4,12},{8,0},{12,4},{1,9},{5,13},{9,1},{13,5},{2,10},{6,14},... | collective-permute-start | bytes 2211848 | tf_op jit(solution)/shard_map/ppermute | solution.py:499
  308.6 9.5 %collective-permute-start.34 = (bf16[5,128,384]{2,1,0:T(8,128)(2,1)}, bf16[5,128,384]{2,1,0:T(8,128)(2,1)}, u32[]{:S(2)}, u32[]{:S(2)}) collective-permute-start(bf16[5,128,384]{2,1,0:T(8,128)(2,1)} %get-tuple-element.149), channel_id=1, source_target_pairs={{0,4},{4,0},{8,12},{12,8},{1,5},{5,1},{9,13},{13,9},{2,6},{6,2},{1... | collective-permute-start | bytes 1474568 | tf_op jit(solution)/shard_map/ppermute | solution.py:499
  316.3 110.5 %reduce-scatter.6.cloned.1.call-start = ((), (), s32[]{:S(2)}) async-start(), calls=%async_computation.6 | async-start | bytes 1679360 | tf_op jit(solution)/shard_map/reduce_scatter | solution.py:722
  319.3 13.6 %collective-permute-start.35 = (bf16[5,128,384]{2,1,0:T(8,128)(2,1)S(1)}, bf16[5,128,384]{2,1,0:T(8,128)(2,1)S(1)}, u32[]{:S(2)}, u32[]{:S(2)}) collective-permute-start(bf16[5,128,384]{2,1,0:T(8,128)(2,1)S(1)} %add_convert_fusion.4), channel_id=1, source_target_pairs={{0,8},{4,12},{8,0},{12,4},{1,9},{5,13},{9,1},{13,5},{2,10},{6,14},... | collective-permute-start | bytes 1474568 | tf_op jit(solution)/shard_map/ppermute | solution.py:499
  319.7 36.3 %collective-permute-start.42 = (bf16[4,480,240]{2,1,0:T(8,128)(2,1)}, bf16[4,480,240]{2,1,0:T(8,128)(2,1)S(1)}, u32[]{:S(2)}, u32[]{:S(2)}) collective-permute-start(bf16[4,480,240]{2,1,0:T(8,128)(2,1)} %get-tuple-element.168), channel_id=1, source_target_pairs={{0,4},{4,0},{8,12},{12,8},{1,5},{5,1},{9,13},{13,9},{2,6},{6,2},{1... | collective-permute-start | bytes 2764808 | tf_op jit(solution)/shard_map/ppermute | solution.py:499
  332.9 23.3 %collective-permute-start.43 = (bf16[4,480,240]{2,1,0:T(8,128)(2,1)S(1)}, bf16[4,480,240]{2,1,0:T(8,128)(2,1)S(1)}, u32[]{:S(2)}, u32[]{:S(2)}) collective-permute-start(bf16[4,480,240]{2,1,0:T(8,128)(2,1)S(1)} %add_convert_fusion.1), channel_id=1, source_target_pairs={{0,8},{4,12},{8,0},{12,4},{1,9},{5,13},{9,1},{13,5},{2,10},{6,14},... | collective-permute-start | bytes 2764808 | tf_op jit(solution)/shard_map/ppermute | solution.py:499
  358.7 10.5 %collective-permute-start.46 = (bf16[4,176,240]{2,1,0:T(8,128)(2,1)S(1)}, bf16[4,176,240]{2,1,0:T(8,128)(2,1)S(1)}, u32[]{:S(2)}, u32[]{:S(2)}) collective-permute-start(bf16[4,176,240]{2,1,0:T(8,128)(2,1)S(1)} %add_convert_fusion.6), channel_id=1, source_target_pairs={{0,8},{4,12},{8,0},{12,4},{1,9},{5,13},{9,1},{13,5},{2,10},{6,14},... | collective-permute-start | bytes 1013768 | tf_op jit(solution)/shard_map/ppermute | solution.py:499
  371.7 15.7 %collective-permute-start.38 = (bf16[480,384]{1,0:T(8,128)(2,1)S(1)}, bf16[480,384]{1,0:T(8,128)(2,1)S(1)}, u32[]{:S(2)}, u32[]{:S(2)}) collective-permute-start(bf16[480,384]{1,0:T(8,128)(2,1)S(1)} %copy-done.48), channel_id=1, source_target_pairs={{0,0},{1,8},{2,4},{3,12},{4,1},{5,9},{6,5},{7,13},{8,2},{9,10},{10... | collective-permute-start | bytes 1105928 | tf_op jit(solution)/shard_map/ppermute | solution.py:558
  372.4 59.3 %collective-permute-start.52 = (bf16[240,896]{1,0:T(8,128)(2,1)}, bf16[240,896]{1,0:T(8,128)(2,1)S(1)}, u32[]{:S(2)}, u32[]{:S(2)}) collective-permute-start(bf16[240,896]{1,0:T(8,128)(2,1)} %reduce-scatter.8.cloned.1.call-done), channel_id=1, source_target_pairs={{0,16},{16,0},{1,17},{17,1},{2,18},{18,2},{3,19},{19,3},{4,20},{20... | collective-permute-start | bytes 1290248 | tf_op jit(solution)/shard_map/ppermute | solution.py:545
  381.8 20.1 %collective-permute-start.39 = (bf16[480,384]{1,0:T(8,128)(2,1)}, bf16[480,384]{1,0:T(8,128)(2,1)S(1)}, u32[]{:S(2)}, u32[]{:S(2)}) collective-permute-start(bf16[480,384]{1,0:T(8,128)(2,1)} %get-tuple-element.160), channel_id=1, source_target_pairs={{0,1},{1,9},{2,5},{3,13},{4,0},{5,8},{6,4},{7,12},{8,3},{9,11},{10... | collective-permute-start | bytes 1105928 | tf_op jit(solution)/shard_map/ppermute | solution.py:558
  384.8 32.9 %collective-permute-start.40 = (bf16[480,384]{1,0:T(8,128)(2,1)}, bf16[480,384]{1,0:T(8,128)(2,1)S(1)}, u32[]{:S(2)}, u32[]{:S(2)}) collective-permute-start(bf16[480,384]{1,0:T(8,128)(2,1)} %get-tuple-element.161), channel_id=1, source_target_pairs={{0,2},{1,10},{2,6},{3,14},{4,3},{5,11},{6,7},{7,15},{8,0},{9,8},{1... | collective-permute-start | bytes 1105928 | tf_op jit(solution)/shard_map/ppermute | solution.py:558
  384.9 41.9 %collective-permute-start.41 = (bf16[480,384]{1,0:T(8,128)(2,1)S(1)}, bf16[480,384]{1,0:T(8,128)(2,1)S(1)}, u32[]{:S(2)}, u32[]{:S(2)}) collective-permute-start(bf16[480,384]{1,0:T(8,128)(2,1)S(1)} %copy-done.45), channel_id=1, source_target_pairs={{0,3},{1,11},{2,7},{3,15},{4,2},{5,10},{6,6},{7,14},{8,1},{9,9},{1... | collective-permute-start | bytes 1105928 | tf_op jit(solution)/shard_map/ppermute | solution.py:558
  387.5 45.4 %collective-permute-start.51 = (bf16[240,1024]{1,0:T(8,128)(2,1)S(1)}, bf16[240,1024]{1,0:T(8,128)(2,1)S(1)}, u32[]{:S(2)}, u32[]{:S(2)}) collective-permute-start(bf16[240,1024]{1,0:T(8,128)(2,1)S(1)} %copy-done.21), channel_id=1, source_target_pairs={{0,16},{16,0},{1,17},{17,1},{2,18},{18,2},{3,19},{19,3},{4,20},{20... | collective-permute-start | bytes 1474568 | tf_op jit(solution)/shard_map/ppermute | solution.py:545
  426.8 10.3 %collective-permute-start.47 = (bf16[656,240]{1,0:T(8,128)(2,1)}, bf16[656,240]{1,0:T(8,128)(2,1)S(1)}, u32[]{:S(2)}, u32[]{:S(2)}) collective-permute-start(bf16[656,240]{1,0:T(8,128)(2,1)} %reduce-scatter.6.cloned.1.call-done), channel_id=1, source_target_pairs={{0,16},{16,0},{1,17},{17,1},{2,18},{18,2},{3,19},{19,3},{4,20},{20... | collective-permute-start | bytes 944648 | tf_op jit(solution)/shard_map/ppermute | solution.py:545
  437.2 9.8 %collective-permute-start.49 = (f32[128,240]{1,0:T(8,128)S(1)}, f32[128,240]{1,0:T(8,128)S(1)}, u32[]{:S(2)}, u32[]{:S(2)}) collective-permute-start(f32[128,240]{1,0:T(8,128)S(1)} %pad_maximum_fusion.5.o0), channel_id=1, source_target_pairs={{0,8},{4,12},{8,0},{12,4},{1,9},{5,13},{9,1},{13,5},{2,10},{6,14},... | collective-permute-start | bytes 368648 | tf_op jit(solution)/shard_map/ppermute | solution.py:499
  444.7 7.6 %collective-permute-start.48 = (f32[128,240]{1,0:T(8,128)S(1)}, f32[128,240]{1,0:T(8,128)S(1)}, u32[]{:S(2)}, u32[]{:S(2)}) collective-permute-start(f32[128,240]{1,0:T(8,128)S(1)} %pad_maximum_fusion.5.o0), channel_id=1, source_target_pairs={{0,4},{4,0},{8,12},{12,8},{1,5},{5,1},{9,13},{13,9},{2,6},{6,2},{1... | collective-permute-start | bytes 368648 | tf_op jit(solution)/shard_map/ppermute | solution.py:499
  447.0 5.3 %collective-permute-start.50 = (f32[128,240]{1,0:T(8,128)S(1)}, f32[128,240]{1,0:T(8,128)S(1)}, u32[]{:S(2)}, u32[]{:S(2)}) collective-permute-start(f32[128,240]{1,0:T(8,128)S(1)} %collective-permute-done.49.o2), channel_id=1, source_target_pairs={{0,4},{4,0},{8,12},{12,8},{1,5},{5,1},{9,13},{13,9},{2,6},{6,2},{1... | collective-permute-start | bytes 368648 | tf_op jit(solution)/shard_map/ppermute | solution.py:499
  (62 other events, 733.0 us)
Sparse Core Ops, SparseCore 0:
  88.8 42.0 all-gather.2
  132.4 30.0 all-gather.4
  273.3 40.1 reduce-scatter.3
  316.4 42.6 reduce-scatter.7
  370.8 55.3 reduce-scatter.5

commit v5 on v3

--- a/solution.py
+++ b/solution.py
@@ -714,10 +714,9 @@
     ).astype(BF)
     packs_b = list(packs_b)
     packs_b[3] = after(packs_b[3], g_a)
-    g_a = lax.psum_scatter(g_a.reshape(ROWS * AP, FB), "gy", scatter_dimension=0, tiled=True)
-    g_b = row_scatter(packs_b).reshape(ROWS * BP, FB)
-    g_b = lax.psum_scatter(g_b, "gy", scatter_dimension=0, tiled=True)
-    g_all = dp_sum(after(jnp.concatenate([g_a, g_b], axis=0), *back))
+    g_all = jnp.concatenate([g_a, row_scatter(packs_b)], axis=1).reshape(ROWS * (AP + BP), FB)
+    g_all = lax.psum_scatter(g_all, "gy", scatter_dimension=0, tiled=True)
+    g_all = dp_sum(after(g_all, *back))
     odds = jnp.concatenate([g_all[AW:AP], g_all[AP + KV : AP + KV + KV // ROWS]], axis=0)
     grad_qkv, grad_out, grad_gains = simple(
         grads_kernel, "grads",

time: 463 us -> 453 us (0.978)
  waiting for transfers between devices: 183 us -> 144 us
  starting transfers between devices: 88.5 us -> 118 us
    reduce_scatter x2 -> x1, waiting for transfers between devices: 53.9 us -> 3.14 us  [per_device(): g_all = lax.psum_scatter(g_all, 'gy', scatter_dimension=0, tiled=True)]
    ppermute x4, waiting for transfers between devices: 0.01 us -> 35.1 us  [to_features(): back.append(lax.ppermute(pieces[k], ('gx', 'gy'), pairs))]
    ppermute x36, starting transfers between devices: 64.7 us -> 86.7 us  [swap(): return lax.ppermute(values, 'gx', [(i, i ^ bit) for i in range(ROWS)])]
    ppermute x36, waiting for transfers between devices: 53.8 us -> 43.3 us  [swap(): return lax.ppermute(values, 'gx', [(i, i ^ bit) for i in range(ROWS)])]
    ppermute x1, waiting for transfers between devices: 18.3 us -> 8.27 us  [per_device(): w_gu.append(lax.ppermute(w_gu[0], 'dp', [(0, 1), (1, 0)]))]
    ppermute x4, starting transfers between devices: 6.55 us -> 11.2 us  [to_features(): back.append(lax.ppermute(pieces[k], ('gx', 'gy'), pairs))]
    unnamed x101 -> x99, local copies, waits for them, and re-layouts: 13.1 us -> 13.9 us
  transfers between devices with their start and end apart: 58 -> 57, of which waited for: 23 -> 27; matrix products, arithmetic and copies ran while one was open for 6% -> 6% of each run, Pallas kernels for 20% -> 20%
where the time goes in v5:
time: 453 us; the launch traced here: 444 us
  waiting for transfers between devices  144 us (32%)
  Pallas kernels  121 us (27%)
  starting transfers between devices  118 us (26%)
  local copies, waits for them, and re-layouts  23.2 us (5%)
  between operations  20.8 us (5%)
  other arithmetic  17.4 us (4%)
    ppermute x36, starting transfers between devices, swap(): return lax.ppermute(values, 'gx', [(i, i ^ bit) for i in range(ROWS)])  86.7 us
    pallas_call x3, Pallas kernels, grouped(): pl.pallas_call(kernel, grid_spec=pltpu.PrefetchScalarGridSpec(num_scalar_...  62.8 us
    pallas_call x7, Pallas kernels, simple(): pl.pallas_call(kernel, in_specs=specs, out_specs=[pl.BlockSpec(memory_spa...  57.9 us
    ppermute x36, waiting for transfers between devices, swap(): return lax.ppermute(values, 'gx', [(i, i ^ bit) for i in range(ROWS)])  43.3 us
    ppermute x3, waiting for transfers between devices, ring(): lax.ppermute(values, 'gy', [(i, (i + 1) % ROWS) for i in range(ROWS)])  39 us
    ppermute x4, waiting for transfers between devices, to_features(): back.append(lax.ppermute(pieces[k], ('gx', 'gy'), pairs))  35.1 us
    unnamed x99, local copies, waits for them, and re-layouts  13.9 us
    ppermute x4, starting transfers between devices, to_features(): back.append(lax.ppermute(pieces[k], ('gx', 'gy'), pairs))  11.2 us
  transfers between devices with their start and end apart: 57, of which 27 were waited for; matrix products, arithmetic and copies ran while one was open for 6% of the time, Pallas kernels for 20%

profile of v5, /device:TPU:0, one launch (start us, length us, event | category | flops | bytes accessed | tf_op | source)
XLA Modules:
  0.0 444.5 jit_solution(6088708886609341547)
XLA Ops:
  13.0 2.9 collective-permute-start.4
  18.9 3.5 split.1
  24.1 1.9 collective-permute-start.5
  26.0 17.4 %collective-permute-done.5 = bf16[240,640]{1,0:T(8,128)(2,1)} collective-permute-done((bf16[240,640]{1,0:T(8,128)(2,1)S(1)}, bf16[240,640]{1,0:T(8,128)(2,1)}, u32[]{:S(2)}, u32[]{:S(2)}) %collective-permute-start.5) | collective-permute-done | bytes 307232 | tf_op jit(solution)/shard_map/ppermute | solution.py:526
  43.5 2.1 collective-permute-start.7
  45.6 15.5 %collective-permute-done.7 = bf16[240,640]{1,0:T(8,128)(2,1)} collective-permute-done((bf16[240,640]{1,0:T(8,128)(2,1)}, bf16[240,640]{1,0:T(8,128)(2,1)}, u32[]{:S(2)}, u32[]{:S(2)}) %collective-permute-start.7) | collective-permute-done | bytes 307232 | tf_op jit(solution)/shard_map/ppermute | solution.py:526
  61.1 4.0 collective-permute-done.6.refs_1_
  66.2 2.0 collective-permute-start.8
  68.2 6.1 %collective-permute-done.9 = bf16[240,640]{1,0:T(8,128)(2,1)} collective-permute-done((bf16[240,640]{1,0:T(8,128)(2,1)}, bf16[240,640]{1,0:T(8,128)(2,1)}, u32[]{:S(2)}, u32[]{:S(2)}) %collective-permute-start.9) | collective-permute-done | bytes 307232 | tf_op jit(solution)/shard_map/ppermute | solution.py:526
  74.3 4.3 collective-permute-start.10
  79.3 2.4 collective-permute-start.13
  83.9 5.8 %collective-permute-done.10.refs_3_ = bf16[480,384]{1,0:T(8,128)(2,1)S(1)} collective-permute-done((bf16[480,384]{1,0:T(8,128)(2,1)}, bf16[480,384]{1,0:T(8,128)(2,1)S(1)}, u32[]{:S(2)}, u32[]{:S(2)}) %collective-permute-start.10) | collective-permute-done | bytes 368672 | tf_op jit(solution)/shard_map/ppermute | solution.py:547
  90.9 8.0 %collective-permute-start.15 = (bf16[240,640]{1,0:T(8,128)(2,1)}, bf16[240,640]{1,0:T(8,128)(2,1)S(1)}, u32[]{:S(2)}, u32[]{:S(2)}) collective-permute-start(bf16[240,640]{1,0:T(8,128)(2,1)} %collective-permute-done.9), channel_id=1, source_target_pairs={{0,8},{4,12},{8,0},{12,4},{1,9},{5,13},{9,1},{13,5},{2,10},{6,14},... | collective-permute-start | bytes 921608 | tf_op jit(solution)/shard_map/ppermute | solution.py:495
  101.0 7.4 %collective-permute-start.11 = (bf16[960,640]{1,0:T(8,128)(2,1)S(1)}, bf16[960,640]{1,0:T(8,128)(2,1)}, u32[]{:S(2)}, u32[]{:S(2)}) collective-permute-start(bf16[960,640]{1,0:T(8,128)(2,1)S(1)} %constant_dynamic-update-slice_fusion.refs_4_), channel_id=1, source_target_pairs={{0,4},{4,0},{8,12},{12,8},{1,5},{5,1},{9,13},{13,9},{2,6},{6,2},{1... | collective-permute-start | bytes 3686408 | tf_op jit(solution)/shard_map/ppermute | solution.py:495
  111.6 2.6 select_add_fusion
  115.1 9.0 %qkv.1 = (bf16[960,384]{1,0:T(8,128)(2,1)}, bf16[960,384]{1,0:T(8,128)(2,1)}, bf16[960,384]{1,0:T(8,128)(2,1)}, f32[1,384]{1,0:T(1,128)}, f32[960,1]{1,0:T(8,128...) custom-call(s32[4]{0:T(128)} %pad_add_fusion.sc, ...), custom_call_target="tpu_custom_call" | custom-call | flops 700000000 | bytes 2100000 | tf_op jit(solution)/shard_map/qkv/pallas_call | solution.py:465
  124.2 2.5 collective-permute-start.18
  132.9 5.5 %collective-permute-done.18.kv2 = bf16[5,128,384]{2,1,0:T(8,128)(2,1)} collective-permute-done((bf16[5,128,384]{2,1,0:T(8,128)(2,1)}, bf16[5,128,384]{2,1,0:T(8,128)(2,1)}, u32[]{:S(2)}, u32[]{:S(2)}) %collective-permute-start.18) | collective-permute-done | bytes 491552 | tf_op jit(solution)/shard_map/ppermute | solution.py:495
  143.7 15.3 %attend.1 = (bf16[5,192,384]{2,1,0:T(8,128)(2,1)}, f32[5,8,384]{2,1,0:T(8,128)}, f32[960,384]{1,0:T(8,128)}, bf16[960,384]{1,0:T(8,128)(2,1)}, f32[1,384]{1,0:T(1,128)}) custom-call(s32[8]{0:T(128)} %concatenate.28.sc, bf16[5,192,384]{2,1,0:T(8,128)(2,1)} %get-tuple-element.109.qs_ref, bf16[5,128,384]{2,1,0:T(8,128)(2,1)} %get-tuple-element.106.kv0, ...), custom_call_target="tpu_custom_call" | custom-call | flops 1800000000 | bytes 5400000 | tf_op jit(solution)/shard_map/attend/pallas_call | solution.py:478
  159.0 7.0 %collective-permute-start.21 = (bf16[960,384]{1,0:T(8,128)(2,1)}, bf16[960,384]{1,0:T(8,128)(2,1)}, u32[]{:S(2)}, u32[]{:S(2)}) collective-permute-start(bf16[960,384]{1,0:T(8,128)(2,1)} %get-tuple-element.123.refs_3_.refs_0_), channel_id=1, source_target_pairs={{0,8},{4,12},{8,0},{12,4},{1,9},{5,13},{9,1},{13,5},{2,10},{6,14},... | collective-permute-start | bytes 2211848 | tf_op jit(solution)/shard_map/ppermute | solution.py:495
  167.5 6.3 %collective-permute-start.24 = (bf16[960,384]{1,0:T(8,128)(2,1)}, bf16[960,384]{1,0:T(8,128)(2,1)}, u32[]{:S(2)}, u32[]{:S(2)}) collective-permute-start(bf16[960,384]{1,0:T(8,128)(2,1)} %collective-permute-done.23.refs_5_.refs_6_), channel_id=1, source_target_pairs={{0,4},{4,0},{8,12},{12,8},{1,5},{5,1},{9,13},{13,9},{2,6},{6,2},{1... | collective-permute-start | bytes 2211848 | tf_op jit(solution)/shard_map/ppermute | solution.py:495
  173.8 3.6 collective-permute-done.21.refs_3_.refs_2_
  177.4 6.3 %collective-permute-start.22 = (bf16[960,384]{1,0:T(8,128)(2,1)}, bf16[960,384]{1,0:T(8,128)(2,1)}, u32[]{:S(2)}, u32[]{:S(2)}) collective-permute-start(bf16[960,384]{1,0:T(8,128)(2,1)} %collective-permute-done.21.refs_3_.refs_2_), channel_id=1, source_target_pairs={{0,4},{4,0},{8,12},{12,8},{1,5},{5,1},{9,13},{13,9},{2,6},{6,2},{1... | collective-permute-start | bytes 2211848 | tf_op jit(solution)/shard_map/ppermute | solution.py:495
  183.7 8.3 %collective-permute-done.20.refs_1_ = bf16[512,1280]{1,0:T(8,128)(2,1)S(1)} collective-permute-done((bf16[512,1280]{1,0:T(8,128)(2,1)S(1)}, bf16[512,1280]{1,0:T(8,128)(2,1)S(1)}, u32[]{:S(2)}, u32[]{:S(2)}) %collective-permute-start.20) | collective-permute-done | bytes 1310752 | tf_op jit(solution)/shard_map/ppermute | solution.py:614
  193.0 12.8 %mlp_far.1 = (bf16[640,384]{1,0:T(8,128)(2,1)}, bf16[640,384]{1,0:T(8,128)(2,1)}, bf16[640,384]{1,0:T(8,128)(2,1)}, bf16[960,384]{1,0:T(8,128)(2,1)}, bf16[960,3...) custom-call(s32[4]{0:T(128)} %pad_add_fusion.sc, ...), custom_call_target="tpu_custom_call" | custom-call | flops 1300000000 | bytes 3900000 | tf_op jit(solution)/shard_map/mlp_far/pallas_call | solution.py:465
  205.8 5.5 %collective-permute-start.28 = (bf16[960,384]{1,0:T(8,128)(2,1)}, bf16[960,384]{1,0:T(8,128)(2,1)S(1)}, u32[]{:S(2)}, u32[]{:S(2)}) collective-permute-start(bf16[960,384]{1,0:T(8,128)(2,1)} %get-tuple-element.118), channel_id=1, source_target_pairs={{0,4},{4,0},{8,12},{12,8},{1,5},{5,1},{9,13},{13,9},{2,6},{6,2},{1... | collective-permute-start | bytes 2211848 | tf_op jit(solution)/shard_map/ppermute | solution.py:495
  216.9 13.0 %mlp_near.1 = (bf16[640,384]{1,0:T(8,128)(2,1)}, bf16[640,384]{1,0:T(8,128)(2,1)}, bf16[640,384]{1,0:T(8,128)(2,1)}, bf16[960,384]{1,0:T(8,128)(2,1)}, bf16[960,...) custom-call(s32[4]{0:T(128)} %pad_add_fusion.sc, ...), custom_call_target="tpu_custom_call" | custom-call | flops 1300000000 | bytes 3900000 | tf_op jit(solution)/shard_map/mlp_near/pallas_call | solution.py:465
  229.9 3.9 collective-permute-done.29.dn_c
  233.9 14.4 %mlp_grad.1 = (bf16[960,1024]{1,0:T(8,128)(2,1)}, bf16[960,896]{1,0:T(8,128)(2,1)}) custom-call(bf16[960,384]{1,0:T(8,128)(2,1)} %get-tuple-element.123.refs_3_.refs_0_, bf16[960,384]{1,0:T(8,128)(2,1)} %copy-done.6, bf16[960,384]{1,0:T(8,128)(2,1)} %collective-permute-done.21.refs_3_.refs_2_, bf16[960,384]{1,0:T(8,128)(2,1)} %collective-permute-done.22.refs_4_.refs_3_, ...), custom_call_target="tpu_custom_call" | custom-call | flops 1800000000 | bytes 5400000 | tf_op jit(solution)/shard_map/mlp_grad/pallas_call | solution.py:465
  253.5 28.5 %attend_back.1 = (bf16[5,192,384]{2,1,0:T(8,128)(2,1)}, f32[5,128,384]{2,1,0:T(8,128)}, bf16[5,128,384]{2,1,0:T(8,128)(2,1)}, bf16[5,128,384]{2,1,0:T(8,128)(2,1...) custom-call(s32[8]{0:T(128)} %concatenate.28.sc, ...), custom_call_target="tpu_custom_call" | custom-call | flops 3000000000 | bytes 9000000 | tf_op jit(solution)/shard_map/attend_back/pallas_call | solution.py:478
  282.1 7.9 %collective-permute-start.33 = (bf16[5,128,384]{2,1,0:T(8,128)(2,1)}, bf16[5,128,384]{2,1,0:T(8,128)(2,1)}, u32[]{:S(2)}, u32[]{:S(2)}) collective-permute-start(bf16[5,128,384]{2,1,0:T(8,128)(2,1)} %get-tuple-element.149), channel_id=1, source_target_pairs={{0,4},{4,0},{8,12},{12,8},{1,5},{5,1},{9,13},{13,9},{2,6},{6,2},{1... | collective-permute-start | bytes 1474568 | tf_op jit(solution)/shard_map/ppermute | solution.py:495
  293.1 8.7 %collective-permute-start.34 = (bf16[5,128,384]{2,1,0:T(8,128)(2,1)S(1)}, bf16[5,128,384]{2,1,0:T(8,128)(2,1)S(1)}, u32[]{:S(2)}, u32[]{:S(2)}) collective-permute-start(bf16[5,128,384]{2,1,0:T(8,128)(2,1)S(1)} %add_convert_fusion.4), channel_id=1, source_target_pairs={{0,8},{4,12},{8,0},{12,4},{1,9},{5,13},{9,1},{13,5},{2,10},{6,14},... | collective-permute-start | bytes 1474568 | tf_op jit(solution)/shard_map/ppermute | solution.py:495
  302.1 11.4 %collective-permute-done.34.d2 = bf16[5,128,384]{2,1,0:T(8,128)(2,1)S(1)} collective-permute-done((bf16[5,128,384]{2,1,0:T(8,128)(2,1)S(1)}, bf16[5,128,384]{2,1,0:T(8,128)(2,1)S(1)}, u32[]{:S(2)}, u32[]{:S(2)}) %collective-permute-start.34) | collective-permute-done | bytes 491552 | tf_op jit(solution)/shard_map/ppermute | solution.py:495
  319.0 19.0 %final.1 = (bf16[4,176,240]{2,1,0:T(8,128)(2,1)}, bf16[4,176,240]{2,1,0:T(8,128)(2,1)}, bf16[4,176,240]{2,1,0:T(8,128)(2,1)}, bf16[4,176,240]{2,1,0:T(8,128)(2,1...) custom-call(s32[8]{0:T(128)} %concatenate.28.sc, ...), custom_call_target="tpu_custom_call" | custom-call | flops 1900000000 | bytes 5700000 | tf_op jit(solution)/shard_map/final/pallas_call | solution.py:478
  341.2 10.1 %collective-permute-done.45 = bf16[4,176,240]{2,1,0:T(8,128)(2,1)S(1)} collective-permute-done((bf16[4,176,240]{2,1,0:T(8,128)(2,1)S(1)}, bf16[4,176,240]{2,1,0:T(8,128)(2,1)S(1)}, u32[]{:S(2)}, u32[]{:S(2)}) %collective-permute-start.45) | collective-permute-done | bytes 337952 | tf_op jit(solution)/shard_map/ppermute | solution.py:495
  356.0 5.4 %collective-permute-start.38 = (bf16[480,384]{1,0:T(8,128)(2,1)}, bf16[480,384]{1,0:T(8,128)(2,1)S(1)}, u32[]{:S(2)}, u32[]{:S(2)}) collective-permute-start(bf16[480,384]{1,0:T(8,128)(2,1)} %get-tuple-element.160), channel_id=1, source_target_pairs={{0,1},{1,9},{2,5},{3,13},{4,0},{5,8},{6,4},{7,12},{8,3},{9,11},{10... | collective-permute-start | bytes 1105928 | tf_op jit(solution)/shard_map/ppermute | solution.py:554
  362.6 3.9 collective-permute-start.40
  367.0 10.7 %collective-permute-done.38.refs_1_ = bf16[480,384]{1,0:T(8,128)(2,1)S(1)} collective-permute-done((bf16[480,384]{1,0:T(8,128)(2,1)}, bf16[480,384]{1,0:T(8,128)(2,1)S(1)}, u32[]{:S(2)}, u32[]{:S(2)}) %collective-permute-start.38) | collective-permute-done | bytes 368672 | tf_op jit(solution)/shard_map/ppermute | solution.py:554
  377.7 15.8 %collective-permute-done.39.refs_2_ = bf16[480,384]{1,0:T(8,128)(2,1)S(1)} collective-permute-done((bf16[480,384]{1,0:T(8,128)(2,1)}, bf16[480,384]{1,0:T(8,128)(2,1)S(1)}, u32[]{:S(2)}, u32[]{:S(2)}) %collective-permute-start.39) | collective-permute-done | bytes 368672 | tf_op jit(solution)/shard_map/ppermute | solution.py:554
  393.5 8.6 %collective-permute-done.40.refs_3_ = bf16[480,384]{1,0:T(8,128)(2,1)S(1)} collective-permute-done((bf16[480,384]{1,0:T(8,128)(2,1)S(1)}, bf16[480,384]{1,0:T(8,128)(2,1)S(1)}, u32[]{:S(2)}, u32[]{:S(2)}) %collective-permute-start.40) | collective-permute-done | bytes 368672 | tf_op jit(solution)/shard_map/ppermute | solution.py:554
  402.0 3.1 reduce-scatter.6.cloned.1.call-done
  405.2 3.6 collective-permute-start.46
  410.1 4.0 collective-permute-done.46
  414.3 4.7 %collective-permute-start.48 = (f32[128,240]{1,0:T(8,128)S(1)}, f32[128,240]{1,0:T(8,128)S(1)}, u32[]{:S(2)}, u32[]{:S(2)}) collective-permute-start(f32[128,240]{1,0:T(8,128)S(1)} %pad_maximum_fusion.5.o0), channel_id=1, source_target_pairs={{0,8},{4,12},{8,0},{12,4},{1,9},{5,13},{9,1},{13,5},{2,10},{6,14},... | collective-permute-start | bytes 368648 | tf_op jit(solution)/shard_map/ppermute | solution.py:495
  419.9 5.2 %collective-permute-start.47 = (f32[128,240]{1,0:T(8,128)S(1)}, f32[128,240]{1,0:T(8,128)S(1)}, u32[]{:S(2)}, u32[]{:S(2)}) collective-permute-start(f32[128,240]{1,0:T(8,128)S(1)} %pad_maximum_fusion.5.o0), channel_id=1, source_target_pairs={{0,4},{4,0},{8,12},{12,8},{1,5},{5,1},{9,13},{13,9},{2,6},{6,2},{1... | collective-permute-start | bytes 368648 | tf_op jit(solution)/shard_map/ppermute | solution.py:495
  425.2 2.8 collective-permute-start.49
  429.7 2.7 merge.1
  433.7 2.5 grads.1
  (231 shorter events, 65.6 us)
Async XLA Ops:
  7.2 136.5 %all-gather.3.cloned.1.call-start = ((), (), s32[]{:S(2)}) async-start(), calls=%async_computation.3 | async-start | bytes 1638400 | tf_op jit(solution)/shard_map/all_gather | solution.py:612
  12.1 11.8 %collective-permute-start.2 = (bf16[240,128]{1,0:T(8,128)(2,1)S(1)}, bf16[240,128]{1,0:T(8,128)(2,1)S(1)}, u32[]{:S(2)}, u32[]{:S(2)}) collective-permute-start(bf16[240,128]{1,0:T(8,128)(2,1)S(1)} %get-tuple-element.210), channel_id=1, source_target_pairs={{0,4},{4,0},{8,12},{12,8},{1,5},{5,1},{9,13},{13,9},{2,6},{6,2},{1... | collective-permute-start | bytes 184328 | tf_op jit(solution)/shard_map/ppermute | solution.py:495
  13.0 10.9 %collective-permute-start.4 = (bf16[240,128]{1,0:T(8,128)(2,1)S(1)}, bf16[240,128]{1,0:T(8,128)(2,1)S(1)}, u32[]{:S(2)}, u32[]{:S(2)}) collective-permute-start(bf16[240,128]{1,0:T(8,128)(2,1)S(1)} %add_convert_fusion.8), channel_id=1, source_target_pairs={{0,8},{4,12},{8,0},{12,4},{1,9},{5,13},{9,1},{13,5},{2,10},{6,14},... | collective-permute-start | bytes 184328 | tf_op jit(solution)/shard_map/ppermute | solution.py:495
  22.3 21.2 %collective-permute-start.1 = (bf16[480,384]{1,0:T(8,128)(2,1)}, bf16[480,384]{1,0:T(8,128)(2,1)S(1)}, u32[]{:S(2)}, u32[]{:S(2)}) collective-permute-start(bf16[480,384]{1,0:T(8,128)(2,1)} %get-tuple-element.93), channel_id=1, source_target_pairs={{0,0},{1,4},{2,8},{3,12},{4,2},{5,6},{6,10},{7,14},{8,1},{9,5},{10... | collective-permute-start | bytes 1105928 | tf_op jit(solution)/shard_map/ppermute | solution.py:547
  24.1 19.4 %collective-permute-start.5 = (bf16[240,640]{1,0:T(8,128)(2,1)S(1)}, bf16[240,640]{1,0:T(8,128)(2,1)}, u32[]{:S(2)}, u32[]{:S(2)}) collective-permute-start(bf16[240,640]{1,0:T(8,128)(2,1)S(1)} %pad_maximum_fusion.4), channel_id=1, source_target_pairs={{0,1},{1,2},{2,3},{3,0},{4,5},{5,6},{6,7},{7,4},{8,9},{9,10},{10,1... | collective-permute-start | bytes 921608 | tf_op jit(solution)/shard_map/ppermute | solution.py:526
  43.5 21.6 %collective-permute-start.6 = (bf16[480,384]{1,0:T(8,128)(2,1)}, bf16[480,384]{1,0:T(8,128)(2,1)S(1)}, u32[]{:S(2)}, u32[]{:S(2)}) collective-permute-start(bf16[480,384]{1,0:T(8,128)(2,1)} %get-tuple-element.96), channel_id=1, source_target_pairs={{0,4},{1,0},{2,12},{3,8},{4,6},{5,2},{6,14},{7,10},{8,5},{9,1},{10... | collective-permute-start | bytes 1105928 | tf_op jit(solution)/shard_map/ppermute | solution.py:547
  43.5 17.6 %collective-permute-start.7 = (bf16[240,640]{1,0:T(8,128)(2,1)}, bf16[240,640]{1,0:T(8,128)(2,1)}, u32[]{:S(2)}, u32[]{:S(2)}) collective-permute-start(bf16[240,640]{1,0:T(8,128)(2,1)} %collective-permute-done.5), channel_id=1, source_target_pairs={{0,1},{1,2},{2,3},{3,0},{4,5},{5,6},{6,7},{7,4},{8,9},{9,10},{10,1... | collective-permute-start | bytes 921608 | tf_op jit(solution)/shard_map/ppermute | solution.py:526
  65.1 9.2 %collective-permute-start.9 = (bf16[240,640]{1,0:T(8,128)(2,1)}, bf16[240,640]{1,0:T(8,128)(2,1)}, u32[]{:S(2)}, u32[]{:S(2)}) collective-permute-start(bf16[240,640]{1,0:T(8,128)(2,1)} %collective-permute-done.7), channel_id=1, source_target_pairs={{0,1},{1,2},{2,3},{3,0},{4,5},{5,6},{6,7},{7,4},{8,9},{9,10},{10,1... | collective-permute-start | bytes 921608 | tf_op jit(solution)/shard_map/ppermute | solution.py:526
  66.1 15.7 %collective-permute-start.12 = (bf16[240,640]{1,0:T(8,128)(2,1)S(1)}, bf16[240,640]{1,0:T(8,128)(2,1)}, u32[]{:S(2)}, u32[]{:S(2)}) collective-permute-start(bf16[240,640]{1,0:T(8,128)(2,1)S(1)} %pad_maximum_fusion.4), channel_id=1, source_target_pairs={{0,8},{4,12},{8,0},{12,4},{1,9},{5,13},{9,1},{13,5},{2,10},{6,14},... | collective-permute-start | bytes 921608 | tf_op jit(solution)/shard_map/ppermute | solution.py:495
  66.2 17.7 %collective-permute-start.8 = (bf16[480,384]{1,0:T(8,128)(2,1)}, bf16[480,384]{1,0:T(8,128)(2,1)S(1)}, u32[]{:S(2)}, u32[]{:S(2)}) collective-permute-start(bf16[480,384]{1,0:T(8,128)(2,1)} %get-tuple-element.99), channel_id=1, source_target_pairs={{0,8},{1,12},{2,0},{3,4},{4,10},{5,14},{6,2},{7,6},{8,9},{9,13},{1... | collective-permute-start | bytes 1105928 | tf_op jit(solution)/shard_map/ppermute | solution.py:547
  74.3 15.5 %collective-permute-start.10 = (bf16[480,384]{1,0:T(8,128)(2,1)}, bf16[480,384]{1,0:T(8,128)(2,1)S(1)}, u32[]{:S(2)}, u32[]{:S(2)}) collective-permute-start(bf16[480,384]{1,0:T(8,128)(2,1)} %get-tuple-element.102), channel_id=1, source_target_pairs={{0,12},{1,8},{2,4},{3,0},{4,14},{5,10},{6,6},{7,2},{8,13},{9,9},{1... | collective-permute-start | bytes 1105928 | tf_op jit(solution)/shard_map/ppermute | solution.py:547
  79.3 19.6 %collective-permute-start.13 = (bf16[240,640]{1,0:T(8,128)(2,1)}, bf16[240,640]{1,0:T(8,128)(2,1)S(1)}, u32[]{:S(2)}, u32[]{:S(2)}) collective-permute-start(bf16[240,640]{1,0:T(8,128)(2,1)} %collective-permute-done.5), channel_id=1, source_target_pairs={{0,8},{4,12},{8,0},{12,4},{1,9},{5,13},{9,1},{13,5},{2,10},{6,14},... | collective-permute-start | bytes 921608 | tf_op jit(solution)/shard_map/ppermute | solution.py:495
  82.8 16.2 %collective-permute-start.14 = (bf16[240,640]{1,0:T(8,128)(2,1)}, bf16[240,640]{1,0:T(8,128)(2,1)}, u32[]{:S(2)}, u32[]{:S(2)}) collective-permute-start(bf16[240,640]{1,0:T(8,128)(2,1)} %collective-permute-done.7), channel_id=1, source_target_pairs={{0,8},{4,12},{8,0},{12,4},{1,9},{5,13},{9,1},{13,5},{2,10},{6,14},... | collective-permute-start | bytes 921608 | tf_op jit(solution)/shard_map/ppermute | solution.py:495
  89.8 93.9 %all-gather.5.cloned.1.call-start = ((), (), s32[]{:S(2)}) async-start(), calls=%async_computation.4 | async-start | bytes 1536000 | tf_op jit(solution)/shard_map/all_gather | solution.py:625
  90.9 17.5 %collective-permute-start.15 = (bf16[240,640]{1,0:T(8,128)(2,1)}, bf16[240,640]{1,0:T(8,128)(2,1)S(1)}, u32[]{:S(2)}, u32[]{:S(2)}) collective-permute-start(bf16[240,640]{1,0:T(8,128)(2,1)} %collective-permute-done.9), channel_id=1, source_target_pairs={{0,8},{4,12},{8,0},{12,4},{1,9},{5,13},{9,1},{13,5},{2,10},{6,14},... | collective-permute-start | bytes 921608 | tf_op jit(solution)/shard_map/ppermute | solution.py:495
  101.0 14.1 %collective-permute-start.11 = (bf16[960,640]{1,0:T(8,128)(2,1)S(1)}, bf16[960,640]{1,0:T(8,128)(2,1)}, u32[]{:S(2)}, u32[]{:S(2)}) collective-permute-start(bf16[960,640]{1,0:T(8,128)(2,1)S(1)} %constant_dynamic-update-slice_fusion.refs_4_), channel_id=1, source_target_pairs={{0,4},{4,0},{8,12},{12,8},{1,5},{5,1},{9,13},{13,9},{2,6},{6,2},{1... | collective-permute-start | bytes 3686408 | tf_op jit(solution)/shard_map/ppermute | solution.py:495
  108.5 6.7 %collective-permute-start.16 = (bf16[960,640]{1,0:T(8,128)(2,1)S(1)}, bf16[960,640]{1,0:T(8,128)(2,1)}, u32[]{:S(2)}, u32[]{:S(2)}) collective-permute-start(bf16[960,640]{1,0:T(8,128)(2,1)S(1)} %constant_dynamic-update-slice_fusion.4.refs_6_), channel_id=1, source_target_pairs={{0,4},{4,0},{8,12},{12,8},{1,5},{5,1},{9,13},{13,9},{2,6},{6,2},{1... | collective-permute-start | bytes 3686408 | tf_op jit(solution)/shard_map/ppermute | solution.py:495
  124.2 14.2 %collective-permute-start.18 = (bf16[5,128,384]{2,1,0:T(8,128)(2,1)}, bf16[5,128,384]{2,1,0:T(8,128)(2,1)}, u32[]{:S(2)}, u32[]{:S(2)}) collective-permute-start(bf16[5,128,384]{2,1,0:T(8,128)(2,1)} %get-tuple-element.106.kv0), channel_id=1, source_target_pairs={{0,8},{4,12},{8,0},{12,4},{1,9},{5,13},{9,1},{13,5},{2,10},{6,14},... | collective-permute-start | bytes 1474568 | tf_op jit(solution)/shard_map/ppermute | solution.py:495
  126.7 165.0 %reduce-scatter.4.cloned.1.call-start = ((), (), s32[]{:S(2)}) async-start(), calls=%async_computation.5 | async-start | bytes 2457600 | tf_op jit(solution)/shard_map/reduce_scatter | solution.py:688
  132.9 10.8 %collective-permute-start.17 = (bf16[5,128,384]{2,1,0:T(8,128)(2,1)}, bf16[5,128,384]{2,1,0:T(8,128)(2,1)}, u32[]{:S(2)}, u32[]{:S(2)}) collective-permute-start(bf16[5,128,384]{2,1,0:T(8,128)(2,1)} %get-tuple-element.106.kv0), channel_id=1, source_target_pairs={{0,4},{4,0},{8,12},{12,8},{1,5},{5,1},{9,13},{13,9},{2,6},{6,2},{1... | collective-permute-start | bytes 1474568 | tf_op jit(solution)/shard_map/ppermute | solution.py:495
  138.4 5.3 %collective-permute-start.19 = (bf16[5,128,384]{2,1,0:T(8,128)(2,1)}, bf16[5,128,384]{2,1,0:T(8,128)(2,1)}, u32[]{:S(2)}, u32[]{:S(2)}) collective-permute-start(bf16[5,128,384]{2,1,0:T(8,128)(2,1)} %collective-permute-done.18.kv2), channel_id=1, source_target_pairs={{0,4},{4,0},{8,12},{12,8},{1,5},{5,1},{9,13},{13,9},{2,6},{6,2},{1... | collective-permute-start | bytes 1474568 | tf_op jit(solution)/shard_map/ppermute | solution.py:495
  141.9 25.6 %collective-permute-start.23 = (bf16[960,384]{1,0:T(8,128)(2,1)S(1)}, bf16[960,384]{1,0:T(8,128)(2,1)}, u32[]{:S(2)}, u32[]{:S(2)}) collective-permute-start(bf16[960,384]{1,0:T(8,128)(2,1)S(1)} %copy-done), channel_id=1, source_target_pairs={{0,8},{4,12},{8,0},{12,4},{1,9},{5,13},{9,1},{13,5},{2,10},{6,14},... | collective-permute-start | bytes 2211848 | tf_op jit(solution)/shard_map/ppermute | solution.py:495
  159.0 18.4 %collective-permute-start.21 = (bf16[960,384]{1,0:T(8,128)(2,1)}, bf16[960,384]{1,0:T(8,128)(2,1)}, u32[]{:S(2)}, u32[]{:S(2)}) collective-permute-start(bf16[960,384]{1,0:T(8,128)(2,1)} %get-tuple-element.123.refs_3_.refs_0_), channel_id=1, source_target_pairs={{0,8},{4,12},{8,0},{12,4},{1,9},{5,13},{9,1},{13,5},{2,10},{6,14},... | collective-permute-start | bytes 2211848 | tf_op jit(solution)/shard_map/ppermute | solution.py:495
  166.0 25.9 %collective-permute-start.20 = (bf16[512,1280]{1,0:T(8,128)(2,1)S(1)}, bf16[512,1280]{1,0:T(8,128)(2,1)S(1)}, u32[]{:S(2)}, u32[]{:S(2)}) collective-permute-start(bf16[512,1280]{1,0:T(8,128)(2,1)S(1)} %copy-done.1), channel_id=1, source_target_pairs={{0,16},{16,0},{1,17},{17,1},{2,18},{18,2},{3,19},{19,3},{4,20},{20... | collective-permute-start | bytes 3932168 | tf_op jit(solution)/shard_map/ppermute | solution.py:614
  167.5 16.2 %collective-permute-start.24 = (bf16[960,384]{1,0:T(8,128)(2,1)}, bf16[960,384]{1,0:T(8,128)(2,1)}, u32[]{:S(2)}, u32[]{:S(2)}) collective-permute-start(bf16[960,384]{1,0:T(8,128)(2,1)} %collective-permute-done.23.refs_5_.refs_6_), channel_id=1, source_target_pairs={{0,4},{4,0},{8,12},{12,8},{1,5},{5,1},{9,13},{13,9},{2,6},{6,2},{1... | collective-permute-start | bytes 2211848 | tf_op jit(solution)/shard_map/ppermute | solution.py:495
  177.4 14.6 %collective-permute-start.22 = (bf16[960,384]{1,0:T(8,128)(2,1)}, bf16[960,384]{1,0:T(8,128)(2,1)}, u32[]{:S(2)}, u32[]{:S(2)}) collective-permute-start(bf16[960,384]{1,0:T(8,128)(2,1)} %collective-permute-done.21.refs_3_.refs_2_), channel_id=1, source_target_pairs={{0,4},{4,0},{8,12},{12,8},{1,5},{5,1},{9,13},{13,9},{2,6},{6,2},{1... | collective-permute-start | bytes 2211848 | tf_op jit(solution)/shard_map/ppermute | solution.py:495
  205.8 7.9 %collective-permute-start.28 = (bf16[960,384]{1,0:T(8,128)(2,1)}, bf16[960,384]{1,0:T(8,128)(2,1)S(1)}, u32[]{:S(2)}, u32[]{:S(2)}) collective-permute-start(bf16[960,384]{1,0:T(8,128)(2,1)} %get-tuple-element.118), channel_id=1, source_target_pairs={{0,4},{4,0},{8,12},{12,8},{1,5},{5,1},{9,13},{13,9},{2,6},{6,2},{1... | collective-permute-start | bytes 2211848 | tf_op jit(solution)/shard_map/ppermute | solution.py:495
  211.4 3.9 collective-permute-start.25
  215.0 18.8 %collective-permute-start.29 = (bf16[960,384]{1,0:T(8,128)(2,1)S(1)}, bf16[960,384]{1,0:T(8,128)(2,1)S(1)}, u32[]{:S(2)}, u32[]{:S(2)}) collective-permute-start(bf16[960,384]{1,0:T(8,128)(2,1)S(1)} %add_convert_fusion.3), channel_id=1, source_target_pairs={{0,8},{4,12},{8,0},{12,4},{1,9},{5,13},{9,1},{13,5},{2,10},{6,14},... | collective-permute-start | bytes 2211848 | tf_op jit(solution)/shard_map/ppermute | solution.py:495
  248.3 106.1 %reduce-scatter.8.cloned.1.call-start = ((), (), s32[]{:S(2)}) async-start(), calls=%async_computation.7 | async-start | bytes 2150400 | tf_op jit(solution)/shard_map/reduce_scatter | solution.py:688
  251.8 38.6 %collective-permute-start.32 = (bf16[960,384]{1,0:T(8,128)(2,1)S(1)}, bf16[960,384]{1,0:T(8,128)(2,1)S(1)}, u32[]{:S(2)}, u32[]{:S(2)}) collective-permute-start(bf16[960,384]{1,0:T(8,128)(2,1)S(1)} %add_convert_fusion.2), channel_id=1, source_target_pairs={{0,8},{4,12},{8,0},{12,4},{1,9},{5,13},{9,1},{13,5},{2,10},{6,14},... | collective-permute-start | bytes 2211848 | tf_op jit(solution)/shard_map/ppermute | solution.py:495
  282.1 9.7 %collective-permute-start.33 = (bf16[5,128,384]{2,1,0:T(8,128)(2,1)}, bf16[5,128,384]{2,1,0:T(8,128)(2,1)}, u32[]{:S(2)}, u32[]{:S(2)}) collective-permute-start(bf16[5,128,384]{2,1,0:T(8,128)(2,1)} %get-tuple-element.149), channel_id=1, source_target_pairs={{0,4},{4,0},{8,12},{12,8},{1,5},{5,1},{9,13},{13,9},{2,6},{6,2},{1... | collective-permute-start | bytes 1474568 | tf_op jit(solution)/shard_map/ppermute | solution.py:495
  290.0 11.9 %collective-permute-start.31 = (bf16[4,480,240]{2,1,0:T(8,128)(2,1)}, bf16[4,480,240]{2,1,0:T(8,128)(2,1)S(1)}, u32[]{:S(2)}, u32[]{:S(2)}) collective-permute-start(bf16[4,480,240]{2,1,0:T(8,128)(2,1)} %get-tuple-element.146), channel_id=1, source_target_pairs={{0,4},{4,0},{8,12},{12,8},{1,5},{5,1},{9,13},{13,9},{2,6},{6,2},{1... | collective-permute-start | bytes 2764808 | tf_op jit(solution)/shard_map/ppermute | solution.py:495
  290.1 115.1 %reduce-scatter.6.cloned.1.call-start = ((), (), s32[]{:S(2)}) async-start(), calls=%async_computation.6 | async-start | bytes 1679360 | tf_op jit(solution)/shard_map/reduce_scatter | solution.py:718
  293.1 20.4 %collective-permute-start.34 = (bf16[5,128,384]{2,1,0:T(8,128)(2,1)S(1)}, bf16[5,128,384]{2,1,0:T(8,128)(2,1)S(1)}, u32[]{:S(2)}, u32[]{:S(2)}) collective-permute-start(bf16[5,128,384]{2,1,0:T(8,128)(2,1)S(1)} %add_convert_fusion.4), channel_id=1, source_target_pairs={{0,8},{4,12},{8,0},{12,4},{1,9},{5,13},{9,1},{13,5},{2,10},{6,14},... | collective-permute-start | bytes 1474568 | tf_op jit(solution)/shard_map/ppermute | solution.py:495
  301.8 36.2 %collective-permute-start.41 = (bf16[4,480,240]{2,1,0:T(8,128)(2,1)}, bf16[4,480,240]{2,1,0:T(8,128)(2,1)S(1)}, u32[]{:S(2)}, u32[]{:S(2)}) collective-permute-start(bf16[4,480,240]{2,1,0:T(8,128)(2,1)} %get-tuple-element.168), channel_id=1, source_target_pairs={{0,4},{4,0},{8,12},{12,8},{1,5},{5,1},{9,13},{13,9},{2,6},{6,2},{1... | collective-permute-start | bytes 2764808 | tf_op jit(solution)/shard_map/ppermute | solution.py:495
  313.5 24.5 %collective-permute-start.42 = (bf16[4,480,240]{2,1,0:T(8,128)(2,1)S(1)}, bf16[4,480,240]{2,1,0:T(8,128)(2,1)S(1)}, u32[]{:S(2)}, u32[]{:S(2)}) collective-permute-start(bf16[4,480,240]{2,1,0:T(8,128)(2,1)S(1)} %add_convert_fusion.1), channel_id=1, source_target_pairs={{0,8},{4,12},{8,0},{12,4},{1,9},{5,13},{9,1},{13,5},{2,10},{6,14},... | collective-permute-start | bytes 2764808 | tf_op jit(solution)/shard_map/ppermute | solution.py:495
  340.8 10.5 %collective-permute-start.45 = (bf16[4,176,240]{2,1,0:T(8,128)(2,1)S(1)}, bf16[4,176,240]{2,1,0:T(8,128)(2,1)S(1)}, u32[]{:S(2)}, u32[]{:S(2)}) collective-permute-start(bf16[4,176,240]{2,1,0:T(8,128)(2,1)S(1)} %add_convert_fusion.6), channel_id=1, source_target_pairs={{0,8},{4,12},{8,0},{12,4},{1,9},{5,13},{9,1},{13,5},{2,10},{6,14},... | collective-permute-start | bytes 1013768 | tf_op jit(solution)/shard_map/ppermute | solution.py:495
  353.7 12.8 %collective-permute-start.37 = (bf16[480,384]{1,0:T(8,128)(2,1)S(1)}, bf16[480,384]{1,0:T(8,128)(2,1)S(1)}, u32[]{:S(2)}, u32[]{:S(2)}) collective-permute-start(bf16[480,384]{1,0:T(8,128)(2,1)S(1)} %copy-done.42), channel_id=1, source_target_pairs={{0,0},{1,8},{2,4},{3,12},{4,1},{5,9},{6,5},{7,13},{8,2},{9,10},{10... | collective-permute-start | bytes 1105928 | tf_op jit(solution)/shard_map/ppermute | solution.py:554
  354.4 54.3 %collective-permute-start.51 = (bf16[240,896]{1,0:T(8,128)(2,1)}, bf16[240,896]{1,0:T(8,128)(2,1)S(1)}, u32[]{:S(2)}, u32[]{:S(2)}) collective-permute-start(bf16[240,896]{1,0:T(8,128)(2,1)} %reduce-scatter.8.cloned.1.call-done), channel_id=1, source_target_pairs={{0,16},{16,0},{1,17},{17,1},{2,18},{18,2},{3,19},{19,3},{4,20},{20... | collective-permute-start | bytes 1290248 | tf_op jit(solution)/shard_map/ppermute | solution.py:541
  356.0 21.7 %collective-permute-start.38 = (bf16[480,384]{1,0:T(8,128)(2,1)}, bf16[480,384]{1,0:T(8,128)(2,1)S(1)}, u32[]{:S(2)}, u32[]{:S(2)}) collective-permute-start(bf16[480,384]{1,0:T(8,128)(2,1)} %get-tuple-element.160), channel_id=1, source_target_pairs={{0,1},{1,9},{2,5},{3,13},{4,0},{5,8},{6,4},{7,12},{8,3},{9,11},{10... | collective-permute-start | bytes 1105928 | tf_op jit(solution)/shard_map/ppermute | solution.py:554
  361.4 32.1 %collective-permute-start.39 = (bf16[480,384]{1,0:T(8,128)(2,1)}, bf16[480,384]{1,0:T(8,128)(2,1)S(1)}, u32[]{:S(2)}, u32[]{:S(2)}) collective-permute-start(bf16[480,384]{1,0:T(8,128)(2,1)} %get-tuple-element.161), channel_id=1, source_target_pairs={{0,2},{1,10},{2,6},{3,14},{4,3},{5,11},{6,7},{7,15},{8,0},{9,8},{1... | collective-permute-start | bytes 1105928 | tf_op jit(solution)/shard_map/ppermute | solution.py:554
  362.6 39.4 %collective-permute-start.40 = (bf16[480,384]{1,0:T(8,128)(2,1)S(1)}, bf16[480,384]{1,0:T(8,128)(2,1)S(1)}, u32[]{:S(2)}, u32[]{:S(2)}) collective-permute-start(bf16[480,384]{1,0:T(8,128)(2,1)S(1)} %copy-done.41), channel_id=1, source_target_pairs={{0,3},{1,11},{2,7},{3,15},{4,2},{5,10},{6,6},{7,14},{8,1},{9,9},{1... | collective-permute-start | bytes 1105928 | tf_op jit(solution)/shard_map/ppermute | solution.py:554
  366.5 43.3 %collective-permute-start.50 = (bf16[240,1024]{1,0:T(8,128)(2,1)S(1)}, bf16[240,1024]{1,0:T(8,128)(2,1)S(1)}, u32[]{:S(2)}, u32[]{:S(2)}) collective-permute-start(bf16[240,1024]{1,0:T(8,128)(2,1)S(1)} %copy-done.20), channel_id=1, source_target_pairs={{0,16},{16,0},{1,17},{17,1},{2,18},{18,2},{3,19},{19,3},{4,20},{20... | collective-permute-start | bytes 1474568 | tf_op jit(solution)/shard_map/ppermute | solution.py:541
  405.2 8.9 %collective-permute-start.46 = (bf16[656,240]{1,0:T(8,128)(2,1)}, bf16[656,240]{1,0:T(8,128)(2,1)S(1)}, u32[]{:S(2)}, u32[]{:S(2)}) collective-permute-start(bf16[656,240]{1,0:T(8,128)(2,1)} %reduce-scatter.6.cloned.1.call-done), channel_id=1, source_target_pairs={{0,16},{16,0},{1,17},{17,1},{2,18},{18,2},{3,19},{19,3},{4,20},{20... | collective-permute-start | bytes 944648 | tf_op jit(solution)/shard_map/ppermute | solution.py:541
  414.3 10.9 %collective-permute-start.48 = (f32[128,240]{1,0:T(8,128)S(1)}, f32[128,240]{1,0:T(8,128)S(1)}, u32[]{:S(2)}, u32[]{:S(2)}) collective-permute-start(f32[128,240]{1,0:T(8,128)S(1)} %pad_maximum_fusion.5.o0), channel_id=1, source_target_pairs={{0,8},{4,12},{8,0},{12,4},{1,9},{5,13},{9,1},{13,5},{2,10},{6,14},... | collective-permute-start | bytes 368648 | tf_op jit(solution)/shard_map/ppermute | solution.py:495
  419.9 12.5 %collective-permute-start.47 = (f32[128,240]{1,0:T(8,128)S(1)}, f32[128,240]{1,0:T(8,128)S(1)}, u32[]{:S(2)}, u32[]{:S(2)}) collective-permute-start(f32[128,240]{1,0:T(8,128)S(1)} %pad_maximum_fusion.5.o0), channel_id=1, source_target_pairs={{0,4},{4,0},{8,12},{12,8},{1,5},{5,1},{9,13},{13,9},{2,6},{6,2},{1... | collective-permute-start | bytes 368648 | tf_op jit(solution)/shard_map/ppermute | solution.py:495
  425.2 7.3 %collective-permute-start.49 = (f32[128,240]{1,0:T(8,128)S(1)}, f32[128,240]{1,0:T(8,128)S(1)}, u32[]{:S(2)}, u32[]{:S(2)}) collective-permute-start(f32[128,240]{1,0:T(8,128)S(1)} %collective-permute-done.48.o2), channel_id=1, source_target_pairs={{0,4},{4,0},{8,12},{12,8},{1,5},{5,1},{9,13},{13,9},{2,6},{6,2},{1... | collective-permute-start | bytes 368648 | tf_op jit(solution)/shard_map/ppermute | solution.py:495
  (55 other events, 509.4 us)
Sparse Core Ops, SparseCore 0:
  89.9 42.9 all-gather.2
  134.4 30.1 all-gather.4
  248.5 43.2 reduce-scatter.3
  293.9 44.3 reduce-scatter.7
  352.9 52.2 reduce-scatter.5
